TPU v7x, 512 devices: a whole 4x8x8 slice. The times are simulated.
512 devices in a mesh: row: 16 (over z, core), col: 32 (over x, y).
Axes of the slice: x: 4, y: 8, z: 8, core: 2. Of those that a mesh axis runs over, the one named last changes fastest.
Arguments:
- inputs: bfloat16 [2048, 12288], P('row', 'col'), may hold values from -0.26367188 to 0.26367188
- pre_act: bfloat16 [2048, 24576], P('row', 'col'), may hold values from -8 to 8
- grad_act: bfloat16 [2048, 24576], P('row', 'col'), may hold values from -6 to 6
- weight_t: bfloat16 [24576, 12288], P('row', 'col'), may hold values from -0.0390625 to 0.0390625
Outputs:
- grad_inputs: bfloat16 [2048, 12288], P('row', 'col')
- grad_weight: bfloat16 [24576, 12288], P('row', 'col')
All inputs are finite; a program needn't handle non-finite values.
Results may differ from a plain program's by a relative error of at most 0.0049.
Values may be sent and summed in bfloat16 or wider, within the bound.
No kernel may reach another device: no remote copies, remote signals or barrier semaphores. Data moves between devices by JAX's collectives and lax.ppermute only.
A program may use at most 64 MiB of HBM per device.

v0:
```python
import jax
import jax.numpy as jnp
from jax import lax
from jax.sharding import PartitionSpec as P


def from_root(block, axis, source):
    block = jnp.where(lax.axis_index(axis) == source, block, jnp.zeros_like(block))
    return lax.psum(block, axis)


def gelu_prime(value):
    inner = 0.7978845608 * (value + 0.044715 * value * value * value)
    tanh_val = jnp.tanh(inner)
    slope = 0.7978845608 * (1.0 + 0.134145 * value * value)
    return 0.5 * (1.0 + tanh_val) + 0.5 * value * (1.0 - tanh_val * tanh_val) * slope


def on_device(inputs, pre_act, grad_act, weight_t):
    hidden_grad = (grad_act.astype(jnp.float32) * gelu_prime(pre_act.astype(jnp.float32))).astype(
        jnp.bfloat16
    )
    column_block = lax.all_gather(hidden_grad, "row", axis=0, tiled=True)
    first_unit = lax.axis_index("row") * 2
    received = []
    for offset in range(2):
        received.append(from_root(column_block, "col", first_unit + offset))
    full_grad = jnp.concatenate(received, axis=1)
    block = full_grad
    grad_inputs = lax.psum_scatter(
        jnp.dot(block, weight_t, preferred_element_type=jnp.float32),
        "row",
        scatter_dimension=0,
        tiled=True,
    ).astype(jnp.bfloat16)
    block = full_grad
    grad_weight = lax.dot_general(
        block,
        lax.all_gather(inputs, "row", axis=0, tiled=True),
        (((0,), (0,)), ((), ())),
        preferred_element_type=jnp.float32,
    ).astype(jnp.bfloat16)
    return (grad_inputs, grad_weight)


def solution(mesh):
    placed = (P("row", "col"), P("row", "col"), P("row", "col"), P("row", "col"))
    return jax.shard_map(
        on_device,
        mesh=mesh,
        in_specs=placed,
        out_specs=(P("row", "col"), P("row", "col")),
        check_vma=False,
    )
```

profile of v0, /device:TPU:1, one launch (start us, length us, event | category | flops | bytes accessed | tf_op | source)
XLA Modules:
  0.0 373.4 jit_solution(496382214691890544)
XLA Ops:
  7.2 0.0 copy-start
  7.2 0.0 all-gather.3.cloned.1.call-start
  7.2 2.1 fusion.6
  9.3 0.0 all-gather.3.cloned.1.call-update
  9.3 0.0 all-reduce.3.cloned.1.call-start
  9.4 51.8 %all-gather.3.cloned.1.call-done = bf16[2048,768]{1,0:T(8,128)(2,1)} async-done(((bf16[128,768]{1,0:T(8,128)(2,1)}), bf16[2048,768]{1,0:T(8,128)(2,1)}) %all-gather.3.cloned.1.call-update) | async-done | bytes 3145744 | tf_op jit(solution)/shard_map/all_gather | solution.py:23
  61.1 4.9 %broadcast_select_fusion = (bf16[2048,768]{1,0:T(8,128)(2,1)}, bf16[2048,768]{1,0:T(8,128)(2,1)}) fusion(bf16[2048,768]{1,0:T(8,128)(2,1)} %all-gather.3.cloned.1.call-done, pred[]{:T(512)S(6)} %eq.7, pred[]{:T(512)S(6)} %eq.6), kind=kLoop, calls=%fused_computation | loop fusion | flops 3145728 | bytes 9437186 | tf_op jit(solution)/shard_map/jit(_where)/select_n | solution.py:8
  66.1 0.0 all-reduce.3.cloned.1.call-update
  66.1 0.0 all-gather.5.cloned.1.call-start
  66.2 0.7 all-gather.5.cloned.1.call-update
  66.8 0.0 reduce-scatter.2.cloned.1.call-start
  66.9 191.7 %all-reduce.3.cloned.1.call-done = (bf16[2048,768]{1,0:T(8,128)(2,1)}, bf16[2048,768]{1,0:T(8,128)(2,1)}) async-done(((bf16[2048,768]{1,0:T(8,128)(2,1)}, bf16[2048,768]{1,0:T(8,128)(2,1)}), (bf16[2048,768]{1,0:T(8,128)(2,1)}, bf16[2048,768]{1,0:T(8,128)(2,1)})) %all-reduce.3.cloned.1.call-update) | async-done | bytes 6291472 | tf_op jit(solution)/shard_map/psum | solution.py:9
  258.6 2.3 constant_dynamic-update-slice_fusion.1
  260.9 0.5 copy-done.1
  261.4 0.2 constant_dynamic-update-slice_fusion
  261.7 0.0 copy-start.2
  261.7 2.6 copy-done.2
  264.4 0.0 copy-done
  264.4 5.1 %fusion.9 = f32[2048,384]{1,0:T(8,128)} fusion(bf16[2048,1536]{1,0:T(8,128)(2,1)S(1)} %constant_dynamic-update-slice_fusion, bf16[1536,384]{1,0:T(8,128)(2,1)S(1)} %copy-done), kind=kOutput, calls=%fused_computation.21 | convolution fusion | flops 2415919104 | bytes 10616832 | tf_op jit(solution)/shard_map/dot_general | solution.py:31
  269.5 0.0 reduce-scatter.2.cloned.1.call-update
  269.5 33.8 %all-gather.5.cloned.1.call-done = bf16[2048,384]{1,0:T(8,128)(2,1)} async-done(((bf16[128,384]{1,0:T(8,128)(2,1)}), bf16[2048,384]{1,0:T(8,128)(2,1)}) %all-gather.5.cloned.1.call-update) | async-done | bytes 1572880 | tf_op jit(solution)/shard_map/all_gather | solution.py:39
  303.3 7.7 %convolution_convert_fusion = bf16[1536,384]{1,0:T(8,128)(2,1)} fusion(bf16[2048,1536]{1,0:T(8,128)(2,1)} %copy-done.2, bf16[2048,384]{1,0:T(8,128)(2,1)} %all-gather.5.cloned.1.call-done), kind=kOutput, calls=%fused_computation.2 | convolution fusion | flops 2416508928 | bytes 9043968 | tf_op jit(solution)/shard_map/dot_general | solution.py:37
  311.0 54.3 %reduce-scatter.2.cloned.1.call-done = f32[128,384]{1,0:T(8,128)} async-done(((f32[2048,384]{1,0:T(8,128)}), f32[128,384]{1,0:T(8,128)}) %reduce-scatter.2.cloned.1.call-update) | async-done | bytes 196624 | tf_op jit(solution)/shard_map/reduce_scatter | solution.py:30
  365.3 1.6 convert_element_type.18
  (1 shorter events, 0.0 us)
Async XLA Ops:
  7.2 257.2 %copy-start = (bf16[1536,384]{1,0:T(8,128)(2,1)S(1)}, bf16[1536,384]{1,0:T(8,128)(2,1)}, u32[]{:S(2)}) copy-start(bf16[1536,384]{1,0:T(8,128)(2,1)} %param.7) | copy-start | bytes 3538948
  7.2 54.0 %all-gather.3.cloned.1.call-start = ((), (), s32[]{:S(2)}) async-start(), calls=%async_computation.1 | async-start | bytes 3342336 | tf_op jit(solution)/shard_map/all_gather | solution.py:23
  9.3 249.3 %all-reduce.3.cloned.1.call-start = ((), (), s32[]{:S(2)}) async-start(), calls=%async_computation.4 | async-start | bytes 12582912 | tf_op jit(solution)/shard_map/psum | solution.py:9
  66.1 237.2 %all-gather.5.cloned.1.call-start = ((), (), s32[]{:S(2)}) async-start(), calls=%async_computation.3 | async-start | bytes 1671168 | tf_op jit(solution)/shard_map/all_gather | solution.py:39
  66.8 298.5 %reduce-scatter.2.cloned.1.call-start = ((), (), s32[]{:S(2)}) async-start(), calls=%async_computation.2 | async-start | bytes 3342336 | tf_op jit(solution)/shard_map/reduce_scatter | solution.py:30
  258.6 2.8 copy-start.1
  261.7 2.7 copy-start.2
Sparse Core Ops, SparseCore 0:
  10.7 50.3 all-gather.2
  66.2 192.3 all-reduce.2
  261.0 42.2 all-gather.4
  306.2 59.0 reduce-scatter.1
where the time goes:
time: 376 us; the launch traced here: 373 us
  waiting for transfers between devices  332 us (88%)
  between operations  13.8 us (4%)
  matrix products  12.8 us (3%)
  other arithmetic  8.59 us (2%)
  local copies, waits for them, and re-layouts  5.72 us (2%)
    psum x1, waiting for transfers between devices, from_root(): return lax.psum(block, axis)  192 us
    reduce_scatter x1, waiting for transfers between devices, on_device(): lax.psum_scatter(jnp.dot(block, weight_t, preferred_element_type=jnp.floa...  54.3 us
    all_gather x1, waiting for transfers between devices, on_device(): column_block = lax.all_gather(hidden_grad, 'row', axis=0, tiled=True)  51.8 us
    all_gather x1, waiting for transfers between devices, on_device(): lax.all_gather(inputs, 'row', axis=0, tiled=True)  33.8 us
    dot_general x1, matrix products, on_device(): lax.dot_general(block, lax.all_gather(inputs, 'row', axis=0, tiled=True),...  7.7 us
  transfers between devices with their start and end apart: 4, of which 4 were waited for; matrix products, arithmetic and copies ran while one was open for 4% of the time, Pallas kernels for 0%

commit v1 on v0

v1 whole, which is shorter than its diff:
```python
import jax
import jax.numpy as jnp
from jax import lax
from jax.sharding import Mesh, PartitionSpec as P

ROW = ("z", "core")
COL = ("x", "y")
ALL = ROW + COL
CHUNKS = 2


def gelu_prime(value):
    inner = 0.7978845608 * (value + 0.044715 * value * value * value)
    tanh_val = jnp.tanh(inner)
    slope = 0.7978845608 * (1.0 + 0.134145 * value * value)
    return 0.5 * (1.0 + tanh_val) + 0.5 * value * (1.0 - tanh_val * tanh_val) * slope


def to_unit_rows():
    pairs = []
    for row in range(16):
        for col in range(32):
            target = (col // 2) * 32 + (col % 2) * 16 + row
            pairs.append((row * 32 + col, target))
    return pairs


def dot(a, b, dims):
    return lax.dot_general(a, b, (dims, ((), ())), preferred_element_type=jnp.float32)


def on_device(inputs, pre_act, grad_act, weight_t):
    hidden_grad = (grad_act.astype(jnp.float32) * gelu_prime(pre_act.astype(jnp.float32))).astype(
        jnp.bfloat16
    )
    mine = lax.ppermute(hidden_grad, ALL, to_unit_rows())
    all_inputs = lax.all_gather(inputs, ROW, axis=0)
    size = 128 // CHUNKS
    shares, sums = [], [0.0, 0.0]
    for k in range(CHUNKS):
        block = lax.all_gather(mine[k * size : (k + 1) * size], COL, axis=0)
        halves = [block[h * 16 : (h + 1) * 16].reshape(16 * size, 768) for h in range(2)]
        share = sum(dot(halves[h], weight_t[h * 768 : (h + 1) * 768], ((1,), (0,))) for h in range(2))
        shares.append(lax.psum_scatter(share, ROW, scatter_dimension=0, tiled=True))
        tokens = all_inputs[:, k * size : (k + 1) * size].reshape(16 * size, 384)
        for h in range(2):
            sums[h] = sums[h] + dot(halves[h], tokens, ((0,), (0,)))
    grad_inputs = jnp.concatenate(shares, axis=0).astype(jnp.bfloat16)
    grad_weight = jnp.concatenate([s.astype(jnp.bfloat16) for s in sums], axis=0)
    return (grad_inputs, grad_weight)


def solution(mesh):
    fine = Mesh(mesh.devices.reshape(8, 2, 4, 8), ALL)
    placed = P(ROW, COL)
    return jax.shard_map(
        on_device,
        mesh=fine,
        in_specs=(placed,) * 4,
        out_specs=(placed, placed),
        check_vma=False,
    )
```

time: 376 us -> 385 us (1.024)
  waiting for transfers between devices: 332 us -> 338 us
  matrix products: 12.8 us -> 17.6 us
  starting transfers between devices: 0.16 us -> 4.79 us
    psum x1 -> x0, waiting for transfers between devices: 192 us -> none  [from_root(): return lax.psum(block, axis)]
    all_gather x2 -> x3, waiting for transfers between devices: 85.5 us -> 208 us  [the longest x2 172 us: on_device(): block = lax.all_gather(mine[k * size:(k + 1) * size], COL, axis=0)]
    reduce_scatter x1 -> x2, waiting for transfers between devices: 54.3 us -> 114 us  [on_device(): shares.append(lax.psum_scatter(share, ROW, scatter_dimension=0, tiled=True))]
    ppermute x0 -> x1, waiting for transfers between devices: none -> 14.2 us  [on_device(): mine = lax.ppermute(hidden_grad, ALL, to_unit_rows())]
    select_n x1 -> x0, other arithmetic: 4.95 us -> none  [from_root(): jnp.where(lax.axis_index(axis) == source, block, jnp.zeros_like(block))]
    dot_general x2 -> x8, matrix products: 12.8 us -> 17.6 us  [dot(): lax.dot_general(a, b, (dims, ((), ())), preferred_element_type=jnp.float32)]
    ppermute x0 -> x1, starting transfers between devices: none -> 4.59 us  [on_device(): mine = lax.ppermute(hidden_grad, ALL, to_unit_rows())]
    unnamed x7 -> x10, local copies, waits for them, and re-layouts: 5.48 us -> 1.06 us
  transfers between devices with their start and end apart: 4 -> 6, of which waited for: 4 -> 6; matrix products, arithmetic and copies ran while one was open for 4% -> 6% of each run, Pallas kernels for 0% -> 0%
where the time goes in v1:
time: 385 us; the launch traced here: 383 us
  waiting for transfers between devices  338 us (88%)
  matrix products  17.6 us (5%)
  between operations  13.9 us (4%)
  other arithmetic  4.88 us (1%)
  starting transfers between devices  4.79 us (1%)
  local copies, waits for them, and re-layouts  3.92 us (1%)
    all_gather x2, waiting for transfers between devices, on_device(): block = lax.all_gather(mine[k * size:(k + 1) * size], COL, axis=0)  172 us
    reduce_scatter x2, waiting for transfers between devices, on_device(): shares.append(lax.psum_scatter(share, ROW, scatter_dimension=0, tiled=True))  114 us
    all_gather x1, waiting for transfers between devices, on_device(): all_inputs = lax.all_gather(inputs, ROW, axis=0)  36.5 us
    dot_general x8, matrix products, dot(): lax.dot_general(a, b, (dims, ((), ())), preferred_element_type=jnp.float32)  17.6 us
    ppermute x1, waiting for transfers between devices, on_device(): mine = lax.ppermute(hidden_grad, ALL, to_unit_rows())  14.2 us
  transfers between devices with their start and end apart: 6, of which 6 were waited for; matrix products, arithmetic and copies ran while one was open for 6% of the time, Pallas kernels for 0%

profile of v1, /device:TPU:1, one launch (start us, length us, event | category | flops | bytes accessed | tf_op | source)
XLA Modules:
  0.0 382.8 jit_solution(15745928655239695057)
XLA Ops:
  7.2 1.3 fusion.20
  8.5 4.6 %collective-permute-start = (bf16[128,768]{1,0:T(8,128)(2,1)S(1)}, bf16[128,768]{1,0:T(8,128)(2,1)S(1)}, u32[]{:S(2)}, u32[]{:S(2)}) collective-permute-start(bf16[128,768]{1,0:T(8,128)(2,1)S(1)} %fusion.20), channel_id=1, source_target_pairs={{0,0},{1,16},{2,32},{3,48},{4,64},{5,80},{6,96},{7,112},{8,128},{9... | collective-permute-start | bytes 589832 | tf_op jit(solution)/shard_map/ppermute | solution.py:36
  13.1 14.2 %collective-permute-done = bf16[128,768]{1,0:T(8,128)(2,1)S(1)} collective-permute-done((bf16[128,768]{1,0:T(8,128)(2,1)S(1)}, bf16[128,768]{1,0:T(8,128)(2,1)S(1)}, u32[]{:S(2)}, u32[]{:S(2)}) %collective-permute-start) | collective-permute-done | bytes 196640 | tf_op jit(solution)/shard_map/ppermute | solution.py:36
  27.3 0.7 fusion.29
  28.1 0.7 all-gather.7.cloned.1.call-update
  28.8 0.7 all-gather.11.cloned.1.call-update
  29.5 92.1 %all-gather.9.cloned.1.call-done = bf16[2048,768]{1,0:T(8,128)(2,1)} async-done(((bf16[64,768]{1,0:T(8,128)(2,1)}), bf16[2048,768]{1,0:T(8,128)(2,1)}) %all-gather.9.cloned.1.call-update) | async-done | bytes 3145744 | tf_op jit(solution)/shard_map/all_gather | solution.py:41
  121.7 2.7 fusion.8
  124.3 3.2 convolution_add_fusion
  127.6 79.9 %all-gather.7.cloned.1.call-done = bf16[2048,768]{1,0:T(8,128)(2,1)} async-done(((bf16[64,768]{1,0:T(8,128)(2,1)}), bf16[2048,768]{1,0:T(8,128)(2,1)}) %all-gather.7.cloned.1.call-update) | async-done | bytes 3145744 | tf_op jit(solution)/shard_map/all_gather | solution.py:41
  207.5 2.7 fusion.10
  210.2 3.3 convolution_add_fusion.1
  213.5 2.0 fusion.28
  215.5 1.0 copy-done.2
  216.7 36.5 %all-gather.11.cloned.1.call-done = bf16[2048,384]{1,0:T(8,128)(2,1)} async-done(((bf16[128,384]{1,0:T(8,128)(2,1)}), bf16[2048,384]{1,0:T(8,128)(2,1)}) %all-gather.11.cloned.1.call-update) | async-done | bytes 1572880 | tf_op jit(solution)/shard_map/all_gather | solution.py:37
  253.2 2.8 convolution_bitcast_fusion
  256.0 1.0 convolution_bitcast_fusion.2
  257.0 1.0 fusion.2
  258.0 1.0 fusion.3
  259.1 1.1 pad_maximum_fusion
  260.2 52.1 %reduce-scatter.5.cloned.1.call-done = f32[64,384]{1,0:T(8,128)} async-done(((f32[1024,384]{1,0:T(8,128)}), f32[64,384]{1,0:T(8,128)}) %reduce-scatter.5.cloned.1.call-update) | async-done | bytes 98320 | tf_op jit(solution)/shard_map/reduce_scatter | solution.py:44
  312.3 0.9 convert.7
  313.2 61.5 %reduce-scatter.3.cloned.1.call-done = f32[64,384]{1,0:T(8,128)} async-done(((f32[1024,384]{1,0:T(8,128)}), f32[64,384]{1,0:T(8,128)}) %reduce-scatter.3.cloned.1.call-update) | async-done | bytes 98320 | tf_op jit(solution)/shard_map/reduce_scatter | solution.py:44
  374.7 0.9 convert.6
  (19 shorter events, 1.1 us)
Async XLA Ops:
  7.2 114.5 %all-gather.9.cloned.1.call-start = ((), (), s32[]{:S(2)}) async-start(), calls=%async_computation.5 | async-start | bytes 3244032 | tf_op jit(solution)/shard_map/all_gather | solution.py:41
  8.5 18.8 %collective-permute-start = (bf16[128,768]{1,0:T(8,128)(2,1)S(1)}, bf16[128,768]{1,0:T(8,128)(2,1)S(1)}, u32[]{:S(2)}, u32[]{:S(2)}) collective-permute-start(bf16[128,768]{1,0:T(8,128)(2,1)S(1)} %fusion.20), channel_id=1, source_target_pairs={{0,0},{1,16},{2,32},{3,48},{4,64},{5,80},{6,96},{7,112},{8,128},{9... | collective-permute-start | bytes 589832 | tf_op jit(solution)/shard_map/ppermute | solution.py:36
  28.0 179.5 %all-gather.7.cloned.1.call-start = ((), (), s32[]{:S(2)}) async-start(), calls=%async_computation.4 | async-start | bytes 3244032 | tf_op jit(solution)/shard_map/all_gather | solution.py:41
  28.8 224.4 %all-gather.11.cloned.1.call-start = ((), (), s32[]{:S(2)}) async-start(), calls=%async_computation.6 | async-start | bytes 1671168 | tf_op jit(solution)/shard_map/all_gather | solution.py:37
  29.5 282.8 %reduce-scatter.5.cloned.1.call-start = ((), (), s32[]{:S(2)}) async-start(), calls=%async_computation.3 | async-start | bytes 1671168 | tf_op jit(solution)/shard_map/reduce_scatter | solution.py:44
  121.7 2.7 copy-start
  127.6 247.1 %reduce-scatter.3.cloned.1.call-start = ((), (), s32[]{:S(2)}) async-start(), calls=%async_computation.2 | async-start | bytes 1671168 | tf_op jit(solution)/shard_map/reduce_scatter | solution.py:44
  207.5 2.7 copy-start.1
  213.5 3.0 copy-start.2
  253.2 2.8 copy-start.3
  253.2 2.8 copy-start.4
Sparse Core Ops, SparseCore 0:
  28.1 93.5 all-gather.8
  125.4 82.0 all-gather.6
  209.7 43.4 all-gather.10
  255.9 56.3 reduce-scatter.4
  315.2 59.4 reduce-scatter.2

commit v2 on v1

v2 whole, which is shorter than its diff:
```python
import jax
import jax.numpy as jnp
from jax import lax
from jax.sharding import Mesh, PartitionSpec as P

ROW = ("z", "core")
COL = ("x", "y")
ALL = ROW + COL
BF, F32 = jnp.bfloat16, jnp.float32
PART = 32


def gelu_prime(value):
    inner = 0.7978845608 * (value + 0.044715 * value * value * value)
    tanh_val = jnp.tanh(inner)
    slope = 0.7978845608 * (1.0 + 0.134145 * value * value)
    return 0.5 * (1.0 + tanh_val) + 0.5 * value * (1.0 - tanh_val * tanh_val) * slope


def slot_of(row, q):
    z, core = row // 2, row % 2
    x, y = q * 2 + z // 4, core * 4 + z % 4
    return x * 8 + y


def to_slots(swap):
    pairs = []
    for row in range(16):
        for col in range(32):
            q = (col % 2) ^ swap
            pairs.append((row * 32 + col, (col // 2) * 32 + slot_of(row, q)))
    return pairs


def fetch(block, axis, size, step):
    return lax.ppermute(block, axis, [((i + step) % size, i) for i in range(size)])


def dot(a, b, dims):
    return lax.dot_general(a, b, (dims, ((), ())), preferred_element_type=F32)


def place(pieces, at, size):
    first = next(iter(pieces.values()))
    whole = jnp.zeros((size, *first.shape), first.dtype)
    for d, piece in pieces.items():
        start = (lax.rem(at + d + size, size),) + (0,) * first.ndim
        whole = lax.dynamic_update_slice(whole, piece[None], start)
    return whole


def line_of_8(mine, axis, cut):
    got = {0: mine}
    got[1], got[-1] = fetch(mine, axis, 8, 1), fetch(mine, axis, 8, -1)
    got[2], got[-2] = fetch(got[1], axis, 8, 1), fetch(got[-1], axis, 8, -1)
    got[3], got[-3] = fetch(got[2], axis, 8, 1), fetch(got[-2], axis, 8, -1)
    got[4] = jnp.concatenate(
        [fetch(got[2][:cut], axis, 8, 2), fetch(got[-2][cut:], axis, 8, -2)], axis=0
    )
    return got


def line_of_4(mine, axis, cut):
    got = {0: mine}
    got[1], got[-1] = fetch(mine, axis, 4, 1), fetch(mine, axis, 4, -1)
    got[2] = jnp.concatenate(
        [fetch(got[1][:cut], axis, 4, 1), fetch(got[-1][cut:], axis, 4, -1)], axis=0
    )
    return got


def on_device(inputs, pre_act, grad_act, weight_t):
    z, core, x, y = (lax.axis_index(a) for a in ALL)
    hidden = (grad_act.astype(F32) * gelu_prime(pre_act.astype(F32))).astype(BF)
    h = y % 2
    q = x // 2
    same = lax.dynamic_slice_in_dim(hidden, h * 64, 64, 0)
    other = lax.dynamic_slice_in_dim(hidden, (1 - h) * 64, 64, 0)
    same = lax.ppermute(same, ALL, to_slots(0))
    other = lax.ppermute(other, ALL, to_slots(1))
    low = jnp.where(q == 0, same, other)
    high = jnp.where(q == 0, other, same)
    slot = jnp.concatenate([low, high], axis=1)
    part_a, part_b = slot[:PART], slot[PART:]

    all_inputs = lax.all_gather(inputs, ROW, axis=0)
    seen = all_inputs.reshape(2, 4, 2, 2, 2, PART, 384)
    in_a = seen[:, :, :, :, 0].transpose(3, 0, 2, 1, 4, 5).reshape(4, 8 * PART, 384)
    in_b = seen[:, :, :, :, 1].transpose(2, 1, 3, 0, 4, 5).reshape(8, 4 * PART, 384)

    ya = line_of_8(part_a, "y", PART // 2)
    xb = line_of_4(part_b, "x", PART // 2)
    xa = line_of_4(place(ya, y, 8), "x", 4)
    yb = line_of_8(place(xb, x, 4), "y", 2)

    total = 0.0
    share_a, share_b = {}, {}
    for d, block in xa.items():
        flat = block.reshape(8 * PART, 1536)
        share_a[d] = dot(flat, weight_t, ((1,), (0,))).reshape(8, PART, 384)
        tokens = lax.dynamic_index_in_dim(in_a, lax.rem(x + d + 4, 4), 0, False)
        total = total + dot(flat, tokens, ((0,), (0,)))
    for group in ((0, 1, -1), (2, -2), (3, -3, 4)):
        flat = jnp.concatenate([yb[d].reshape(4 * PART, 1536) for d in group], axis=0)
        share = dot(flat, weight_t, ((1,), (0,))).reshape(len(group), 4, PART, 384)
        tokens = []
        for i, d in enumerate(group):
            share_b[d] = share[i]
            tokens.append(lax.dynamic_index_in_dim(in_b, lax.rem(y + d + 8, 8), 0, False))
        total = total + dot(flat, jnp.concatenate(tokens, axis=0), ((0,), (0,)))
    grad_weight = total.astype(BF)

    share_a = place(share_a, x, 4).reshape(2, 2, 2, 4, PART, 384)
    share_b = place(share_b, y, 8).reshape(2, 4, 2, 2, PART, 384).transpose(2, 3, 0, 1, 4, 5)
    share = jnp.stack([share_a, share_b], axis=4)
    keep = lax.dynamic_index_in_dim(share, core, 2, False)
    give = lax.dynamic_index_in_dim(share, 1 - core, 2, False)
    both = keep + lax.ppermute(give, "core", [(0, 1), (1, 0)])
    both = both.transpose(1, 2, 0, 3, 4, 5).reshape(8, 128, 384)
    sums = lax.dynamic_index_in_dim(both, z, 0, False)
    sent = both.astype(BF)
    for d in (4, 3, -3, 2, -2, 1, -1):
        piece = lax.dynamic_index_in_dim(sent, lax.rem(z + d + 8, 8), 0, False)
        sums = sums + fetch(piece, "z", 8, -d).astype(F32)
    return (sums.astype(BF), grad_weight)


def solution(mesh):
    fine = Mesh(mesh.devices.reshape(8, 2, 4, 8), ALL)
    placed = P(ROW, COL)
    return jax.shard_map(
        on_device,
        mesh=fine,
        in_specs=(placed,) * 4,
        out_specs=(placed, placed),
        check_vma=False,
    )
```

time: 385 us -> 207 us (0.54)
  waiting for transfers between devices: 338 us -> 19.3 us
  starting transfers between devices: 4.79 us -> 149 us
  matrix products: 17.6 us -> 10.3 us
    all_gather x2 -> x0, waiting for transfers between devices: 172 us -> none  [on_device(): block = lax.all_gather(mine[k * size:(k + 1) * size], COL, axis=0)]
    ppermute x1 -> x34, starting transfers between devices: 4.59 us -> 149 us  [the longest x31 116 us: fetch(): lax.ppermute(block, axis, [((i + step) % size, i) for i in range(size)])]
    reduce_scatter x2 -> x0, waiting for transfers between devices: 114 us -> none  [on_device(): shares.append(lax.psum_scatter(share, ROW, scatter_dimension=0, tiled=True))]
    all_gather x1, waiting for transfers between devices: 36.5 us -> 0.02 us  [on_device(): all_inputs = lax.all_gather(inputs, ROW, axis=0)]
    dot_general x8 -> x14, matrix products: 17.6 us -> 10.3 us  [dot(): return lax.dot_general(a, b, (dims, ((), ())), preferred_element_type=F32)]
    ppermute x1 -> x34, waiting for transfers between devices: 14.2 us -> 19.3 us  [the longest x31 17.7 us: fetch(): lax.ppermute(block, axis, [((i + step) % size, i) for i in range(size)])]
  transfers between devices with their start and end apart: 6 -> 35, of which waited for: 6 -> 7; matrix products, arithmetic and copies ran while one was open for 6% -> 7% of each run, Pallas kernels for 0% -> 0%
where the time goes in v2:
time: 207 us; the launch traced here: 205 us
  starting transfers between devices  149 us (72%)
  waiting for transfers between devices  19.3 us (9%)
  between operations  15.4 us (7%)
  matrix products  10.3 us (5%)
  local copies, waits for them, and re-layouts  7.02 us (3%)
  other arithmetic  4.2 us (2%)
    ppermute x31, starting transfers between devices, fetch(): lax.ppermute(block, axis, [((i + step) % size, i) for i in range(size)])  116 us
    ppermute x31, waiting for transfers between devices, fetch(): lax.ppermute(block, axis, [((i + step) % size, i) for i in range(size)])  17.7 us
    ppermute x1, starting transfers between devices, on_device(): other = lax.ppermute(other, ALL, to_slots(1))  12.9 us
    ppermute x1, starting transfers between devices, on_device(): both = keep + lax.ppermute(give, 'core', [(0, 1), (1, 0)])  10.7 us
    dot_general x14, matrix products, dot(): return lax.dot_general(a, b, (dims, ((), ())), preferred_element_type=F32)  10.3 us
    ppermute x1, starting transfers between devices, on_device(): same = lax.ppermute(same, ALL, to_slots(0))  8.84 us
  transfers between devices with their start and end apart: 35, of which 7 were waited for; matrix products, arithmetic and copies ran while one was open for 7% of the time, Pallas kernels for 0%

profile of v2, /device:TPU:1, one launch (start us, length us, event | category | flops | bytes accessed | tf_op | source)
XLA Modules:
  0.0 205.2 jit_solution(8228573583979209770)
XLA Ops:
  8.7 8.8 %collective-permute-start = (bf16[64,768]{1,0:T(8,128)(2,1)S(1)}, bf16[64,768]{1,0:T(8,128)(2,1)S(1)}, u32[]{:S(2)}, u32[]{:S(2)}) collective-permute-start(bf16[64,768]{1,0:T(8,128)(2,1)S(1)} %get-tuple-element.37), channel_id=1, source_target_pairs={{0,0},{1,16},{2,32},{3,48},{4,64},{5,80},{6,96},{7,112},{8,128},{9... | collective-permute-start | bytes 294920 | tf_op jit(solution)/shard_map/ppermute | solution.py:79
  17.5 12.9 %collective-permute-start.1 = (bf16[64,768]{1,0:T(8,128)(2,1)S(1)}, bf16[64,768]{1,0:T(8,128)(2,1)S(1)}, u32[]{:S(2)}, u32[]{:S(2)}) collective-permute-start(bf16[64,768]{1,0:T(8,128)(2,1)S(1)} %get-tuple-element.38), channel_id=1, source_target_pairs={{0,16},{1,0},{2,48},{3,32},{4,80},{5,64},{6,112},{7,96},{8,144},{9... | collective-permute-start | bytes 294920 | tf_op jit(solution)/shard_map/ppermute | solution.py:80
  32.2 12.0 %collective-permute-start.14 = (bf16[32,1536]{1,0:T(8,128)(2,1)S(1)}, bf16[32,1536]{1,0:T(8,128)(2,1)S(1)}, u32[]{:S(2)}, u32[]{:S(2)}) collective-permute-start(bf16[32,1536]{1,0:T(8,128)(2,1)S(1)} %get-tuple-element.3), channel_id=1, source_target_pairs={{8,0},{16,8},{24,16},{0,24},{9,1},{17,9},{25,17},{1,25},{10,2},{18... | collective-permute-start | bytes 294920 | tf_op jit(solution)/shard_map/ppermute | solution.py:36
  48.1 3.4 %collective-permute-start.3 = (bf16[32,1536]{1,0:T(8,128)(2,1)S(1)}, bf16[32,1536]{1,0:T(8,128)(2,1)S(1)}, u32[]{:S(2)}, u32[]{:S(2)}) collective-permute-start(bf16[32,1536]{1,0:T(8,128)(2,1)S(1)} %get-tuple-element.34), channel_id=1, source_target_pairs={{7,0},{0,1},{1,2},{2,3},{3,4},{4,5},{5,6},{6,7},{15,8},{8,9},{9,10... | collective-permute-start | bytes 294920 | tf_op jit(solution)/shard_map/ppermute | solution.py:36
  51.6 4.6 %collective-permute-start.16 = (bf16[16,1536]{1,0:T(8,128)(2,1)S(1)}, bf16[16,1536]{1,0:T(8,128)(2,1)S(1)}, u32[]{:S(2)}, u32[]{:S(2)}) collective-permute-start(bf16[16,1536]{1,0:T(8,128)(2,1)S(1)} %slice.118), channel_id=1, source_target_pairs={{8,0},{16,8},{24,16},{0,24},{9,1},{17,9},{25,17},{1,25},{10,2},{18... | collective-permute-start | bytes 147464 | tf_op jit(solution)/shard_map/ppermute | solution.py:36
  58.1 3.1 %collective-permute-start.4 = (bf16[32,1536]{1,0:T(8,128)(2,1)S(1)}, bf16[32,1536]{1,0:T(8,128)(2,1)S(1)}, u32[]{:S(2)}, u32[]{:S(2)}) collective-permute-start(bf16[32,1536]{1,0:T(8,128)(2,1)S(1)} %collective-permute-done.2), channel_id=1, source_target_pairs={{1,0},{2,1},{3,2},{4,3},{5,4},{6,5},{7,6},{0,7},{9,8},{10,9},{11,1... | collective-permute-start | bytes 294920 | tf_op jit(solution)/shard_map/ppermute | solution.py:36
  63.6 4.3 %collective-permute-start.18 = (bf16[4,32,1536]{2,1,0:T(8,128)(2,1)S(1)}, bf16[4,32,1536]{2,1,0:T(8,128)(2,1)S(1)}, u32[]{:S(2)}, u32[]{:S(2)}) collective-permute-start(bf16[4,32,1536]{2,1,0:T(8,128)(2,1)S(1)} %fusion.59), channel_id=1, source_target_pairs={{1,0},{2,1},{3,2},{4,3},{5,4},{6,5},{7,6},{0,7},{9,8},{10,9},{11,1... | collective-permute-start | bytes 1179656 | tf_op jit(solution)/shard_map/ppermute | solution.py:36
  69.9 3.1 %collective-permute-start.8 = (bf16[16,1536]{1,0:T(8,128)(2,1)S(1)}, bf16[16,1536]{1,0:T(8,128)(2,1)S(1)}, u32[]{:S(2)}, u32[]{:S(2)}) collective-permute-start(bf16[16,1536]{1,0:T(8,128)(2,1)S(1)} %slice.114), channel_id=1, source_target_pairs={{2,0},{3,1},{4,2},{5,3},{6,4},{7,5},{0,6},{1,7},{10,8},{11,9},{12,... | collective-permute-start | bytes 147464 | tf_op jit(solution)/shard_map/ppermute | solution.py:36
  73.0 3.1 %collective-permute-start.9 = (bf16[16,1536]{1,0:T(8,128)(2,1)S(1)}, bf16[16,1536]{1,0:T(8,128)(2,1)S(1)}, u32[]{:S(2)}, u32[]{:S(2)}) collective-permute-start(bf16[16,1536]{1,0:T(8,128)(2,1)S(1)} %slice.115), channel_id=1, source_target_pairs={{6,0},{7,1},{0,2},{1,3},{2,4},{3,5},{4,6},{5,7},{14,8},{15,9},{8,1... | collective-permute-start | bytes 147464 | tf_op jit(solution)/shard_map/ppermute | solution.py:36
  76.1 5.8 %collective-permute-start.6 = (bf16[32,1536]{1,0:T(8,128)(2,1)S(1)}, bf16[32,1536]{1,0:T(8,128)(2,1)S(1)}, u32[]{:S(2)}, u32[]{:S(2)}) collective-permute-start(bf16[32,1536]{1,0:T(8,128)(2,1)S(1)} %collective-permute-done.4), channel_id=1, source_target_pairs={{1,0},{2,1},{3,2},{4,3},{5,4},{6,5},{7,6},{0,7},{9,8},{10,9},{11,1... | collective-permute-start | bytes 294920 | tf_op jit(solution)/shard_map/ppermute | solution.py:36
  85.9 4.9 %collective-permute-done.7 = bf16[32,1536]{1,0:T(8,128)(2,1)S(1)} collective-permute-done((bf16[32,1536]{1,0:T(8,128)(2,1)S(1)}, bf16[32,1536]{1,0:T(8,128)(2,1)S(1)}, u32[]{:S(2)}, u32[]{:S(2)}) %collective-permute-start.7) | collective-permute-done | bytes 98336 | tf_op jit(solution)/shard_map/ppermute | solution.py:36
  90.9 4.3 %collective-permute-start.10 = (bf16[8,32,1536]{2,1,0:T(8,128)(2,1)S(1)}, bf16[8,32,1536]{2,1,0:T(8,128)(2,1)S(1)}, u32[]{:S(2)}, u32[]{:S(2)}) collective-permute-start(bf16[8,32,1536]{2,1,0:T(8,128)(2,1)S(1)} %fusion.58), channel_id=1, source_target_pairs={{8,0},{16,8},{24,16},{0,24},{9,1},{17,9},{25,17},{1,25},{10,2},{18... | collective-permute-start | bytes 2359304 | tf_op jit(solution)/shard_map/ppermute | solution.py:36
  98.8 3.8 %collective-permute-start.20 = (bf16[4,32,1536]{2,1,0:T(8,128)(2,1)S(1)}, bf16[4,32,1536]{2,1,0:T(8,128)(2,1)S(1)}, u32[]{:S(2)}, u32[]{:S(2)}) collective-permute-start(bf16[4,32,1536]{2,1,0:T(8,128)(2,1)S(1)} %collective-permute-done.18), channel_id=1, source_target_pairs={{1,0},{2,1},{3,2},{4,3},{5,4},{6,5},{7,6},{0,7},{9,8},{10,9},{11,1... | collective-permute-start | bytes 1179656 | tf_op jit(solution)/shard_map/ppermute | solution.py:36
  104.8 2.8 %collective-permute-done.20 = bf16[4,32,1536]{2,1,0:T(8,128)(2,1)S(1)} collective-permute-done((bf16[4,32,1536]{2,1,0:T(8,128)(2,1)S(1)}, bf16[4,32,1536]{2,1,0:T(8,128)(2,1)S(1)}, u32[]{:S(2)}, u32[]{:S(2)}) %collective-permute-start.20) | collective-permute-done | bytes 393248 | tf_op jit(solution)/shard_map/ppermute | solution.py:36
  107.6 3.5 %collective-permute-start.24 = (bf16[2,32,1536]{2,1,0:T(8,128)(2,1)S(1)}, bf16[2,32,1536]{2,1,0:T(8,128)(2,1)S(1)}, u32[]{:S(2)}, u32[]{:S(2)}) collective-permute-start(bf16[2,32,1536]{2,1,0:T(8,128)(2,1)S(1)} %slice.125), channel_id=1, source_target_pairs={{2,0},{3,1},{4,2},{5,3},{6,4},{7,5},{0,6},{1,7},{10,8},{11,9},{12,... | collective-permute-start | bytes 589832 | tf_op jit(solution)/shard_map/ppermute | solution.py:36
  115.2 5.5 %collective-permute-start.22 = (bf16[4,32,1536]{2,1,0:T(8,128)(2,1)S(1)}, bf16[4,32,1536]{2,1,0:T(8,128)(2,1)S(1)}, u32[]{:S(2)}, u32[]{:S(2)}) collective-permute-start(bf16[4,32,1536]{2,1,0:T(8,128)(2,1)S(1)} %collective-permute-done.20), channel_id=1, source_target_pairs={{1,0},{2,1},{3,2},{4,3},{5,4},{6,5},{7,6},{0,7},{9,8},{10,9},{11,1... | collective-permute-start | bytes 1179656 | tf_op jit(solution)/shard_map/ppermute | solution.py:36
  122.8 4.6 %collective-permute-start.12 = (bf16[4,32,1536]{2,1,0:T(8,128)(2,1)S(1)}, bf16[4,32,1536]{2,1,0:T(8,128)(2,1)S(1)}, u32[]{:S(2)}, u32[]{:S(2)}) collective-permute-start(bf16[4,32,1536]{2,1,0:T(8,128)(2,1)S(1)} %slice.116), channel_id=1, source_target_pairs={{8,0},{16,8},{24,16},{0,24},{9,1},{17,9},{25,17},{1,25},{10,2},{18... | collective-permute-start | bytes 1179656 | tf_op jit(solution)/shard_map/ppermute | solution.py:36
  130.6 4.0 %collective-permute-done.23 = bf16[4,32,1536]{2,1,0:T(8,128)(2,1)S(1)} collective-permute-done((bf16[4,32,1536]{2,1,0:T(8,128)(2,1)S(1)}, bf16[4,32,1536]{2,1,0:T(8,128)(2,1)S(1)}, u32[]{:S(2)}, u32[]{:S(2)}) %collective-permute-start.23) | collective-permute-done | bytes 393248 | tf_op jit(solution)/shard_map/ppermute | solution.py:36
  135.7 2.8 %collective-permute-done.13 = bf16[4,32,1536]{2,1,0:T(8,128)(2,1)S(1)} collective-permute-done((bf16[4,32,1536]{2,1,0:T(8,128)(2,1)S(1)}, bf16[4,32,1536]{2,1,0:T(8,128)(2,1)S(1)}, u32[]{:S(2)}, u32[]{:S(2)}) %collective-permute-start.13) | collective-permute-done | bytes 393248 | tf_op jit(solution)/shard_map/ppermute | solution.py:36
  140.9 10.7 %collective-permute-start.26 = (f32[2,2,4,2,32,384]{5,4,3,2,1,0:T(8,128)}, f32[2,2,4,2,32,384]{5,4,3,2,1,0:T(8,128)}, u32[]{:S(2)}, u32[]{:S(2)}) collective-permute-start(f32[2,2,4,2,32,384]{5,4,3,2,1,0:T(8,128)} %bitcast.168), channel_id=1, source_target_pairs={{0,32},{32,0},{1,33},{33,1},{2,34},{34,2},{3,35},{35,3},{4,36},{36... | collective-permute-start | bytes 4718600 | tf_op jit(solution)/shard_map/ppermute | solution.py:118
  161.2 11.4 %collective-permute-start.27 = (bf16[128,384]{1,0:T(8,128)(2,1)S(1)}, bf16[128,384]{1,0:T(8,128)(2,1)S(1)}, u32[]{:S(2)}, u32[]{:S(2)}) collective-permute-start(bf16[128,384]{1,0:T(8,128)(2,1)S(1)} %get-tuple-element.18), channel_id=1, source_target_pairs={{256,0},{320,64},{384,128},{448,192},{0,256},{64,320},{128,384},{1... | collective-permute-start | bytes 294920 | tf_op jit(solution)/shard_map/ppermute | solution.py:36
  175.2 6.3 %collective-permute-start.29 = (bf16[128,384]{1,0:T(8,128)(2,1)S(1)}, bf16[128,384]{1,0:T(8,128)(2,1)S(1)}, u32[]{:S(2)}, u32[]{:S(2)}) collective-permute-start(bf16[128,384]{1,0:T(8,128)(2,1)S(1)} %get-tuple-element.23), channel_id=1, source_target_pairs={{192,0},{256,64},{320,128},{384,192},{448,256},{0,320},{64,384},{1... | collective-permute-start | bytes 294920 | tf_op jit(solution)/shard_map/ppermute | solution.py:36
  183.5 5.5 %collective-permute-start.31 = (bf16[128,384]{1,0:T(8,128)(2,1)S(1)}, bf16[128,384]{1,0:T(8,128)(2,1)S(1)}, u32[]{:S(2)}, u32[]{:S(2)}) collective-permute-start(bf16[128,384]{1,0:T(8,128)(2,1)S(1)} %get-tuple-element.21), channel_id=1, source_target_pairs={{128,0},{192,64},{256,128},{320,192},{384,256},{448,320},{0,384},{... | collective-permute-start | bytes 294920 | tf_op jit(solution)/shard_map/ppermute | solution.py:36
  190.9 4.6 %collective-permute-start.33 = (bf16[128,384]{1,0:T(8,128)(2,1)S(1)}, bf16[128,384]{1,0:T(8,128)(2,1)S(1)}, u32[]{:S(2)}, u32[]{:S(2)}) collective-permute-start(bf16[128,384]{1,0:T(8,128)(2,1)S(1)} %get-tuple-element.19), channel_id=1, source_target_pairs={{64,0},{128,64},{192,128},{256,192},{320,256},{384,320},{448,384},... | collective-permute-start | bytes 294920 | tf_op jit(solution)/shard_map/ppermute | solution.py:36
  (159 shorter events, 53.9 us)
Async XLA Ops:
  7.2 144.5 %all-gather.3.cloned.1.call-start = ((), (), s32[]{:S(2)}) async-start(), calls=%async_computation | async-start | bytes 1671168 | tf_op jit(solution)/shard_map/all_gather | solution.py:86
  8.7 21.8 %collective-permute-start = (bf16[64,768]{1,0:T(8,128)(2,1)S(1)}, bf16[64,768]{1,0:T(8,128)(2,1)S(1)}, u32[]{:S(2)}, u32[]{:S(2)}) collective-permute-start(bf16[64,768]{1,0:T(8,128)(2,1)S(1)} %get-tuple-element.37), channel_id=1, source_target_pairs={{0,0},{1,16},{2,32},{3,48},{4,64},{5,80},{6,96},{7,112},{8,128},{9... | collective-permute-start | bytes 294920 | tf_op jit(solution)/shard_map/ppermute | solution.py:79
  17.5 14.5 %collective-permute-start.1 = (bf16[64,768]{1,0:T(8,128)(2,1)S(1)}, bf16[64,768]{1,0:T(8,128)(2,1)S(1)}, u32[]{:S(2)}, u32[]{:S(2)}) collective-permute-start(bf16[64,768]{1,0:T(8,128)(2,1)S(1)} %get-tuple-element.38), channel_id=1, source_target_pairs={{0,16},{1,0},{2,48},{3,32},{4,80},{5,64},{6,112},{7,96},{8,144},{9... | collective-permute-start | bytes 294920 | tf_op jit(solution)/shard_map/ppermute | solution.py:80
  32.2 19.4 %collective-permute-start.14 = (bf16[32,1536]{1,0:T(8,128)(2,1)S(1)}, bf16[32,1536]{1,0:T(8,128)(2,1)S(1)}, u32[]{:S(2)}, u32[]{:S(2)}) collective-permute-start(bf16[32,1536]{1,0:T(8,128)(2,1)S(1)} %get-tuple-element.3), channel_id=1, source_target_pairs={{8,0},{16,8},{24,16},{0,24},{9,1},{17,9},{25,17},{1,25},{10,2},{18... | collective-permute-start | bytes 294920 | tf_op jit(solution)/shard_map/ppermute | solution.py:36
  44.2 12.0 %collective-permute-start.15 = (bf16[32,1536]{1,0:T(8,128)(2,1)S(1)}, bf16[32,1536]{1,0:T(8,128)(2,1)S(1)}, u32[]{:S(2)}, u32[]{:S(2)}) collective-permute-start(bf16[32,1536]{1,0:T(8,128)(2,1)S(1)} %get-tuple-element.3), channel_id=1, source_target_pairs={{24,0},{0,8},{8,16},{16,24},{25,1},{1,9},{9,17},{17,25},{26,2},{2,... | collective-permute-start | bytes 294920 | tf_op jit(solution)/shard_map/ppermute | solution.py:36
  46.1 12.0 %collective-permute-start.2 = (bf16[32,1536]{1,0:T(8,128)(2,1)S(1)}, bf16[32,1536]{1,0:T(8,128)(2,1)S(1)}, u32[]{:S(2)}, u32[]{:S(2)}) collective-permute-start(bf16[32,1536]{1,0:T(8,128)(2,1)S(1)} %get-tuple-element.34), channel_id=1, source_target_pairs={{1,0},{2,1},{3,2},{4,3},{5,4},{6,5},{7,6},{0,7},{9,8},{10,9},{11,1... | collective-permute-start | bytes 294920 | tf_op jit(solution)/shard_map/ppermute | solution.py:36
  48.1 13.2 %collective-permute-start.3 = (bf16[32,1536]{1,0:T(8,128)(2,1)S(1)}, bf16[32,1536]{1,0:T(8,128)(2,1)S(1)}, u32[]{:S(2)}, u32[]{:S(2)}) collective-permute-start(bf16[32,1536]{1,0:T(8,128)(2,1)S(1)} %get-tuple-element.34), channel_id=1, source_target_pairs={{7,0},{0,1},{1,2},{2,3},{3,4},{4,5},{5,6},{6,7},{15,8},{8,9},{9,10... | collective-permute-start | bytes 294920 | tf_op jit(solution)/shard_map/ppermute | solution.py:36
  63.6 34.4 %collective-permute-start.18 = (bf16[4,32,1536]{2,1,0:T(8,128)(2,1)S(1)}, bf16[4,32,1536]{2,1,0:T(8,128)(2,1)S(1)}, u32[]{:S(2)}, u32[]{:S(2)}) collective-permute-start(bf16[4,32,1536]{2,1,0:T(8,128)(2,1)S(1)} %fusion.59), channel_id=1, source_target_pairs={{1,0},{2,1},{3,2},{4,3},{5,4},{6,5},{7,6},{0,7},{9,8},{10,9},{11,1... | collective-permute-start | bytes 1179656 | tf_op jit(solution)/shard_map/ppermute | solution.py:36
  67.9 30.0 %collective-permute-start.19 = (bf16[4,32,1536]{2,1,0:T(8,128)(2,1)S(1)}, bf16[4,32,1536]{2,1,0:T(8,128)(2,1)S(1)}, u32[]{:S(2)}, u32[]{:S(2)}) collective-permute-start(bf16[4,32,1536]{2,1,0:T(8,128)(2,1)S(1)} %fusion.59), channel_id=1, source_target_pairs={{7,0},{0,1},{1,2},{2,3},{3,4},{4,5},{5,6},{6,7},{15,8},{8,9},{9,10... | collective-permute-start | bytes 1179656 | tf_op jit(solution)/shard_map/ppermute | solution.py:36
  69.9 21.0 %collective-permute-start.8 = (bf16[16,1536]{1,0:T(8,128)(2,1)S(1)}, bf16[16,1536]{1,0:T(8,128)(2,1)S(1)}, u32[]{:S(2)}, u32[]{:S(2)}) collective-permute-start(bf16[16,1536]{1,0:T(8,128)(2,1)S(1)} %slice.114), channel_id=1, source_target_pairs={{2,0},{3,1},{4,2},{5,3},{6,4},{7,5},{0,6},{1,7},{10,8},{11,9},{12,... | collective-permute-start | bytes 147464 | tf_op jit(solution)/shard_map/ppermute | solution.py:36
  73.0 17.9 %collective-permute-start.9 = (bf16[16,1536]{1,0:T(8,128)(2,1)S(1)}, bf16[16,1536]{1,0:T(8,128)(2,1)S(1)}, u32[]{:S(2)}, u32[]{:S(2)}) collective-permute-start(bf16[16,1536]{1,0:T(8,128)(2,1)S(1)} %slice.115), channel_id=1, source_target_pairs={{6,0},{7,1},{0,2},{1,3},{2,4},{3,5},{4,6},{5,7},{14,8},{15,9},{8,1... | collective-permute-start | bytes 147464 | tf_op jit(solution)/shard_map/ppermute | solution.py:36
  90.9 29.8 %collective-permute-start.10 = (bf16[8,32,1536]{2,1,0:T(8,128)(2,1)S(1)}, bf16[8,32,1536]{2,1,0:T(8,128)(2,1)S(1)}, u32[]{:S(2)}, u32[]{:S(2)}) collective-permute-start(bf16[8,32,1536]{2,1,0:T(8,128)(2,1)S(1)} %fusion.58), channel_id=1, source_target_pairs={{8,0},{16,8},{24,16},{0,24},{9,1},{17,9},{25,17},{1,25},{10,2},{18... | collective-permute-start | bytes 2359304 | tf_op jit(solution)/shard_map/ppermute | solution.py:36
  95.3 27.5 %collective-permute-start.11 = (bf16[8,32,1536]{2,1,0:T(8,128)(2,1)S(1)}, bf16[8,32,1536]{2,1,0:T(8,128)(2,1)S(1)}, u32[]{:S(2)}, u32[]{:S(2)}) collective-permute-start(bf16[8,32,1536]{2,1,0:T(8,128)(2,1)S(1)} %fusion.58), channel_id=1, source_target_pairs={{24,0},{0,8},{8,16},{16,24},{25,1},{1,9},{9,17},{17,25},{26,2},{2,... | collective-permute-start | bytes 2359304 | tf_op jit(solution)/shard_map/ppermute | solution.py:36
  107.6 20.9 %collective-permute-start.24 = (bf16[2,32,1536]{2,1,0:T(8,128)(2,1)S(1)}, bf16[2,32,1536]{2,1,0:T(8,128)(2,1)S(1)}, u32[]{:S(2)}, u32[]{:S(2)}) collective-permute-start(bf16[2,32,1536]{2,1,0:T(8,128)(2,1)S(1)} %slice.125), channel_id=1, source_target_pairs={{2,0},{3,1},{4,2},{5,3},{6,4},{7,5},{0,6},{1,7},{10,8},{11,9},{12,... | collective-permute-start | bytes 589832 | tf_op jit(solution)/shard_map/ppermute | solution.py:36
  112.6 17.9 %collective-permute-start.25 = (bf16[2,32,1536]{2,1,0:T(8,128)(2,1)S(1)}, bf16[2,32,1536]{2,1,0:T(8,128)(2,1)S(1)}, u32[]{:S(2)}, u32[]{:S(2)}) collective-permute-start(bf16[2,32,1536]{2,1,0:T(8,128)(2,1)S(1)} %slice.126), channel_id=1, source_target_pairs={{6,0},{7,1},{0,2},{1,3},{2,4},{3,5},{4,6},{5,7},{14,8},{15,9},{8,1... | collective-permute-start | bytes 589832 | tf_op jit(solution)/shard_map/ppermute | solution.py:36
  115.2 15.4 %collective-permute-start.22 = (bf16[4,32,1536]{2,1,0:T(8,128)(2,1)S(1)}, bf16[4,32,1536]{2,1,0:T(8,128)(2,1)S(1)}, u32[]{:S(2)}, u32[]{:S(2)}) collective-permute-start(bf16[4,32,1536]{2,1,0:T(8,128)(2,1)S(1)} %collective-permute-done.20), channel_id=1, source_target_pairs={{1,0},{2,1},{3,2},{4,3},{5,4},{6,5},{7,6},{0,7},{9,8},{10,9},{11,1... | collective-permute-start | bytes 1179656 | tf_op jit(solution)/shard_map/ppermute | solution.py:36
  120.8 13.8 %collective-permute-start.23 = (bf16[4,32,1536]{2,1,0:T(8,128)(2,1)S(1)}, bf16[4,32,1536]{2,1,0:T(8,128)(2,1)S(1)}, u32[]{:S(2)}, u32[]{:S(2)}) collective-permute-start(bf16[4,32,1536]{2,1,0:T(8,128)(2,1)S(1)} %collective-permute-done.21), channel_id=1, source_target_pairs={{7,0},{0,1},{1,2},{2,3},{3,4},{4,5},{5,6},{6,7},{15,8},{8,9},{9,10... | collective-permute-start | bytes 1179656 | tf_op jit(solution)/shard_map/ppermute | solution.py:36
  122.8 12.9 %collective-permute-start.12 = (bf16[4,32,1536]{2,1,0:T(8,128)(2,1)S(1)}, bf16[4,32,1536]{2,1,0:T(8,128)(2,1)S(1)}, u32[]{:S(2)}, u32[]{:S(2)}) collective-permute-start(bf16[4,32,1536]{2,1,0:T(8,128)(2,1)S(1)} %slice.116), channel_id=1, source_target_pairs={{8,0},{16,8},{24,16},{0,24},{9,1},{17,9},{25,17},{1,25},{10,2},{18... | collective-permute-start | bytes 1179656 | tf_op jit(solution)/shard_map/ppermute | solution.py:36
  140.9 18.3 %collective-permute-start.26 = (f32[2,2,4,2,32,384]{5,4,3,2,1,0:T(8,128)}, f32[2,2,4,2,32,384]{5,4,3,2,1,0:T(8,128)}, u32[]{:S(2)}, u32[]{:S(2)}) collective-permute-start(f32[2,2,4,2,32,384]{5,4,3,2,1,0:T(8,128)} %bitcast.168), channel_id=1, source_target_pairs={{0,32},{32,0},{1,33},{33,1},{2,34},{34,2},{3,35},{35,3},{4,36},{36... | collective-permute-start | bytes 4718600 | tf_op jit(solution)/shard_map/ppermute | solution.py:118
  161.2 27.8 %collective-permute-start.27 = (bf16[128,384]{1,0:T(8,128)(2,1)S(1)}, bf16[128,384]{1,0:T(8,128)(2,1)S(1)}, u32[]{:S(2)}, u32[]{:S(2)}) collective-permute-start(bf16[128,384]{1,0:T(8,128)(2,1)S(1)} %get-tuple-element.18), channel_id=1, source_target_pairs={{256,0},{320,64},{384,128},{448,192},{0,256},{64,320},{128,384},{1... | collective-permute-start | bytes 294920 | tf_op jit(solution)/shard_map/ppermute | solution.py:36
  172.6 18.3 %collective-permute-start.28 = (bf16[128,384]{1,0:T(8,128)(2,1)S(1)}, bf16[128,384]{1,0:T(8,128)(2,1)S(1)}, u32[]{:S(2)}, u32[]{:S(2)}) collective-permute-start(bf16[128,384]{1,0:T(8,128)(2,1)S(1)} %get-tuple-element.24), channel_id=1, source_target_pairs={{320,0},{384,64},{448,128},{0,192},{64,256},{128,320},{192,384},{2... | collective-permute-start | bytes 294920 | tf_op jit(solution)/shard_map/ppermute | solution.py:36
  175.2 22.3 %collective-permute-start.29 = (bf16[128,384]{1,0:T(8,128)(2,1)S(1)}, bf16[128,384]{1,0:T(8,128)(2,1)S(1)}, u32[]{:S(2)}, u32[]{:S(2)}) collective-permute-start(bf16[128,384]{1,0:T(8,128)(2,1)S(1)} %get-tuple-element.23), channel_id=1, source_target_pairs={{192,0},{256,64},{320,128},{384,192},{448,256},{0,320},{64,384},{1... | collective-permute-start | bytes 294920 | tf_op jit(solution)/shard_map/ppermute | solution.py:36
  181.6 16.0 %collective-permute-start.30 = (bf16[128,384]{1,0:T(8,128)(2,1)S(1)}, bf16[128,384]{1,0:T(8,128)(2,1)S(1)}, u32[]{:S(2)}, u32[]{:S(2)}) collective-permute-start(bf16[128,384]{1,0:T(8,128)(2,1)S(1)} %get-tuple-element.22), channel_id=1, source_target_pairs={{384,0},{448,64},{0,128},{64,192},{128,256},{192,320},{256,384},{3... | collective-permute-start | bytes 294920 | tf_op jit(solution)/shard_map/ppermute | solution.py:36
  183.5 14.0 %collective-permute-start.31 = (bf16[128,384]{1,0:T(8,128)(2,1)S(1)}, bf16[128,384]{1,0:T(8,128)(2,1)S(1)}, u32[]{:S(2)}, u32[]{:S(2)}) collective-permute-start(bf16[128,384]{1,0:T(8,128)(2,1)S(1)} %get-tuple-element.21), channel_id=1, source_target_pairs={{128,0},{192,64},{256,128},{320,192},{384,256},{448,320},{0,384},{... | collective-permute-start | bytes 294920 | tf_op jit(solution)/shard_map/ppermute | solution.py:36
  (34 other events, 367.6 us)
Sparse Core Ops, SparseCore 0:
  51.6 42.6 all-gather.2

commit v3 on v1

v3 whole, which is shorter than its diff:
```python
import jax
import jax.numpy as jnp
from jax import lax
from jax.sharding import Mesh, PartitionSpec as P

ROW = ("z", "core")
COL = ("x", "y")
ALL = ROW + COL
BF, F32 = jnp.bfloat16, jnp.float32
PART = 32


def gelu_prime(value):
    inner = 0.7978845608 * (value + 0.044715 * value * value * value)
    tanh_val = jnp.tanh(inner)
    slope = 0.7978845608 * (1.0 + 0.134145 * value * value)
    return 0.5 * (1.0 + tanh_val) + 0.5 * value * (1.0 - tanh_val * tanh_val) * slope


def slot_of(row, q):
    z, core = row // 2, row % 2
    x, y = q * 2 + z // 4, core * 4 + z % 4
    return x * 8 + y


def to_slots(swap):
    pairs = []
    for row in range(16):
        for col in range(32):
            q = (col % 2) ^ swap
            pairs.append((row * 32 + col, (col // 2) * 32 + slot_of(row, q)))
    return pairs


def exchange(block, axis, size, turn):
    pairs = []
    for core in range(2):
        for i in range(size):
            step = 1 if (i + core + turn) % 2 == 0 else -1
            pairs.append((core * size + i, core * size + (i + step) % size))
    return lax.ppermute(block, ("core", axis), pairs)


def dot(a, b, dims):
    return lax.dot_general(a, b, (dims, ((), ())), preferred_element_type=F32)


def line_of_4(mine, axis):
    first = jnp.stack([mine, exchange(mine, axis, 4, 0)])
    return [((0, 1), first), ((-1, -2), exchange(first, axis, 4, 1))]


def line_of_8(mine, axis):
    first = jnp.stack([mine, exchange(mine, axis, 8, 0)])
    second = exchange(first, axis, 8, 1)
    third = exchange(second, axis, 8, 0)
    fourth = exchange(third, axis, 8, 1)
    return [((0, 1), first), ((-1, -2), second), ((2, 3), third), ((-3, -4), fourth)]


def place(pairs, at, size, sign):
    block = pairs[0][1]
    whole = jnp.zeros((size, *block.shape[1:]), block.dtype)
    for steps, pair in pairs:
        for i, k in enumerate(steps):
            start = ((at + k * sign) & (size - 1),) + (0,) * (block.ndim - 1)
            whole = lax.dynamic_update_slice(whole, pair[i : i + 1], start)
    return whole


def products(pairs, weight_t, tokens_of, at, size, sign, total):
    shares = []
    for steps, pair in pairs:
        flat = pair.reshape(-1, 1536)
        share = dot(flat, weight_t, ((1,), (0,)))
        shares.append((steps, share.reshape(*pair.shape[:-1], 384)))
        tokens = [
            lax.dynamic_index_in_dim(tokens_of, (at + k * sign) & (size - 1), 0, False)
            for k in steps
        ]
        total = total + dot(flat, jnp.concatenate(tokens, axis=0), ((0,), (0,)))
    return shares, total


def on_device(inputs, pre_act, grad_act, weight_t):
    z, core, x, y = (lax.axis_index(a) for a in ALL)
    hidden = (grad_act.astype(F32) * gelu_prime(pre_act.astype(F32))).astype(BF)
    h = y % 2
    q = x // 2
    same = lax.dynamic_slice_in_dim(hidden, h * 64, 64, 0)
    other = lax.dynamic_slice_in_dim(hidden, (1 - h) * 64, 64, 0)
    same = lax.ppermute(same, ALL, to_slots(0))
    other = lax.ppermute(other, ALL, to_slots(1))
    low = jnp.where(q == 0, same, other)
    high = jnp.where(q == 0, other, same)
    slot = jnp.concatenate([low, high], axis=1)
    part_a, part_b = slot[:PART], slot[PART:]

    all_inputs = lax.all_gather(inputs, ROW, axis=0)
    seen = all_inputs.reshape(2, 4, 2, 2, 2, PART, 384)
    in_a = seen[:, :, :, :, 0].transpose(3, 0, 2, 1, 4, 5).reshape(4, 8 * PART, 384)
    in_b = seen[:, :, :, :, 1].transpose(2, 1, 3, 0, 4, 5).reshape(8, 4 * PART, 384)

    sign_x = 1 - 2 * ((x + core) & 1)
    sign_y = 1 - 2 * ((y + core) & 1)
    lines_b = place(line_of_4(part_b, "x"), x, 4, sign_x)
    lines_a = place(line_of_8(part_a, "y"), y, 8, sign_y)
    pairs_a = line_of_4(lines_a, "x")
    pairs_b = line_of_8(lines_b, "y")
    shares_a, total = products(pairs_a, weight_t, in_a, x, 4, sign_x, 0.0)
    shares_b, total = products(pairs_b, weight_t, in_b, y, 8, sign_y, total)
    grad_weight = total.astype(BF)

    share_a = place(shares_a, x, 4, sign_x).reshape(2, 2, 2, 4, PART, 384)
    share_b = place(shares_b, y, 8, sign_y).reshape(2, 4, 2, 2, PART, 384).transpose(2, 3, 0, 1, 4, 5)
    share = jnp.stack([share_a, share_b], axis=4)
    keep = lax.dynamic_index_in_dim(share, core, 2, False)
    give = lax.dynamic_index_in_dim(share, 1 - core, 2, False).astype(BF)
    both = keep + lax.ppermute(give, "core", [(0, 1), (1, 0)]).astype(F32)
    sent = both.astype(BF).transpose(1, 2, 0, 3, 4, 5).reshape(8, 128, 384)
    parts = lax.all_to_all(sent, "z", 0, 0)
    grad_inputs = parts.astype(F32).sum(axis=0).astype(BF)
    return (grad_inputs, grad_weight)


def solution(mesh):
    fine = Mesh(mesh.devices.reshape(8, 2, 4, 8), ALL)
    placed = P(ROW, COL)
    return jax.shard_map(
        on_device,
        mesh=fine,
        in_specs=(placed,) * 4,
        out_specs=(placed, placed),
        check_vma=False,
    )
```

time: 385 us -> 197 us (0.51)
  waiting for transfers between devices: 338 us -> 47.6 us
  starting transfers between devices: 4.79 us -> 92.4 us
  local copies, waits for them, and re-layouts: 3.92 us -> 12.4 us
    all_gather x2 -> x0, waiting for transfers between devices: 172 us -> none  [on_device(): block = lax.all_gather(mine[k * size:(k + 1) * size], COL, axis=0)]
    reduce_scatter x2 -> x0, waiting for transfers between devices: 114 us -> none  [on_device(): shares.append(lax.psum_scatter(share, ROW, scatter_dimension=0, tiled=True))]
    ppermute x1 -> x15, starting transfers between devices: 4.59 us -> 72.4 us  [the longest x12 41.9 us: exchange(): return lax.ppermute(block, ('core', axis), pairs)]
    all_gather x1, waiting for transfers between devices: 36.5 us -> 0.01 us  [on_device(): all_inputs = lax.all_gather(inputs, ROW, axis=0)]
    all_to_all x0 -> x1, starting transfers between devices: none -> 20 us  [on_device(): parts = lax.all_to_all(sent, 'z', 0, 0)]
    all_to_all x0 -> x1, waiting for transfers between devices: none -> 17 us  [on_device(): parts = lax.all_to_all(sent, 'z', 0, 0)]
    ppermute x1 -> x15, waiting for transfers between devices: 14.2 us -> 30.6 us  [the longest x12 28.3 us: exchange(): return lax.ppermute(block, ('core', axis), pairs)]
    dynamic_update_slice x0 -> x22, local copies, waits for them, and re-layouts: none -> 5.88 us  [place(): whole = lax.dynamic_update_slice(whole, pair[i:i + 1], start)]
  transfers between devices with their start and end apart: 6 -> 17, of which waited for: 6 -> 8; matrix products, arithmetic and copies ran while one was open for 6% -> 14% of each run, Pallas kernels for 0% -> 0%
where the time goes in v3:
time: 197 us; the launch traced here: 194 us
  starting transfers between devices  92.4 us (47%)
  waiting for transfers between devices  47.6 us (24%)
  matrix products  19 us (10%)
  between operations  14.8 us (8%)
  local copies, waits for them, and re-layouts  12.4 us (6%)
  other arithmetic  7.43 us (4%)
    ppermute x12, starting transfers between devices, exchange(): return lax.ppermute(block, ('core', axis), pairs)  41.9 us
    ppermute x12, waiting for transfers between devices, exchange(): return lax.ppermute(block, ('core', axis), pairs)  28.3 us
    all_to_all x1, starting transfers between devices, on_device(): parts = lax.all_to_all(sent, 'z', 0, 0)  20 us
    dot_general x12, matrix products, dot(): return lax.dot_general(a, b, (dims, ((), ())), preferred_element_type=F32)  19 us
    all_to_all x1, waiting for transfers between devices, on_device(): parts = lax.all_to_all(sent, 'z', 0, 0)  17 us
    ppermute x1, starting transfers between devices, on_device(): other = lax.ppermute(other, ALL, to_slots(1))  12.9 us
    ppermute x1, starting transfers between devices, on_device(): same = lax.ppermute(same, ALL, to_slots(0))  8.84 us
    ppermute x1, starting transfers between devices, on_device(): both = keep + lax.ppermute(give, 'core', [(0, 1), (1, 0)]).astype(F32)  8.77 us
  transfers between devices with their start and end apart: 17, of which 8 were waited for; matrix products, arithmetic and copies ran while one was open for 14% of the time, Pallas kernels for 0%

profile of v3, /device:TPU:1, one launch (start us, length us, event | category | flops | bytes accessed | tf_op | source)
XLA Modules:
  0.0 193.7 jit_solution(12856337356001039895)
XLA Ops:
  8.7 8.8 %collective-permute-start = (bf16[64,768]{1,0:T(8,128)(2,1)S(1)}, bf16[64,768]{1,0:T(8,128)(2,1)S(1)}, u32[]{:S(2)}, u32[]{:S(2)}) collective-permute-start(bf16[64,768]{1,0:T(8,128)(2,1)S(1)} %get-tuple-element.36), channel_id=1, source_target_pairs={{0,0},{1,16},{2,32},{3,48},{4,64},{5,80},{6,96},{7,112},{8,128},{9... | collective-permute-start | bytes 294920 | tf_op jit(solution)/shard_map/ppermute | solution.py:92
  17.5 12.9 %collective-permute-start.1 = (bf16[64,768]{1,0:T(8,128)(2,1)S(1)}, bf16[64,768]{1,0:T(8,128)(2,1)S(1)}, u32[]{:S(2)}, u32[]{:S(2)}) collective-permute-start(bf16[64,768]{1,0:T(8,128)(2,1)S(1)} %get-tuple-element.37), channel_id=1, source_target_pairs={{0,16},{1,0},{2,48},{3,32},{4,80},{5,64},{6,112},{7,96},{8,144},{9... | collective-permute-start | bytes 294920 | tf_op jit(solution)/shard_map/ppermute | solution.py:93
  32.8 2.8 %collective-permute-start.2 = (bf16[32,1536]{1,0:T(8,128)(2,1)S(1)}, bf16[32,1536]{1,0:T(8,128)(2,1)S(1)}, u32[]{:S(2)}, u32[]{:S(2)}) collective-permute-start(bf16[32,1536]{1,0:T(8,128)(2,1)S(1)} %get-tuple-element.3), channel_id=1, source_target_pairs={{0,1},{1,0},{2,3},{3,2},{4,5},{5,4},{6,7},{7,6},{32,39},{33,34},{3... | collective-permute-start | bytes 294920 | tf_op jit(solution)/shard_map/ppermute | solution.py:41
  35.7 10.5 %collective-permute-start.8 = (bf16[32,1536]{1,0:T(8,128)(2,1)S(1)}, bf16[32,1536]{1,0:T(8,128)(2,1)S(1)}, u32[]{:S(2)}, u32[]{:S(2)}) collective-permute-start(bf16[32,1536]{1,0:T(8,128)(2,1)S(1)} %get-tuple-element.33), channel_id=1, source_target_pairs={{0,8},{8,0},{16,24},{24,16},{32,56},{40,48},{48,40},{56,32},{1,9},... | collective-permute-start | bytes 294920 | tf_op jit(solution)/shard_map/ppermute | solution.py:41
  46.2 2.3 %collective-permute-start.3 = (bf16[2,32,1536]{2,1,0:T(8,128)(2,1)S(1)}, bf16[2,32,1536]{2,1,0:T(8,128)(2,1)S(1)}, u32[]{:S(2)}, u32[]{:S(2)}) collective-permute-start(bf16[2,32,1536]{2,1,0:T(8,128)(2,1)S(1)} %pad_maximum_fusion.2), channel_id=1, source_target_pairs={{0,7},{1,2},{2,1},{3,4},{4,3},{5,6},{6,5},{7,0},{32,33},{33,32},{3... | collective-permute-start | bytes 589832 | tf_op jit(solution)/shard_map/ppermute | solution.py:41
  50.5 4.7 %collective-permute-done.9 = bf16[2,32,1536]{2,1,0:T(8,128)(2,1)S(1)} collective-permute-done((bf16[2,32,1536]{2,1,0:T(8,128)(2,1)S(1)}, bf16[2,32,1536]{2,1,0:T(8,128)(2,1)S(1)}, u32[]{:S(2)}, u32[]{:S(2)}) %collective-permute-start.9) | collective-permute-done | bytes 196640 | tf_op jit(solution)/shard_map/ppermute | solution.py:41
  55.3 4.2 %collective-permute-start.10 = (bf16[4,32,1536]{2,1,0:T(8,128)(2,1)S(1)}, bf16[4,32,1536]{2,1,0:T(8,128)(2,1)S(1)}, u32[]{:S(2)}, u32[]{:S(2)}) collective-permute-start(bf16[4,32,1536]{2,1,0:T(8,128)(2,1)S(1)} %slice_dynamic-update-slice_fusion), channel_id=1, source_target_pairs={{0,1},{1,0},{2,3},{3,2},{4,5},{5,4},{6,7},{7,6},{32,39},{33,34},{3... | collective-permute-start | bytes 1179656 | tf_op jit(solution)/shard_map/ppermute | solution.py:41
  59.5 2.3 %collective-permute-start.4 = (bf16[2,32,1536]{2,1,0:T(8,128)(2,1)S(1)}, bf16[2,32,1536]{2,1,0:T(8,128)(2,1)S(1)}, u32[]{:S(2)}, u32[]{:S(2)}) collective-permute-start(bf16[2,32,1536]{2,1,0:T(8,128)(2,1)S(1)} %collective-permute-done.3), channel_id=1, source_target_pairs={{0,1},{1,0},{2,3},{3,2},{4,5},{5,4},{6,7},{7,6},{32,39},{33,34},{3... | collective-permute-start | bytes 589832 | tf_op jit(solution)/shard_map/ppermute | solution.py:41
  61.9 5.6 %collective-permute-done.4 = bf16[2,32,1536]{2,1,0:T(8,128)(2,1)S(1)} collective-permute-done((bf16[2,32,1536]{2,1,0:T(8,128)(2,1)S(1)}, bf16[2,32,1536]{2,1,0:T(8,128)(2,1)S(1)}, u32[]{:S(2)}, u32[]{:S(2)}) %collective-permute-start.4) | collective-permute-done | bytes 196640 | tf_op jit(solution)/shard_map/ppermute | solution.py:41
  67.5 3.5 %collective-permute-start.5 = (bf16[2,32,1536]{2,1,0:T(8,128)(2,1)S(1)}, bf16[2,32,1536]{2,1,0:T(8,128)(2,1)S(1)}, u32[]{:S(2)}, u32[]{:S(2)}) collective-permute-start(bf16[2,32,1536]{2,1,0:T(8,128)(2,1)S(1)} %collective-permute-done.4), channel_id=1, source_target_pairs={{0,7},{1,2},{2,1},{3,4},{4,3},{5,6},{6,5},{7,0},{32,33},{33,32},{3... | collective-permute-start | bytes 589832 | tf_op jit(solution)/shard_map/ppermute | solution.py:41
  71.1 3.4 %collective-permute-done.5 = bf16[2,32,1536]{2,1,0:T(8,128)(2,1)S(1)} collective-permute-done((bf16[2,32,1536]{2,1,0:T(8,128)(2,1)S(1)}, bf16[2,32,1536]{2,1,0:T(8,128)(2,1)S(1)}, u32[]{:S(2)}, u32[]{:S(2)}) %collective-permute-start.5) | collective-permute-done | bytes 196640 | tf_op jit(solution)/shard_map/ppermute | solution.py:41
  74.5 4.2 %collective-permute-start.6 = (bf16[8,32,1536]{2,1,0:T(8,128)(2,1)S(1)}, bf16[8,32,1536]{2,1,0:T(8,128)(2,1)S(1)}, u32[]{:S(2)}, u32[]{:S(2)}) collective-permute-start(bf16[8,32,1536]{2,1,0:T(8,128)(2,1)S(1)} %slice_dynamic-update-slice_fusion.2), channel_id=1, source_target_pairs={{0,8},{8,0},{16,24},{24,16},{32,56},{40,48},{48,40},{56,32},{1,9},... | collective-permute-start | bytes 2359304 | tf_op jit(solution)/shard_map/ppermute | solution.py:41
  84.2 4.6 %collective-permute-done.6 = bf16[8,32,1536]{2,1,0:T(8,128)(2,1)S(1)} collective-permute-done((bf16[8,32,1536]{2,1,0:T(8,128)(2,1)S(1)}, bf16[8,32,1536]{2,1,0:T(8,128)(2,1)S(1)}, u32[]{:S(2)}, u32[]{:S(2)}) %collective-permute-start.6) | collective-permute-done | bytes 786464 | tf_op jit(solution)/shard_map/ppermute | solution.py:41
  92.0 4.3 %collective-permute-start.12 = (bf16[2,4,32,1536]{3,2,1,0:T(8,128)(2,1)S(1)}, bf16[2,4,32,1536]{3,2,1,0:T(8,128)(2,1)S(1)}, u32[]{:S(2)}, u32[]{:S(2)}) collective-permute-start(bf16[2,4,32,1536]{3,2,1,0:T(8,128)(2,1)S(1)} %collective-permute-done.11), channel_id=1, source_target_pairs={{0,1},{1,0},{2,3},{3,2},{4,5},{5,4},{6,7},{7,6},{32,39},{33,34},{3... | collective-permute-start | bytes 2359304 | tf_op jit(solution)/shard_map/ppermute | solution.py:41
  96.9 2.4 %fusion.51 = f32[512,384]{1,0:T(8,128)S(1)} fusion(bf16[512,1536]{1,0:T(8,128)(2,1)} %bitcast.4, bf16[1536,384]{1,0:T(8,128)(2,1)S(1)} %copy-done), kind=kOutput, calls=%fused_computation.115 | convolution fusion | flops 603979776 | bytes 3538944 | tf_op jit(solution)/shard_map/dot_general | solution.py:45
  101.0 5.3 %collective-permute-done.12 = bf16[2,4,32,1536]{3,2,1,0:T(8,128)(2,1)S(1)} collective-permute-done((bf16[2,4,32,1536]{3,2,1,0:T(8,128)(2,1)S(1)}, bf16[2,4,32,1536]{3,2,1,0:T(8,128)(2,1)S(1)}, u32[]{:S(2)}, u32[]{:S(2)}) %collective-permute-start.12) | collective-permute-done | bytes 786464 | tf_op jit(solution)/shard_map/ppermute | solution.py:41
  112.4 2.4 %fusion.52 = f32[512,384]{1,0:T(8,128)S(1)} fusion(bf16[512,1536]{1,0:T(8,128)(2,1)} %bitcast.9, bf16[1536,384]{1,0:T(8,128)(2,1)S(1)} %copy-done), kind=kOutput, calls=%fused_computation.116 | convolution fusion | flops 603979776 | bytes 3538944 | tf_op jit(solution)/shard_map/dot_general | solution.py:45
  114.8 4.7 %collective-permute-done.13 = bf16[2,4,32,1536]{3,2,1,0:T(8,128)(2,1)} collective-permute-done((bf16[2,4,32,1536]{3,2,1,0:T(8,128)(2,1)S(1)}, bf16[2,4,32,1536]{3,2,1,0:T(8,128)(2,1)}, u32[]{:S(2)}, u32[]{:S(2)}) %collective-permute-start.13) | collective-permute-done | bytes 786464 | tf_op jit(solution)/shard_map/ppermute | solution.py:41
  124.0 8.8 %collective-permute-start.14 = (bf16[2,2,4,2,32,384]{5,4,1,0,2,3:T(8,128)(2,1)S(1)}, bf16[2,2,4,2,32,384]{5,4,1,0,2,3:T(8,128)(2,1)S(1)}, u32[]{:S(2)}, u32[]{:S(2)}) collective-permute-start(bf16[2,2,4,2,32,384]{5,4,1,0,2,3:T(8,128)(2,1)S(1)} %fusion.8), channel_id=1, source_target_pairs={{0,32},{32,0},{1,33},{33,1},{2,34},{34,2},{3,35},{35,3},{4,36},{36... | collective-permute-start | bytes 2359304 | tf_op jit(solution)/shard_map/ppermute | solution.py:119
  133.7 2.4 %fusion.21 = f32[1536,384]{1,0:T(8,128)S(1)} fusion(bf16[512,1536]{1,0:T(8,128)(2,1)} %bitcast.9, bf16[256,384]{1,0:T(8,128)(2,1)S(1)} %get-tuple-element.17, bf16[256,384]{1,0:T(8,128)(2,1)S(1)} %get-tuple-element.18), kind=kOutput, calls=%fused_computation.41 | convolution fusion | flops 604766208 | bytes 4325376 | tf_op jit(solution)/shard_map/dot_general | solution.py:45
  136.1 2.6 %convolution_add_fusion.4 = f32[1536,384]{1,0:T(8,128)S(1)} fusion(f32[1536,384]{1,0:T(8,128)S(1)} %fusion.21, bf16[512,1536]{1,0:T(8,128)(2,1)} %bitcast.4, bf16[256,384]{1,0:T(8,128)(2,1)S(1)} %get-tuple-element.19, bf16[256,384]{1,0:T(8,128)(2,1)S(1)} %get-tuple-element.16), kind=kOutput, calls=%fused_computation.8 | convolution fusion | flops 605356032 | bytes 6684672 | tf_op jit(solution)/shard_map/dot_general | solution.py:45
  141.2 20.0 %all-to-all-start = ((bf16[8,128,384]{2,1,0:T(8,128)(2,1)}), bf16[8,128,384]{2,1,0:T(8,128)(2,1)}, u32[]{:S(2)}, u32[]{:S(2)}) async-start(bf16[8,128,384]{2,1,0:T(8,128)(2,1)} %bitcast.115), calls=%async_computation | async-start | bytes 1572864 | tf_op jit(solution)/shard_map/all_to_all | solution.py:121
  165.2 2.8 %fusion = bf16[1536,384]{1,0:T(8,128)(2,1)} fusion(f32[1536,384]{1,0:T(8,128)S(1)} %convolution_add_fusion.1, bf16[256,1536]{1,0:T(8,128)(2,1)} %bitcast.28, bf16[128,384]{1,0:T(8,128)(2,1)S(1)} %copy-done.9, bf16[128,384]{1,0:T(8,128)(2,1)S(1)} %copy-done.8), kind=kOutput, calls=%fused_computation.9 | convolution fusion | flops 303562752 | bytes 4521984 | tf_op jit(solution)/shard_map/dot_general | solution.py:45
  167.9 17.0 %all-to-all-done = bf16[8,128,384]{2,1,0:T(8,128)(2,1)} async-done(((bf16[8,128,384]{2,1,0:T(8,128)(2,1)}), bf16[8,128,384]{2,1,0:T(8,128)(2,1)}, u32[]{:S(2)}, u32[]{:S(2)}) %all-to-all-start) | async-done | bytes 786464 | tf_op jit(solution)/shard_map/all_to_all | solution.py:121
  (100 shorter events, 36.6 us)
Async XLA Ops:
  7.2 73.6 %copy-start = (bf16[1536,384]{1,0:T(8,128)(2,1)S(1)}, bf16[1536,384]{1,0:T(8,128)(2,1)}, u32[]{:S(2)}) copy-start(bf16[1536,384]{1,0:T(8,128)(2,1)} %param.7) | copy-start | bytes 3538948
  7.2 103.3 %all-gather.3.cloned.1.call-start = ((), (), s32[]{:S(2)}) async-start(), calls=%async_computation.1 | async-start | bytes 1671168 | tf_op jit(solution)/shard_map/all_gather | solution.py:99
  8.7 21.8 %collective-permute-start = (bf16[64,768]{1,0:T(8,128)(2,1)S(1)}, bf16[64,768]{1,0:T(8,128)(2,1)S(1)}, u32[]{:S(2)}, u32[]{:S(2)}) collective-permute-start(bf16[64,768]{1,0:T(8,128)(2,1)S(1)} %get-tuple-element.36), channel_id=1, source_target_pairs={{0,0},{1,16},{2,32},{3,48},{4,64},{5,80},{6,96},{7,112},{8,128},{9... | collective-permute-start | bytes 294920 | tf_op jit(solution)/shard_map/ppermute | solution.py:92
  17.5 15.2 %collective-permute-start.1 = (bf16[64,768]{1,0:T(8,128)(2,1)S(1)}, bf16[64,768]{1,0:T(8,128)(2,1)S(1)}, u32[]{:S(2)}, u32[]{:S(2)}) collective-permute-start(bf16[64,768]{1,0:T(8,128)(2,1)S(1)} %get-tuple-element.37), channel_id=1, source_target_pairs={{0,16},{1,0},{2,48},{3,32},{4,80},{5,64},{6,112},{7,96},{8,144},{9... | collective-permute-start | bytes 294920 | tf_op jit(solution)/shard_map/ppermute | solution.py:93
  32.8 13.4 %collective-permute-start.2 = (bf16[32,1536]{1,0:T(8,128)(2,1)S(1)}, bf16[32,1536]{1,0:T(8,128)(2,1)S(1)}, u32[]{:S(2)}, u32[]{:S(2)}) collective-permute-start(bf16[32,1536]{1,0:T(8,128)(2,1)S(1)} %get-tuple-element.3), channel_id=1, source_target_pairs={{0,1},{1,0},{2,3},{3,2},{4,5},{5,4},{6,7},{7,6},{32,39},{33,34},{3... | collective-permute-start | bytes 294920 | tf_op jit(solution)/shard_map/ppermute | solution.py:41
  35.7 12.8 %collective-permute-start.8 = (bf16[32,1536]{1,0:T(8,128)(2,1)S(1)}, bf16[32,1536]{1,0:T(8,128)(2,1)S(1)}, u32[]{:S(2)}, u32[]{:S(2)}) collective-permute-start(bf16[32,1536]{1,0:T(8,128)(2,1)S(1)} %get-tuple-element.33), channel_id=1, source_target_pairs={{0,8},{8,0},{16,24},{24,16},{32,56},{40,48},{48,40},{56,32},{1,9},... | collective-permute-start | bytes 294920 | tf_op jit(solution)/shard_map/ppermute | solution.py:41
  46.2 13.3 %collective-permute-start.3 = (bf16[2,32,1536]{2,1,0:T(8,128)(2,1)S(1)}, bf16[2,32,1536]{2,1,0:T(8,128)(2,1)S(1)}, u32[]{:S(2)}, u32[]{:S(2)}) collective-permute-start(bf16[2,32,1536]{2,1,0:T(8,128)(2,1)S(1)} %pad_maximum_fusion.2), channel_id=1, source_target_pairs={{0,7},{1,2},{2,1},{3,4},{4,3},{5,6},{6,5},{7,0},{32,33},{33,32},{3... | collective-permute-start | bytes 589832 | tf_op jit(solution)/shard_map/ppermute | solution.py:41
  48.6 6.7 %collective-permute-start.9 = (bf16[2,32,1536]{2,1,0:T(8,128)(2,1)S(1)}, bf16[2,32,1536]{2,1,0:T(8,128)(2,1)S(1)}, u32[]{:S(2)}, u32[]{:S(2)}) collective-permute-start(bf16[2,32,1536]{2,1,0:T(8,128)(2,1)S(1)} %pad_maximum_fusion.3), channel_id=1, source_target_pairs={{0,24},{8,16},{16,8},{24,0},{32,40},{40,32},{48,56},{56,48},{1,25}... | collective-permute-start | bytes 589832 | tf_op jit(solution)/shard_map/ppermute | solution.py:41
  55.3 23.4 %collective-permute-start.10 = (bf16[4,32,1536]{2,1,0:T(8,128)(2,1)S(1)}, bf16[4,32,1536]{2,1,0:T(8,128)(2,1)S(1)}, u32[]{:S(2)}, u32[]{:S(2)}) collective-permute-start(bf16[4,32,1536]{2,1,0:T(8,128)(2,1)S(1)} %slice_dynamic-update-slice_fusion), channel_id=1, source_target_pairs={{0,1},{1,0},{2,3},{3,2},{4,5},{5,4},{6,7},{7,6},{32,39},{33,34},{3... | collective-permute-start | bytes 1179656 | tf_op jit(solution)/shard_map/ppermute | solution.py:41
  59.5 8.0 %collective-permute-start.4 = (bf16[2,32,1536]{2,1,0:T(8,128)(2,1)S(1)}, bf16[2,32,1536]{2,1,0:T(8,128)(2,1)S(1)}, u32[]{:S(2)}, u32[]{:S(2)}) collective-permute-start(bf16[2,32,1536]{2,1,0:T(8,128)(2,1)S(1)} %collective-permute-done.3), channel_id=1, source_target_pairs={{0,1},{1,0},{2,3},{3,2},{4,5},{5,4},{6,7},{7,6},{32,39},{33,34},{3... | collective-permute-start | bytes 589832 | tf_op jit(solution)/shard_map/ppermute | solution.py:41
  67.5 7.0 %collective-permute-start.5 = (bf16[2,32,1536]{2,1,0:T(8,128)(2,1)S(1)}, bf16[2,32,1536]{2,1,0:T(8,128)(2,1)S(1)}, u32[]{:S(2)}, u32[]{:S(2)}) collective-permute-start(bf16[2,32,1536]{2,1,0:T(8,128)(2,1)S(1)} %collective-permute-done.4), channel_id=1, source_target_pairs={{0,7},{1,2},{2,1},{3,4},{4,3},{5,6},{6,5},{7,0},{32,33},{33,32},{3... | collective-permute-start | bytes 589832 | tf_op jit(solution)/shard_map/ppermute | solution.py:41
  74.5 14.2 %collective-permute-start.6 = (bf16[8,32,1536]{2,1,0:T(8,128)(2,1)S(1)}, bf16[8,32,1536]{2,1,0:T(8,128)(2,1)S(1)}, u32[]{:S(2)}, u32[]{:S(2)}) collective-permute-start(bf16[8,32,1536]{2,1,0:T(8,128)(2,1)S(1)} %slice_dynamic-update-slice_fusion.2), channel_id=1, source_target_pairs={{0,8},{8,0},{16,24},{24,16},{32,56},{40,48},{48,40},{56,32},{1,9},... | collective-permute-start | bytes 2359304 | tf_op jit(solution)/shard_map/ppermute | solution.py:41
  78.8 2.6 %copy-start.3 = (bf16[2,4,32,1536]{3,2,1,0:T(8,128)(2,1)}, bf16[2,4,32,1536]{3,2,1,0:T(8,128)(2,1)S(1)}, u32[]{:S(2)}) copy-start(bf16[2,4,32,1536]{3,2,1,0:T(8,128)(2,1)S(1)} %pad_maximum_fusion.1) | copy-start | bytes 2359300
  78.8 13.2 %collective-permute-start.11 = (bf16[2,4,32,1536]{3,2,1,0:T(8,128)(2,1)S(1)}, bf16[2,4,32,1536]{3,2,1,0:T(8,128)(2,1)S(1)}, u32[]{:S(2)}, u32[]{:S(2)}) collective-permute-start(bf16[2,4,32,1536]{3,2,1,0:T(8,128)(2,1)S(1)} %pad_maximum_fusion.1), channel_id=1, source_target_pairs={{0,7},{1,2},{2,1},{3,4},{4,3},{5,6},{6,5},{7,0},{32,33},{33,32},{3... | collective-permute-start | bytes 2359304 | tf_op jit(solution)/shard_map/ppermute | solution.py:41
  90.1 22.3 %collective-permute-start.7 = (bf16[2,8,32,1536]{3,2,1,0:T(8,128)(2,1)}, bf16[2,8,32,1536]{3,2,1,0:T(8,128)(2,1)}, u32[]{:S(2)}, u32[]{:S(2)}) collective-permute-start(bf16[2,8,32,1536]{3,2,1,0:T(8,128)(2,1)} %pad_maximum_fusion), channel_id=1, source_target_pairs={{0,24},{8,16},{16,8},{24,0},{32,40},{40,32},{48,56},{56,48},{1,25}... | collective-permute-start | bytes 4718600 | tf_op jit(solution)/shard_map/ppermute | solution.py:41
  92.0 7.3 %copy-start.4 = (bf16[2,4,32,1536]{3,2,1,0:T(8,128)(2,1)}, bf16[2,4,32,1536]{3,2,1,0:T(8,128)(2,1)S(1)}, u32[]{:S(2)}) copy-start(bf16[2,4,32,1536]{3,2,1,0:T(8,128)(2,1)S(1)} %collective-permute-done.11) | copy-start | bytes 2359300
  92.0 14.3 %collective-permute-start.12 = (bf16[2,4,32,1536]{3,2,1,0:T(8,128)(2,1)S(1)}, bf16[2,4,32,1536]{3,2,1,0:T(8,128)(2,1)S(1)}, u32[]{:S(2)}, u32[]{:S(2)}) collective-permute-start(bf16[2,4,32,1536]{3,2,1,0:T(8,128)(2,1)S(1)} %collective-permute-done.11), channel_id=1, source_target_pairs={{0,1},{1,0},{2,3},{3,2},{4,5},{5,4},{6,7},{7,6},{32,39},{33,34},{3... | collective-permute-start | bytes 2359304 | tf_op jit(solution)/shard_map/ppermute | solution.py:41
  106.3 2.8 %copy-start.6 = (bf16[2,4,32,1536]{3,2,1,0:T(8,128)(2,1)}, bf16[2,4,32,1536]{3,2,1,0:T(8,128)(2,1)S(1)}, u32[]{:S(2)}) copy-start(bf16[2,4,32,1536]{3,2,1,0:T(8,128)(2,1)S(1)} %collective-permute-done.12) | copy-start | bytes 2359300
  106.3 13.1 %collective-permute-start.13 = (bf16[2,4,32,1536]{3,2,1,0:T(8,128)(2,1)S(1)}, bf16[2,4,32,1536]{3,2,1,0:T(8,128)(2,1)}, u32[]{:S(2)}, u32[]{:S(2)}) collective-permute-start(bf16[2,4,32,1536]{3,2,1,0:T(8,128)(2,1)S(1)} %collective-permute-done.12), channel_id=1, source_target_pairs={{0,7},{1,2},{2,1},{3,4},{4,3},{5,6},{6,5},{7,0},{32,33},{33,32},{3... | collective-permute-start | bytes 2359304 | tf_op jit(solution)/shard_map/ppermute | solution.py:41
  121.3 2.7 %copy-start.1 = (f32[4,8,32,384]{3,2,0,1:T(8,128)}, f32[4,8,32,384]{3,2,0,1:T(8,128)S(1)}, u32[]{:S(2)}) copy-start(f32[4,8,32,384]{3,2,0,1:T(8,128)S(1)} %constant_dynamic-update-slice_fusion.10) | copy-start | bytes 4718596
  124.0 14.7 %collective-permute-start.14 = (bf16[2,2,4,2,32,384]{5,4,1,0,2,3:T(8,128)(2,1)S(1)}, bf16[2,2,4,2,32,384]{5,4,1,0,2,3:T(8,128)(2,1)S(1)}, u32[]{:S(2)}, u32[]{:S(2)}) collective-permute-start(bf16[2,2,4,2,32,384]{5,4,1,0,2,3:T(8,128)(2,1)S(1)} %fusion.8), channel_id=1, source_target_pairs={{0,32},{32,0},{1,33},{33,1},{2,34},{34,2},{3,35},{35,3},{4,36},{36... | collective-permute-start | bytes 2359304 | tf_op jit(solution)/shard_map/ppermute | solution.py:119
  136.1 2.6 %copy-start.2 = (f32[4,8,32,384]{3,2,0,1:T(8,128)S(1)}, f32[4,8,32,384]{3,2,0,1:T(8,128)}, u32[]{:S(2)}) copy-start(f32[4,8,32,384]{3,2,0,1:T(8,128)} %copy-done.1) | copy-start | bytes 4718596
  141.2 43.8 %all-to-all-start = ((bf16[8,128,384]{2,1,0:T(8,128)(2,1)}), bf16[8,128,384]{2,1,0:T(8,128)(2,1)}, u32[]{:S(2)}, u32[]{:S(2)}) async-start(bf16[8,128,384]{2,1,0:T(8,128)(2,1)} %bitcast.115), calls=%async_computation | async-start | bytes 1572864 | tf_op jit(solution)/shard_map/all_to_all | solution.py:121
  161.2 1.9 copy-start.12
  (7 other events, 9.0 us)
Sparse Core Ops, SparseCore 0:
  35.8 48.7 all-gather.2

commit v4 on v3

--- a/solution.py
+++ b/solution.py
@@ -7,7 +7,7 @@
 COL = ("x", "y")
 ALL = ROW + COL
 BF, F32 = jnp.bfloat16, jnp.float32
-PART = 32
+A, B = 24, 40
 
 
 def gelu_prime(value):
@@ -37,25 +37,16 @@
     for core in range(2):
         for i in range(size):
             step = 1 if (i + core + turn) % 2 == 0 else -1
-            pairs.append((core * size + i, core * size + (i + step) % size))
-    return lax.ppermute(block, ("core", axis), pairs)
+            j = (i + step) % size
+            if axis == "z":
+                pairs.append((i * 2 + core, j * 2 + core))
+            else:
+                pairs.append((core * size + i, core * size + j))
+    return lax.ppermute(block, ROW if axis == "z" else ("core", axis), pairs)
 
 
 def dot(a, b, dims):
     return lax.dot_general(a, b, (dims, ((), ())), preferred_element_type=F32)
-
-
-def line_of_4(mine, axis):
-    first = jnp.stack([mine, exchange(mine, axis, 4, 0)])
-    return [((0, 1), first), ((-1, -2), exchange(first, axis, 4, 1))]
-
-
-def line_of_8(mine, axis):
-    first = jnp.stack([mine, exchange(mine, axis, 8, 0)])
-    second = exchange(first, axis, 8, 1)
-    third = exchange(second, axis, 8, 0)
-    fourth = exchange(third, axis, 8, 1)
-    return [((0, 1), first), ((-1, -2), second), ((2, 3), third), ((-3, -4), fourth)]
 
 
 def place(pairs, at, size, sign):
@@ -94,32 +85,66 @@
     low = jnp.where(q == 0, same, other)
     high = jnp.where(q == 0, other, same)
     slot = jnp.concatenate([low, high], axis=1)
-    part_a, part_b = slot[:PART], slot[PART:]
+    part_a, part_b = slot[:A], slot[A:]
 
     all_inputs = lax.all_gather(inputs, ROW, axis=0)
-    seen = all_inputs.reshape(2, 4, 2, 2, 2, PART, 384)
-    in_a = seen[:, :, :, :, 0].transpose(3, 0, 2, 1, 4, 5).reshape(4, 8 * PART, 384)
-    in_b = seen[:, :, :, :, 1].transpose(2, 1, 3, 0, 4, 5).reshape(8, 4 * PART, 384)
+    seen = all_inputs.reshape(2, 4, 2, 2, 64, 384)
+    in_a = seen[:, :, :, :, :A].transpose(3, 0, 2, 1, 4, 5).reshape(4, 8 * A, 384)
+    in_b = seen[:, :, :, :, A:].transpose(2, 1, 3, 0, 4, 5).reshape(8, 4 * B, 384)
 
     sign_x = 1 - 2 * ((x + core) & 1)
     sign_y = 1 - 2 * ((y + core) & 1)
-    lines_b = place(line_of_4(part_b, "x"), x, 4, sign_x)
-    lines_a = place(line_of_8(part_a, "y"), y, 8, sign_y)
-    pairs_a = line_of_4(lines_a, "x")
-    pairs_b = line_of_8(lines_b, "y")
+    a1, b1 = exchange(part_a, "y", 8, 0), exchange(part_b, "x", 4, 0)
+    a01, b01 = jnp.stack([part_a, a1]), jnp.stack([part_b, b1])
+    a12, b12 = exchange(a01, "y", 8, 1), exchange(b01, "x", 4, 1)
+    line_b = place([((0, 1), b01), ((-1, -2), b12)], x, 4, sign_x).reshape(4 * B, 1536)
+    third = exchange(jnp.concatenate([a12.reshape(2 * A, 1536), line_b]), "y", 8, 0)
+    a23, near_b = third[: 2 * A], third[2 * A :]
+    fourth = exchange(jnp.concatenate([third, line_b]), "y", 8, 1)
+    a34, pair_b = fourth[: 2 * A], fourth[2 * A :]
+    far_b = exchange(pair_b, "y", 8, 0)
+    line_a = place(
+        [
+            ((0, 1), a01),
+            ((-1, -2), a12),
+            ((2, 3), a23.reshape(2, A, 1536)),
+            ((-3, -4), a34.reshape(2, A, 1536)),
+        ],
+        y,
+        8,
+        sign_y,
+    )
+    pair_a = jnp.stack([line_a, exchange(line_a, "x", 4, 0)])
+    pairs_a = [((0, 1), pair_a), ((-1, -2), exchange(pair_a, "x", 4, 1))]
+    pairs_b = [
+        ((0, 1), jnp.concatenate([line_b, near_b]).reshape(2, 4, B, 1536)),
+        ((-2, -1), pair_b.reshape(2, 4, B, 1536)),
+        ((3, 2), far_b.reshape(2, 4, B, 1536)),
+        ((-4, -3), exchange(far_b, "y", 8, 1).reshape(2, 4, B, 1536)),
+    ]
     shares_a, total = products(pairs_a, weight_t, in_a, x, 4, sign_x, 0.0)
     shares_b, total = products(pairs_b, weight_t, in_b, y, 8, sign_y, total)
     grad_weight = total.astype(BF)
 
-    share_a = place(shares_a, x, 4, sign_x).reshape(2, 2, 2, 4, PART, 384)
-    share_b = place(shares_b, y, 8, sign_y).reshape(2, 4, 2, 2, PART, 384).transpose(2, 3, 0, 1, 4, 5)
-    share = jnp.stack([share_a, share_b], axis=4)
+    share_a = place(shares_a, x, 4, sign_x).reshape(2, 2, 2, 4, A, 384)
+    share_b = place(shares_b, y, 8, sign_y).reshape(2, 4, 2, 2, B, 384).transpose(2, 3, 0, 1, 4, 5)
+    share = jnp.concatenate([share_a, share_b], axis=4)
     keep = lax.dynamic_index_in_dim(share, core, 2, False)
     give = lax.dynamic_index_in_dim(share, 1 - core, 2, False).astype(BF)
     both = keep + lax.ppermute(give, "core", [(0, 1), (1, 0)]).astype(F32)
-    sent = both.astype(BF).transpose(1, 2, 0, 3, 4, 5).reshape(8, 128, 384)
-    parts = lax.all_to_all(sent, "z", 0, 0)
-    grad_inputs = parts.astype(F32).sum(axis=0).astype(BF)
+    both = both.reshape(2, 8, 64, 384)
+    sign_z = 1 - 2 * ((z + core) & 1)
+
+    def own(*steps):
+        return jnp.stack(
+            [lax.dynamic_index_in_dim(both, (z + k * sign_z) & 7, 1, False) for k in steps]
+        )
+
+    sums = own(2, 3) + exchange(own(-3, -4).astype(BF), "z", 8, 1).astype(F32)
+    sums = own(-1, -2) + exchange(sums.astype(BF), "z", 8, 0).astype(F32)
+    sums = own(0, 1) + exchange(sums.astype(BF), "z", 8, 1).astype(F32)
+    sums = sums[0] + exchange(sums[1], "z", 8, 0)
+    grad_inputs = sums.reshape(128, 384).astype(BF)
     return (grad_inputs, grad_weight)
 
 

time: 197 us -> 198 us (level)
  starting transfers between devices: 92.4 us -> 98.5 us
  local copies, waits for them, and re-layouts: 12.4 us -> 9.29 us
    ppermute x12 -> x14, starting transfers between devices: 41.9 us -> 68.6 us  [exchange(): return lax.ppermute(block, ROW if axis == 'z' else ('core', axis), pairs)]
    all_to_all x1 -> x0, starting transfers between devices: 20 us -> none  [on_device(): parts = lax.all_to_all(sent, 'z', 0, 0)]
    ppermute x12 -> x14, waiting for transfers between devices: 28.3 us -> 45.9 us  [exchange(): return lax.ppermute(block, ROW if axis == 'z' else ('core', axis), pairs)]
    all_to_all x1 -> x0, waiting for transfers between devices: 17 us -> none  [on_device(): parts = lax.all_to_all(sent, 'z', 0, 0)]
    dynamic_update_slice x22, local copies, waits for them, and re-layouts: 5.88 us -> 3.26 us  [place(): whole = lax.dynamic_update_slice(whole, pair[i:i + 1], start)]
  transfers between devices with their start and end apart: 17 -> 18, of which waited for: 8 -> 11; matrix products, arithmetic and copies ran while one was open for 14% -> 14% of each run, Pallas kernels for 0% -> 0%
where the time goes in v4:
time: 198 us; the launch traced here: 195 us
  starting transfers between devices  98.5 us (50%)
  waiting for transfers between devices  48.1 us (24%)
  matrix products  18.5 us (9%)
  between operations  14.9 us (8%)
  local copies, waits for them, and re-layouts  9.29 us (5%)
  other arithmetic  6 us (3%)
    ppermute x14, starting transfers between devices, exchange(): return lax.ppermute(block, ROW if axis == 'z' else ('core', axis), pairs)  68.6 us
    ppermute x14, waiting for transfers between devices, exchange(): return lax.ppermute(block, ROW if axis == 'z' else ('core', axis), pairs)  45.9 us
    dot_general x12, matrix products, dot(): return lax.dot_general(a, b, (dims, ((), ())), preferred_element_type=F32)  18.5 us
    ppermute x1, starting transfers between devices, on_device(): other = lax.ppermute(other, ALL, to_slots(1))  12.9 us
    ppermute x1, starting transfers between devices, on_device(): same = lax.ppermute(same, ALL, to_slots(0))  8.84 us
    ppermute x1, starting transfers between devices, on_device(): both = keep + lax.ppermute(give, 'core', [(0, 1), (1, 0)]).astype(F32)  8.1 us
  transfers between devices with their start and end apart: 18, of which 11 were waited for; matrix products, arithmetic and copies ran while one was open for 14% of the time, Pallas kernels for 0%

profile of v4, /device:TPU:1, one launch (start us, length us, event | category | flops | bytes accessed | tf_op | source)
XLA Modules:
  0.0 195.2 jit_solution(2077767608742747866)
XLA Ops:
  8.7 8.8 %collective-permute-start = (bf16[64,768]{1,0:T(8,128)(2,1)S(1)}, bf16[64,768]{1,0:T(8,128)(2,1)S(1)}, u32[]{:S(2)}, u32[]{:S(2)}) collective-permute-start(bf16[64,768]{1,0:T(8,128)(2,1)S(1)} %get-tuple-element.40), channel_id=1, source_target_pairs={{0,0},{1,16},{2,32},{3,48},{4,64},{5,80},{6,96},{7,112},{8,128},{9... | collective-permute-start | bytes 294920 | tf_op jit(solution)/shard_map/ppermute | solution.py:83
  17.5 12.9 %collective-permute-start.1 = (bf16[64,768]{1,0:T(8,128)(2,1)S(1)}, bf16[64,768]{1,0:T(8,128)(2,1)S(1)}, u32[]{:S(2)}, u32[]{:S(2)}) collective-permute-start(bf16[64,768]{1,0:T(8,128)(2,1)S(1)} %get-tuple-element.41), channel_id=1, source_target_pairs={{0,16},{1,0},{2,48},{3,32},{4,80},{5,64},{6,112},{7,96},{8,144},{9... | collective-permute-start | bytes 294920 | tf_op jit(solution)/shard_map/ppermute | solution.py:84
  30.5 2.2 %collective-permute-done.1 = bf16[64,768]{1,0:T(8,128)(2,1)S(1)} collective-permute-done((bf16[64,768]{1,0:T(8,128)(2,1)S(1)}, bf16[64,768]{1,0:T(8,128)(2,1)S(1)}, u32[]{:S(2)}, u32[]{:S(2)}) %collective-permute-start.1) | collective-permute-done | bytes 98336 | tf_op jit(solution)/shard_map/ppermute | solution.py:84
  32.8 2.8 %collective-permute-start.2 = (bf16[24,1536]{1,0:T(8,128)(2,1)S(1)}, bf16[24,1536]{1,0:T(8,128)(2,1)S(1)}, u32[]{:S(2)}, u32[]{:S(2)}) collective-permute-start(bf16[24,1536]{1,0:T(8,128)(2,1)S(1)} %get-tuple-element.3), channel_id=1, source_target_pairs={{0,1},{1,0},{2,3},{3,2},{4,5},{5,4},{6,7},{7,6},{32,39},{33,34},{3... | collective-permute-start | bytes 221192 | tf_op jit(solution)/shard_map/ppermute | solution.py:45
  35.7 10.5 %collective-permute-start.4 = (bf16[40,1536]{1,0:T(8,128)(2,1)S(1)}, bf16[40,1536]{1,0:T(8,128)(2,1)S(1)}, u32[]{:S(2)}, u32[]{:S(2)}) collective-permute-start(bf16[40,1536]{1,0:T(8,128)(2,1)S(1)} %get-tuple-element.5), channel_id=1, source_target_pairs={{0,8},{8,0},{16,24},{24,16},{32,56},{40,48},{48,40},{56,32},{1,9},... | collective-permute-start | bytes 368648 | tf_op jit(solution)/shard_map/ppermute | solution.py:45
  46.2 2.3 %collective-permute-start.3 = (bf16[2,24,1536]{2,1,0:T(8,128)(2,1)S(1)}, bf16[2,24,1536]{2,1,0:T(8,128)(2,1)S(1)}, u32[]{:S(2)}, u32[]{:S(2)}) collective-permute-start(bf16[2,24,1536]{2,1,0:T(8,128)(2,1)S(1)} %pad_maximum_fusion.8), channel_id=1, source_target_pairs={{0,7},{1,2},{2,1},{3,4},{4,3},{5,6},{6,5},{7,0},{32,33},{33,32},{3... | collective-permute-start | bytes 442376 | tf_op jit(solution)/shard_map/ppermute | solution.py:45
  50.5 5.4 %collective-permute-done.5 = bf16[2,40,1536]{2,1,0:T(8,128)(2,1)S(1)} collective-permute-done((bf16[2,40,1536]{2,1,0:T(8,128)(2,1)S(1)}, bf16[2,40,1536]{2,1,0:T(8,128)(2,1)S(1)}, u32[]{:S(2)}, u32[]{:S(2)}) %collective-permute-start.5) | collective-permute-done | bytes 245792 | tf_op jit(solution)/shard_map/ppermute | solution.py:45
  56.0 4.5 %collective-permute-start.6 = (bf16[208,1536]{1,0:T(8,128)(2,1)S(1)}, bf16[208,1536]{1,0:T(8,128)(2,1)S(1)}, u32[]{:S(2)}, u32[]{:S(2)}) collective-permute-start(bf16[208,1536]{1,0:T(8,128)(2,1)S(1)} %pad_maximum_fusion.3), channel_id=1, source_target_pairs={{0,1},{1,0},{2,3},{3,2},{4,5},{5,4},{6,7},{7,6},{32,39},{33,34},{3... | collective-permute-start | bytes 1916936 | tf_op jit(solution)/shard_map/ppermute | solution.py:45
  60.5 7.9 %collective-permute-done.6 = bf16[208,1536]{1,0:T(8,128)(2,1)S(1)} collective-permute-done((bf16[208,1536]{1,0:T(8,128)(2,1)S(1)}, bf16[208,1536]{1,0:T(8,128)(2,1)S(1)}, u32[]{:S(2)}, u32[]{:S(2)}) %collective-permute-start.6) | collective-permute-done | bytes 639008 | tf_op jit(solution)/shard_map/ppermute | solution.py:45
  69.3 4.1 %collective-permute-start.7 = (bf16[368,1536]{1,0:T(8,128)(2,1)S(1)}, bf16[368,1536]{1,0:T(8,128)(2,1)S(1)}, u32[]{:S(2)}, u32[]{:S(2)}) collective-permute-start(bf16[368,1536]{1,0:T(8,128)(2,1)S(1)} %pad_maximum_fusion.1), channel_id=1, source_target_pairs={{0,7},{1,2},{2,1},{3,4},{4,3},{5,6},{6,5},{7,0},{32,33},{33,32},{3... | collective-permute-start | bytes 3391496 | tf_op jit(solution)/shard_map/ppermute | solution.py:45
  73.6 13.1 %collective-permute-done.7 = bf16[368,1536]{1,0:T(8,128)(2,1)S(1)} collective-permute-done((bf16[368,1536]{1,0:T(8,128)(2,1)S(1)}, bf16[368,1536]{1,0:T(8,128)(2,1)S(1)}, u32[]{:S(2)}, u32[]{:S(2)}) %collective-permute-start.7) | collective-permute-done | bytes 1130528 | tf_op jit(solution)/shard_map/ppermute | solution.py:45
  87.8 3.8 %collective-permute-start.10 = (bf16[320,1536]{1,0:T(8,128)(2,1)}, bf16[320,1536]{1,0:T(8,128)(2,1)}, u32[]{:S(2)}, u32[]{:S(2)}) collective-permute-start(bf16[320,1536]{1,0:T(8,128)(2,1)} %slice.197), channel_id=1, source_target_pairs={{0,1},{1,0},{2,3},{3,2},{4,5},{5,4},{6,7},{7,6},{32,39},{33,34},{3... | collective-permute-start | bytes 2949128 | tf_op jit(solution)/shard_map/ppermute | solution.py:45
  91.6 4.8 %collective-permute-start.8 = (bf16[8,24,1536]{2,1,0:T(8,128)(2,1)S(1)}, bf16[8,24,1536]{2,1,0:T(8,128)(2,1)S(1)}, u32[]{:S(2)}, u32[]{:S(2)}) collective-permute-start(bf16[8,24,1536]{2,1,0:T(8,128)(2,1)S(1)} %fusion.46), channel_id=1, source_target_pairs={{0,8},{8,0},{16,24},{24,16},{32,56},{40,48},{48,40},{56,32},{1,9},... | collective-permute-start | bytes 1769480 | tf_op jit(solution)/shard_map/ppermute | solution.py:45
  97.3 6.5 %collective-permute-done.8 = bf16[8,24,1536]{2,1,0:T(8,128)(2,1)S(1)} collective-permute-done((bf16[8,24,1536]{2,1,0:T(8,128)(2,1)S(1)}, bf16[8,24,1536]{2,1,0:T(8,128)(2,1)S(1)}, u32[]{:S(2)}, u32[]{:S(2)}) %collective-permute-start.8) | collective-permute-done | bytes 589856 | tf_op jit(solution)/shard_map/ppermute | solution.py:45
  113.2 2.7 %collective-permute-start.11 = (bf16[320,1536]{1,0:T(8,128)(2,1)}, bf16[320,1536]{1,0:T(8,128)(2,1)S(1)}, u32[]{:S(2)}, u32[]{:S(2)}) collective-permute-start(bf16[320,1536]{1,0:T(8,128)(2,1)} %collective-permute-done.10), channel_id=1, source_target_pairs={{0,7},{1,2},{2,1},{3,4},{4,3},{5,6},{6,5},{7,0},{32,33},{33,32},{3... | collective-permute-start | bytes 2949128 | tf_op jit(solution)/shard_map/ppermute | solution.py:45
  117.9 4.5 %collective-permute-done.9 = bf16[2,8,24,1536]{3,2,1,0:T(8,128)(2,1)} collective-permute-done((bf16[2,8,24,1536]{3,2,1,0:T(8,128)(2,1)}, bf16[2,8,24,1536]{3,2,1,0:T(8,128)(2,1)}, u32[]{:S(2)}, u32[]{:S(2)}) %collective-permute-start.9) | collective-permute-done | bytes 1179680 | tf_op jit(solution)/shard_map/ppermute | solution.py:45
  126.0 2.5 %collective-permute-done.11 = bf16[320,1536]{1,0:T(8,128)(2,1)S(1)} collective-permute-done((bf16[320,1536]{1,0:T(8,128)(2,1)}, bf16[320,1536]{1,0:T(8,128)(2,1)S(1)}, u32[]{:S(2)}, u32[]{:S(2)}) %collective-permute-start.11) | collective-permute-done | bytes 983072 | tf_op jit(solution)/shard_map/ppermute | solution.py:45
  130.5 8.1 %collective-permute-start.12 = (bf16[2,2,4,64,384]{4,3,1,0,2:T(8,128)(2,1)S(1)}, bf16[2,2,4,64,384]{4,3,1,0,2:T(8,128)(2,1)S(1)}, u32[]{:S(2)}, u32[]{:S(2)}) collective-permute-start(bf16[2,2,4,64,384]{4,3,1,0,2:T(8,128)(2,1)S(1)} %fusion.8), channel_id=1, source_target_pairs={{0,32},{32,0},{1,33},{33,1},{2,34},{34,2},{3,35},{35,3},{4,36},{36... | collective-permute-start | bytes 2359304 | tf_op jit(solution)/shard_map/ppermute | solution.py:134
  144.5 4.0 %collective-permute-start.13 = (bf16[2,2,64,384]{3,2,1,0:T(8,128)(2,1)S(1)}, bf16[2,2,64,384]{3,2,1,0:T(8,128)(2,1)S(1)}, u32[]{:S(2)}, u32[]{:S(2)}) collective-permute-start(bf16[2,2,64,384]{3,2,1,0:T(8,128)(2,1)S(1)} %pad_maximum_fusion.7), channel_id=1, source_target_pairs={{0,448},{64,128},{128,64},{192,256},{256,192},{320,384},{384,320},... | collective-permute-start | bytes 589832 | tf_op jit(solution)/shard_map/ppermute | solution.py:45
  148.5 2.2 %fusion.24 = f32[1536,384]{1,0:T(8,128)S(1)} fusion(bf16[384,1536]{1,0:T(8,128)(2,1)} %bitcast.15, bf16[192,384]{1,0:T(8,128)(2,1)S(1)} %get-tuple-element.23, bf16[192,384]{1,0:T(8,128)(2,1)S(1)} %get-tuple-element.24), kind=kOutput, calls=%fused_computation.47 | convolution fusion | flops 453574656 | bytes 3833856 | tf_op jit(solution)/shard_map/dot_general | solution.py:49
  151.6 18.9 %collective-permute-start.14 = (bf16[2,2,64,384]{3,2,1,0:T(8,128)(2,1)S(1)}, bf16[2,2,64,384]{3,2,1,0:T(8,128)(2,1)S(1)}, u32[]{:S(2)}, u32[]{:S(2)}) collective-permute-start(bf16[2,2,64,384]{3,2,1,0:T(8,128)(2,1)S(1)} %fusion.20), channel_id=1, source_target_pairs={{0,64},{64,0},{128,192},{192,128},{256,320},{320,256},{384,448},{4... | collective-permute-start | bytes 589832 | tf_op jit(solution)/shard_map/ppermute | solution.py:45
  170.5 2.3 %convolution_add_fusion.2 = f32[1536,384]{1,0:T(8,128)S(1)} fusion(f32[1536,384]{1,0:T(8,128)S(1)} %fusion.24, bf16[384,1536]{1,0:T(8,128)(2,1)} %bitcast.12, bf16[192,384]{1,0:T(8,128)(2,1)S(1)} %get-tuple-element.25, bf16[192,384]{1,0:T(8,128)(2,1)S(1)} %get-tuple-element.22), kind=kOutput, calls=%fused_computation.8 | convolution fusion | flops 454164480 | bytes 6193152 | tf_op jit(solution)/shard_map/dot_general | solution.py:49
  176.5 3.5 %collective-permute-done.15 = bf16[2,2,64,384]{3,2,1,0:T(8,128)(2,1)S(1)} collective-permute-done((bf16[2,2,64,384]{3,2,1,0:T(8,128)(2,1)S(1)}, bf16[2,2,64,384]{3,2,1,0:T(8,128)(2,1)S(1)}, u32[]{:S(2)}, u32[]{:S(2)}) %collective-permute-start.15) | collective-permute-done | bytes 196640 | tf_op jit(solution)/shard_map/ppermute | solution.py:45
  180.1 4.6 %collective-permute-start.16 = (f32[2,64,384]{2,1,0:T(8,128)S(1)}, f32[2,64,384]{2,1,0:T(8,128)S(1)}, u32[]{:S(2)}, u32[]{:S(2)}) collective-permute-start(f32[2,64,384]{2,1,0:T(8,128)S(1)} %slice_bitcast_fusion.2), channel_id=1, source_target_pairs={{0,64},{64,0},{128,192},{192,128},{256,320},{320,256},{384,448},{4... | collective-permute-start | bytes 589832 | tf_op jit(solution)/shard_map/ppermute | solution.py:45
  (102 shorter events, 37.6 us)
Async XLA Ops:
  7.2 61.2 %copy-start = (bf16[1536,384]{1,0:T(8,128)(2,1)S(1)}, bf16[1536,384]{1,0:T(8,128)(2,1)}, u32[]{:S(2)}) copy-start(bf16[1536,384]{1,0:T(8,128)(2,1)} %param.7) | copy-start | bytes 3538948
  7.2 104.3 %all-gather.3.cloned.1.call-start = ((), (), s32[]{:S(2)}) async-start(), calls=%async_computation | async-start | bytes 1671168 | tf_op jit(solution)/shard_map/all_gather | solution.py:90
  8.7 21.8 %collective-permute-start = (bf16[64,768]{1,0:T(8,128)(2,1)S(1)}, bf16[64,768]{1,0:T(8,128)(2,1)S(1)}, u32[]{:S(2)}, u32[]{:S(2)}) collective-permute-start(bf16[64,768]{1,0:T(8,128)(2,1)S(1)} %get-tuple-element.40), channel_id=1, source_target_pairs={{0,0},{1,16},{2,32},{3,48},{4,64},{5,80},{6,96},{7,112},{8,128},{9... | collective-permute-start | bytes 294920 | tf_op jit(solution)/shard_map/ppermute | solution.py:83
  17.5 15.2 %collective-permute-start.1 = (bf16[64,768]{1,0:T(8,128)(2,1)S(1)}, bf16[64,768]{1,0:T(8,128)(2,1)S(1)}, u32[]{:S(2)}, u32[]{:S(2)}) collective-permute-start(bf16[64,768]{1,0:T(8,128)(2,1)S(1)} %get-tuple-element.41), channel_id=1, source_target_pairs={{0,16},{1,0},{2,48},{3,32},{4,80},{5,64},{6,112},{7,96},{8,144},{9... | collective-permute-start | bytes 294920 | tf_op jit(solution)/shard_map/ppermute | solution.py:84
  32.8 13.4 %collective-permute-start.2 = (bf16[24,1536]{1,0:T(8,128)(2,1)S(1)}, bf16[24,1536]{1,0:T(8,128)(2,1)S(1)}, u32[]{:S(2)}, u32[]{:S(2)}) collective-permute-start(bf16[24,1536]{1,0:T(8,128)(2,1)S(1)} %get-tuple-element.3), channel_id=1, source_target_pairs={{0,1},{1,0},{2,3},{3,2},{4,5},{5,4},{6,7},{7,6},{32,39},{33,34},{3... | collective-permute-start | bytes 221192 | tf_op jit(solution)/shard_map/ppermute | solution.py:45
  35.7 12.8 %collective-permute-start.4 = (bf16[40,1536]{1,0:T(8,128)(2,1)S(1)}, bf16[40,1536]{1,0:T(8,128)(2,1)S(1)}, u32[]{:S(2)}, u32[]{:S(2)}) collective-permute-start(bf16[40,1536]{1,0:T(8,128)(2,1)S(1)} %get-tuple-element.5), channel_id=1, source_target_pairs={{0,8},{8,0},{16,24},{24,16},{32,56},{40,48},{48,40},{56,32},{1,9},... | collective-permute-start | bytes 368648 | tf_op jit(solution)/shard_map/ppermute | solution.py:45
  46.2 9.7 %collective-permute-start.3 = (bf16[2,24,1536]{2,1,0:T(8,128)(2,1)S(1)}, bf16[2,24,1536]{2,1,0:T(8,128)(2,1)S(1)}, u32[]{:S(2)}, u32[]{:S(2)}) collective-permute-start(bf16[2,24,1536]{2,1,0:T(8,128)(2,1)S(1)} %pad_maximum_fusion.8), channel_id=1, source_target_pairs={{0,7},{1,2},{2,1},{3,4},{4,3},{5,6},{6,5},{7,0},{32,33},{33,32},{3... | collective-permute-start | bytes 442376 | tf_op jit(solution)/shard_map/ppermute | solution.py:45
  48.5 7.3 %collective-permute-start.5 = (bf16[2,40,1536]{2,1,0:T(8,128)(2,1)S(1)}, bf16[2,40,1536]{2,1,0:T(8,128)(2,1)S(1)}, u32[]{:S(2)}, u32[]{:S(2)}) collective-permute-start(bf16[2,40,1536]{2,1,0:T(8,128)(2,1)S(1)} %pad_maximum_fusion.6), channel_id=1, source_target_pairs={{0,24},{8,16},{16,8},{24,0},{32,40},{40,32},{48,56},{56,48},{1,25}... | collective-permute-start | bytes 737288 | tf_op jit(solution)/shard_map/ppermute | solution.py:45
  55.9 13.3 %copy-start.1 = (bf16[4,40,1536]{2,1,0:T(8,128)(2,1)}, bf16[4,40,1536]{2,1,0:T(8,128)(2,1)S(1)}, u32[]{:S(2)}) copy-start(bf16[4,40,1536]{2,1,0:T(8,128)(2,1)S(1)} %slice_dynamic-update-slice_fusion) | copy-start | bytes 1474564
  56.0 12.4 %collective-permute-start.6 = (bf16[208,1536]{1,0:T(8,128)(2,1)S(1)}, bf16[208,1536]{1,0:T(8,128)(2,1)S(1)}, u32[]{:S(2)}, u32[]{:S(2)}) collective-permute-start(bf16[208,1536]{1,0:T(8,128)(2,1)S(1)} %pad_maximum_fusion.3), channel_id=1, source_target_pairs={{0,1},{1,0},{2,3},{3,2},{4,5},{5,4},{6,7},{7,6},{32,39},{33,34},{3... | collective-permute-start | bytes 1916936 | tf_op jit(solution)/shard_map/ppermute | solution.py:45
  69.3 17.4 %collective-permute-start.7 = (bf16[368,1536]{1,0:T(8,128)(2,1)S(1)}, bf16[368,1536]{1,0:T(8,128)(2,1)S(1)}, u32[]{:S(2)}, u32[]{:S(2)}) collective-permute-start(bf16[368,1536]{1,0:T(8,128)(2,1)S(1)} %pad_maximum_fusion.1), channel_id=1, source_target_pairs={{0,7},{1,2},{2,1},{3,4},{4,3},{5,6},{6,5},{7,0},{32,33},{33,32},{3... | collective-permute-start | bytes 3391496 | tf_op jit(solution)/shard_map/ppermute | solution.py:45
  86.7 10.4 %copy-start.3 = (bf16[368,1536]{1,0:T(8,128)(2,1)}, bf16[368,1536]{1,0:T(8,128)(2,1)S(1)}, u32[]{:S(2)}) copy-start(bf16[368,1536]{1,0:T(8,128)(2,1)S(1)} %collective-permute-done.7) | copy-start | bytes 3391492
  87.8 25.3 %collective-permute-start.10 = (bf16[320,1536]{1,0:T(8,128)(2,1)}, bf16[320,1536]{1,0:T(8,128)(2,1)}, u32[]{:S(2)}, u32[]{:S(2)}) collective-permute-start(bf16[320,1536]{1,0:T(8,128)(2,1)} %slice.197), channel_id=1, source_target_pairs={{0,1},{1,0},{2,3},{3,2},{4,5},{5,4},{6,7},{7,6},{32,39},{33,34},{3... | collective-permute-start | bytes 2949128 | tf_op jit(solution)/shard_map/ppermute | solution.py:45
  91.6 12.1 %collective-permute-start.8 = (bf16[8,24,1536]{2,1,0:T(8,128)(2,1)S(1)}, bf16[8,24,1536]{2,1,0:T(8,128)(2,1)S(1)}, u32[]{:S(2)}, u32[]{:S(2)}) collective-permute-start(bf16[8,24,1536]{2,1,0:T(8,128)(2,1)S(1)} %fusion.46), channel_id=1, source_target_pairs={{0,8},{8,0},{16,24},{24,16},{32,56},{40,48},{48,40},{56,32},{1,9},... | collective-permute-start | bytes 1769480 | tf_op jit(solution)/shard_map/ppermute | solution.py:45
  104.9 17.5 %collective-permute-start.9 = (bf16[2,8,24,1536]{3,2,1,0:T(8,128)(2,1)}, bf16[2,8,24,1536]{3,2,1,0:T(8,128)(2,1)}, u32[]{:S(2)}, u32[]{:S(2)}) collective-permute-start(bf16[2,8,24,1536]{3,2,1,0:T(8,128)(2,1)} %pad_maximum_fusion), channel_id=1, source_target_pairs={{0,24},{8,16},{16,8},{24,0},{32,40},{40,32},{48,56},{56,48},{1,25}... | collective-permute-start | bytes 3538952 | tf_op jit(solution)/shard_map/ppermute | solution.py:45
  111.5 1.6 copy-start.7
  113.2 15.3 %collective-permute-start.11 = (bf16[320,1536]{1,0:T(8,128)(2,1)}, bf16[320,1536]{1,0:T(8,128)(2,1)S(1)}, u32[]{:S(2)}, u32[]{:S(2)}) collective-permute-start(bf16[320,1536]{1,0:T(8,128)(2,1)} %collective-permute-done.10), channel_id=1, source_target_pairs={{0,7},{1,2},{2,1},{3,4},{4,3},{5,6},{6,5},{7,0},{32,33},{33,32},{3... | collective-permute-start | bytes 2949128 | tf_op jit(solution)/shard_map/ppermute | solution.py:45
  130.5 12.5 %collective-permute-start.12 = (bf16[2,2,4,64,384]{4,3,1,0,2:T(8,128)(2,1)S(1)}, bf16[2,2,4,64,384]{4,3,1,0,2:T(8,128)(2,1)S(1)}, u32[]{:S(2)}, u32[]{:S(2)}) collective-permute-start(bf16[2,2,4,64,384]{4,3,1,0,2:T(8,128)(2,1)S(1)} %fusion.8), channel_id=1, source_target_pairs={{0,32},{32,0},{1,33},{33,1},{2,34},{34,2},{3,35},{35,3},{4,36},{36... | collective-permute-start | bytes 2359304 | tf_op jit(solution)/shard_map/ppermute | solution.py:134
  144.5 7.0 %collective-permute-start.13 = (bf16[2,2,64,384]{3,2,1,0:T(8,128)(2,1)S(1)}, bf16[2,2,64,384]{3,2,1,0:T(8,128)(2,1)S(1)}, u32[]{:S(2)}, u32[]{:S(2)}) collective-permute-start(bf16[2,2,64,384]{3,2,1,0:T(8,128)(2,1)S(1)} %pad_maximum_fusion.7), channel_id=1, source_target_pairs={{0,448},{64,128},{128,64},{192,256},{256,192},{320,384},{384,320},... | collective-permute-start | bytes 589832 | tf_op jit(solution)/shard_map/ppermute | solution.py:45
  151.6 21.9 %collective-permute-start.14 = (bf16[2,2,64,384]{3,2,1,0:T(8,128)(2,1)S(1)}, bf16[2,2,64,384]{3,2,1,0:T(8,128)(2,1)S(1)}, u32[]{:S(2)}, u32[]{:S(2)}) collective-permute-start(bf16[2,2,64,384]{3,2,1,0:T(8,128)(2,1)S(1)} %fusion.20), channel_id=1, source_target_pairs={{0,64},{64,0},{128,192},{192,128},{256,320},{320,256},{384,448},{4... | collective-permute-start | bytes 589832 | tf_op jit(solution)/shard_map/ppermute | solution.py:45
  170.5 5.0 %copy-start.2 = (bf16[4,40,1536]{2,1,0:T(8,128)(2,1)S(1)}, bf16[4,40,1536]{2,1,0:T(8,128)(2,1)}, u32[]{:S(2)}) copy-start(bf16[4,40,1536]{2,1,0:T(8,128)(2,1)} %copy-done.1) | copy-start | bytes 1474564
  170.5 5.0 %copy-start.6 = (bf16[160,1536]{1,0:T(8,128)(2,1)S(1)}, bf16[160,1536]{1,0:T(8,128)(2,1)}, u32[]{:S(2)}) copy-start(bf16[160,1536]{1,0:T(8,128)(2,1)} %copy-done.5) | copy-start | bytes 1474564
  173.6 6.4 %collective-permute-start.15 = (bf16[2,2,64,384]{3,2,1,0:T(8,128)(2,1)S(1)}, bf16[2,2,64,384]{3,2,1,0:T(8,128)(2,1)S(1)}, u32[]{:S(2)}, u32[]{:S(2)}) collective-permute-start(bf16[2,2,64,384]{3,2,1,0:T(8,128)(2,1)S(1)} %fusion.19), channel_id=1, source_target_pairs={{0,448},{64,128},{128,64},{192,256},{256,192},{320,384},{384,320},... | collective-permute-start | bytes 589832 | tf_op jit(solution)/shard_map/ppermute | solution.py:45
  180.1 7.6 %collective-permute-start.16 = (f32[2,64,384]{2,1,0:T(8,128)S(1)}, f32[2,64,384]{2,1,0:T(8,128)S(1)}, u32[]{:S(2)}, u32[]{:S(2)}) collective-permute-start(f32[2,64,384]{2,1,0:T(8,128)S(1)} %slice_bitcast_fusion.2), channel_id=1, source_target_pairs={{0,64},{64,0},{128,192},{192,128},{256,320},{320,256},{384,448},{4... | collective-permute-start | bytes 589832 | tf_op jit(solution)/shard_map/ppermute | solution.py:45
  (2 other events, 2.0 us)
Sparse Core Ops, SparseCore 0:
  30.5 39.3 all-gather.2

commit v5 on v3

--- a/solution.py
+++ b/solution.py
@@ -7,7 +7,7 @@
 COL = ("x", "y")
 ALL = ROW + COL
 BF, F32 = jnp.bfloat16, jnp.float32
-PART = 32
+A, B = 40, 24
 
 
 def gelu_prime(value):
@@ -37,8 +37,12 @@
     for core in range(2):
         for i in range(size):
             step = 1 if (i + core + turn) % 2 == 0 else -1
-            pairs.append((core * size + i, core * size + (i + step) % size))
-    return lax.ppermute(block, ("core", axis), pairs)
+            j = (i + step) % size
+            if axis == "z":
+                pairs.append((i * 2 + core, j * 2 + core))
+            else:
+                pairs.append((core * size + i, core * size + j))
+    return lax.ppermute(block, ROW if axis == "z" else ("core", axis), pairs)
 
 
 def dot(a, b, dims):
@@ -94,12 +98,16 @@
     low = jnp.where(q == 0, same, other)
     high = jnp.where(q == 0, other, same)
     slot = jnp.concatenate([low, high], axis=1)
-    part_a, part_b = slot[:PART], slot[PART:]
+    part_a, part_b = slot[:A], slot[A:]
 
-    all_inputs = lax.all_gather(inputs, ROW, axis=0)
-    seen = all_inputs.reshape(2, 4, 2, 2, 2, PART, 384)
-    in_a = seen[:, :, :, :, 0].transpose(3, 0, 2, 1, 4, 5).reshape(4, 8 * PART, 384)
-    in_b = seen[:, :, :, :, 1].transpose(2, 1, 3, 0, 4, 5).reshape(8, 4 * PART, 384)
+    own_z = place(line_of_8(inputs, "z"), z, 8, 1 - 2 * ((z + core) & 1))
+    mate_z = lax.ppermute(own_z, "core", [(0, 1), (1, 0)])
+    all_inputs = jnp.stack(
+        [jnp.where(core == 0, own_z, mate_z), jnp.where(core == 0, mate_z, own_z)], axis=1
+    )
+    seen = all_inputs.reshape(2, 4, 2, 2, 64, 384)
+    in_a = seen[:, :, :, :, :A].transpose(3, 0, 2, 1, 4, 5).reshape(4, 8 * A, 384)
+    in_b = seen[:, :, :, :, A:].transpose(2, 1, 3, 0, 4, 5).reshape(8, 4 * B, 384)
 
     sign_x = 1 - 2 * ((x + core) & 1)
     sign_y = 1 - 2 * ((y + core) & 1)
@@ -111,13 +119,13 @@
     shares_b, total = products(pairs_b, weight_t, in_b, y, 8, sign_y, total)
     grad_weight = total.astype(BF)
 
-    share_a = place(shares_a, x, 4, sign_x).reshape(2, 2, 2, 4, PART, 384)
-    share_b = place(shares_b, y, 8, sign_y).reshape(2, 4, 2, 2, PART, 384).transpose(2, 3, 0, 1, 4, 5)
-    share = jnp.stack([share_a, share_b], axis=4)
+    share_a = place(shares_a, x, 4, sign_x).reshape(2, 2, 2, 4, A, 384)
+    share_b = place(shares_b, y, 8, sign_y).reshape(2, 4, 2, 2, B, 384).transpose(2, 3, 0, 1, 4, 5)
+    share = jnp.concatenate([share_a, share_b], axis=4)
     keep = lax.dynamic_index_in_dim(share, core, 2, False)
     give = lax.dynamic_index_in_dim(share, 1 - core, 2, False).astype(BF)
     both = keep + lax.ppermute(give, "core", [(0, 1), (1, 0)]).astype(F32)
-    sent = both.astype(BF).transpose(1, 2, 0, 3, 4, 5).reshape(8, 128, 384)
+    sent = both.astype(BF).transpose(1, 2, 0, 3, 4).reshape(8, 128, 384)
     parts = lax.all_to_all(sent, "z", 0, 0)
     grad_inputs = parts.astype(F32).sum(axis=0).astype(BF)
     return (grad_inputs, grad_weight)

time: 197 us -> 174 us (0.88)
  the two profiles are of different devices: /device:TPU:1 before, /device:TPU:5 now
where the time goes in v5:
time: 174 us; the launch traced here: 173 us
  starting transfers between devices  89.8 us (52%)
  waiting for transfers between devices  58.7 us (34%)
  matrix products  13.8 us (8%)
  local copies, waits for them, and re-layouts  5.16 us (3%)
  other arithmetic  4.22 us (2%)
    ppermute x16, starting transfers between devices, exchange(): return lax.ppermute(block, ROW if axis == 'z' else ('core', axis), pairs)  56.5 us
    ppermute x16, waiting for transfers between devices, exchange(): return lax.ppermute(block, ROW if axis == 'z' else ('core', axis), pairs)  36.8 us
    all_to_all x1, waiting for transfers between devices, on_device(): parts = lax.all_to_all(sent, 'z', 0, 0)  16.2 us
    dot_general x12, matrix products, dot(): return lax.dot_general(a, b, (dims, ((), ())), preferred_element_type=F32)  13.8 us
    ppermute x1, starting transfers between devices, on_device(): same = lax.ppermute(same, ALL, to_slots(0))  9.11 us
    ppermute x1, starting transfers between devices, on_device(): both = keep + lax.ppermute(give, 'core', [(0, 1), (1, 0)]).astype(F32)  8.22 us
    ppermute x1, starting transfers between devices, on_device(): mate_z = lax.ppermute(own_z, 'core', [(0, 1), (1, 0)])  7.8 us
    all_to_all x1, starting transfers between devices, on_device(): parts = lax.all_to_all(sent, 'z', 0, 0)  6.07 us
  transfers between devices with their start and end apart: 21, of which 8 were waited for; matrix products, arithmetic and copies ran while one was open for 10% of the time, Pallas kernels for 0%

profile of v5, /device:TPU:5, one launch (start us, length us, event | category | flops | bytes accessed | tf_op | source)
XLA Modules:
  0.0 173.3 jit_solution(14861179695009275897)
XLA Ops:
  0.7 10.8 %collective-permute-start.15 = (bf16[128,384]{1,0:T(8,128)(2,1)}, bf16[128,384]{1,0:T(8,128)(2,1)S(1)}, u32[]{:S(2)}, u32[]{:S(2)}) collective-permute-start(bf16[128,384]{1,0:T(8,128)(2,1)} %param.4), channel_id=1, source_target_pairs={{0,64},{64,0},{128,192},{192,128},{256,320},{320,256},{384,448},{4... | collective-permute-start | bytes 294920 | tf_op jit(solution)/shard_map/ppermute | solution.py:45
  12.8 9.1 %collective-permute-start = (bf16[64,768]{1,0:T(8,128)(2,1)S(1)}, bf16[64,768]{1,0:T(8,128)(2,1)S(1)}, u32[]{:S(2)}, u32[]{:S(2)}) collective-permute-start(bf16[64,768]{1,0:T(8,128)(2,1)S(1)} %get-tuple-element.34), channel_id=1, source_target_pairs={{0,0},{1,16},{2,32},{3,48},{4,64},{5,80},{6,96},{7,112},{8,128},{9... | collective-permute-start | bytes 294920 | tf_op jit(solution)/shard_map/ppermute | solution.py:96
  21.9 2.0 %collective-permute-start.1 = (bf16[64,768]{1,0:T(8,128)(2,1)S(1)}, bf16[64,768]{1,0:T(8,128)(2,1)S(1)}, u32[]{:S(2)}, u32[]{:S(2)}) collective-permute-start(bf16[64,768]{1,0:T(8,128)(2,1)S(1)} %get-tuple-element.35), channel_id=1, source_target_pairs={{0,16},{1,0},{2,48},{3,32},{4,80},{5,64},{6,112},{7,96},{8,144},{9... | collective-permute-start | bytes 294920 | tf_op jit(solution)/shard_map/ppermute | solution.py:97
  26.2 5.7 %collective-permute-done.1 = bf16[64,768]{1,0:T(8,128)(2,1)S(1)} collective-permute-done((bf16[64,768]{1,0:T(8,128)(2,1)S(1)}, bf16[64,768]{1,0:T(8,128)(2,1)S(1)}, u32[]{:S(2)}, u32[]{:S(2)}) %collective-permute-start.1) | collective-permute-done | bytes 98336 | tf_op jit(solution)/shard_map/ppermute | solution.py:97
  32.0 6.3 %collective-permute-start.2 = (bf16[40,1536]{1,0:T(8,128)(2,1)S(1)}, bf16[40,1536]{1,0:T(8,128)(2,1)S(1)}, u32[]{:S(2)}, u32[]{:S(2)}) collective-permute-start(bf16[40,1536]{1,0:T(8,128)(2,1)S(1)} %get-tuple-element.3), channel_id=1, source_target_pairs={{0,1},{1,0},{2,3},{3,2},{4,5},{5,4},{6,7},{7,6},{32,39},{33,34},{3... | collective-permute-start | bytes 368648 | tf_op jit(solution)/shard_map/ppermute | solution.py:45
  40.3 3.1 %collective-permute-done.8 = bf16[24,1536]{1,0:T(8,128)(2,1)S(1)} collective-permute-done((bf16[24,1536]{1,0:T(8,128)(2,1)S(1)}, bf16[24,1536]{1,0:T(8,128)(2,1)S(1)}, u32[]{:S(2)}, u32[]{:S(2)}) %collective-permute-start.8) | collective-permute-done | bytes 73760 | tf_op jit(solution)/shard_map/ppermute | solution.py:45
  43.5 3.6 %collective-permute-start.9 = (bf16[2,24,1536]{2,1,0:T(8,128)(2,1)S(1)}, bf16[2,24,1536]{2,1,0:T(8,128)(2,1)S(1)}, u32[]{:S(2)}, u32[]{:S(2)}) collective-permute-start(bf16[2,24,1536]{2,1,0:T(8,128)(2,1)S(1)} %pad_maximum_fusion.5), channel_id=1, source_target_pairs={{0,24},{8,16},{16,8},{24,0},{32,40},{40,32},{48,56},{56,48},{1,25}... | collective-permute-start | bytes 442376 | tf_op jit(solution)/shard_map/ppermute | solution.py:45
  47.2 5.2 %collective-permute-start.3 = (bf16[2,40,1536]{2,1,0:T(8,128)(2,1)S(1)}, bf16[2,40,1536]{2,1,0:T(8,128)(2,1)S(1)}, u32[]{:S(2)}, u32[]{:S(2)}) collective-permute-start(bf16[2,40,1536]{2,1,0:T(8,128)(2,1)S(1)} %pad_maximum_fusion.3), channel_id=1, source_target_pairs={{0,7},{1,2},{2,1},{3,4},{4,3},{5,6},{6,5},{7,0},{32,33},{33,32},{3... | collective-permute-start | bytes 737288 | tf_op jit(solution)/shard_map/ppermute | solution.py:45
  54.4 2.7 %collective-permute-start.10 = (bf16[4,24,1536]{2,1,0:T(8,128)(2,1)S(1)}, bf16[4,24,1536]{2,1,0:T(8,128)(2,1)S(1)}, u32[]{:S(2)}, u32[]{:S(2)}) collective-permute-start(bf16[4,24,1536]{2,1,0:T(8,128)(2,1)S(1)} %slice_dynamic-update-slice_fusion.12), channel_id=1, source_target_pairs={{0,1},{1,0},{2,3},{3,2},{4,5},{5,4},{6,7},{7,6},{32,39},{33,34},{3... | collective-permute-start | bytes 884744 | tf_op jit(solution)/shard_map/ppermute | solution.py:45
  57.2 3.7 %collective-permute-start.4 = (bf16[2,40,1536]{2,1,0:T(8,128)(2,1)S(1)}, bf16[2,40,1536]{2,1,0:T(8,128)(2,1)S(1)}, u32[]{:S(2)}, u32[]{:S(2)}) collective-permute-start(bf16[2,40,1536]{2,1,0:T(8,128)(2,1)S(1)} %collective-permute-done.3), channel_id=1, source_target_pairs={{0,1},{1,0},{2,3},{3,2},{4,5},{5,4},{6,7},{7,6},{32,39},{33,34},{3... | collective-permute-start | bytes 737288 | tf_op jit(solution)/shard_map/ppermute | solution.py:45
  61.0 2.5 %collective-permute-start.18 = (bf16[2,128,384]{2,1,0:T(8,128)(2,1)S(1)}, bf16[2,128,384]{2,1,0:T(8,128)(2,1)S(1)}, u32[]{:S(2)}, u32[]{:S(2)}) collective-permute-start(bf16[2,128,384]{2,1,0:T(8,128)(2,1)S(1)} %collective-permute-done.17), channel_id=1, source_target_pairs={{0,448},{64,128},{128,64},{192,256},{256,192},{320,384},{384,320},... | collective-permute-start | bytes 589832 | tf_op jit(solution)/shard_map/ppermute | solution.py:45
  63.7 2.6 %collective-permute-start.11 = (bf16[2,4,24,1536]{3,2,1,0:T(8,128)(2,1)S(1)}, bf16[2,4,24,1536]{3,2,1,0:T(8,128)(2,1)S(1)}, u32[]{:S(2)}, u32[]{:S(2)}) collective-permute-start(bf16[2,4,24,1536]{3,2,1,0:T(8,128)(2,1)S(1)} %pad_maximum_fusion.2), channel_id=1, source_target_pairs={{0,7},{1,2},{2,1},{3,4},{4,3},{5,6},{6,5},{7,0},{32,33},{33,32},{3... | collective-permute-start | bytes 1769480 | tf_op jit(solution)/shard_map/ppermute | solution.py:45
  67.5 7.8 %collective-permute-start.19 = (bf16[8,128,384]{2,1,0:T(8,128)(2,1)S(1)}, bf16[8,128,384]{2,1,0:T(8,128)(2,1)S(1)}, u32[]{:S(2)}, u32[]{:S(2)}) collective-permute-start(bf16[8,128,384]{2,1,0:T(8,128)(2,1)S(1)} %slice_dynamic-update-slice_fusion.6), channel_id=1, source_target_pairs={{0,32},{32,0},{1,33},{33,1},{2,34},{34,2},{3,35},{35,3},{4,36},{36... | collective-permute-start | bytes 2359304 | tf_op jit(solution)/shard_map/ppermute | solution.py:104
  77.3 5.3 %collective-permute-done.5 = bf16[2,40,1536]{2,1,0:T(8,128)(2,1)S(1)} collective-permute-done((bf16[2,40,1536]{2,1,0:T(8,128)(2,1)S(1)}, bf16[2,40,1536]{2,1,0:T(8,128)(2,1)S(1)}, u32[]{:S(2)}, u32[]{:S(2)}) %collective-permute-start.5) | collective-permute-done | bytes 245792 | tf_op jit(solution)/shard_map/ppermute | solution.py:45
  85.0 3.3 %collective-permute-start.12 = (bf16[2,4,24,1536]{3,2,1,0:T(8,128)(2,1)S(1)}, bf16[2,4,24,1536]{3,2,1,0:T(8,128)(2,1)S(1)}, u32[]{:S(2)}, u32[]{:S(2)}) collective-permute-start(bf16[2,4,24,1536]{3,2,1,0:T(8,128)(2,1)S(1)} %collective-permute-done.11), channel_id=1, source_target_pairs={{0,1},{1,0},{2,3},{3,2},{4,5},{5,4},{6,7},{7,6},{32,39},{33,34},{3... | collective-permute-start | bytes 1769480 | tf_op jit(solution)/shard_map/ppermute | solution.py:45
  88.8 8.1 %collective-permute-done.12 = bf16[2,4,24,1536]{3,2,1,0:T(8,128)(2,1)S(1)} collective-permute-done((bf16[2,4,24,1536]{3,2,1,0:T(8,128)(2,1)S(1)}, bf16[2,4,24,1536]{3,2,1,0:T(8,128)(2,1)S(1)}, u32[]{:S(2)}, u32[]{:S(2)}) %collective-permute-start.12) | collective-permute-done | bytes 589856 | tf_op jit(solution)/shard_map/ppermute | solution.py:45
  99.5 4.2 %collective-permute-start.7 = (bf16[2,8,40,1536]{3,2,1,0:T(8,128)(2,1)S(1)}, bf16[2,8,40,1536]{3,2,1,0:T(8,128)(2,1)S(1)}, u32[]{:S(2)}, u32[]{:S(2)}) collective-permute-start(bf16[2,8,40,1536]{3,2,1,0:T(8,128)(2,1)S(1)} %pad_maximum_fusion), channel_id=1, source_target_pairs={{0,24},{8,16},{16,8},{24,0},{32,40},{40,32},{48,56},{56,48},{1,25}... | collective-permute-start | bytes 5898248 | tf_op jit(solution)/shard_map/ppermute | solution.py:45
  105.3 2.5 %collective-permute-done.13 = bf16[2,4,24,1536]{3,2,1,0:T(8,128)(2,1)S(1)} collective-permute-done((bf16[2,4,24,1536]{3,2,1,0:T(8,128)(2,1)S(1)}, bf16[2,4,24,1536]{3,2,1,0:T(8,128)(2,1)S(1)}, u32[]{:S(2)}, u32[]{:S(2)}) %collective-permute-start.13) | collective-permute-done | bytes 589856 | tf_op jit(solution)/shard_map/ppermute | solution.py:45
  108.7 17.3 %collective-permute-done.7 = bf16[2,8,40,1536]{3,2,1,0:T(8,128)(2,1)S(1)} collective-permute-done((bf16[2,8,40,1536]{3,2,1,0:T(8,128)(2,1)S(1)}, bf16[2,8,40,1536]{3,2,1,0:T(8,128)(2,1)S(1)}, u32[]{:S(2)}, u32[]{:S(2)}) %collective-permute-start.7) | collective-permute-done | bytes 1966112 | tf_op jit(solution)/shard_map/ppermute | solution.py:45
  127.5 8.2 %collective-permute-start.14 = (bf16[2,2,4,64,384]{4,3,2,1,0:T(8,128)(2,1)S(1)}, bf16[2,2,4,64,384]{4,3,2,1,0:T(8,128)(2,1)S(1)}, u32[]{:S(2)}, u32[]{:S(2)}) collective-permute-start(bf16[2,2,4,64,384]{4,3,2,1,0:T(8,128)(2,1)S(1)} %fusion.12), channel_id=1, source_target_pairs={{0,32},{32,0},{1,33},{33,1},{2,34},{34,2},{3,35},{35,3},{4,36},{36... | collective-permute-start | bytes 2359304 | tf_op jit(solution)/shard_map/ppermute | solution.py:127
  138.3 2.0 %fusion.34 = f32[1536,384]{1,0:T(8,128)} fusion(bf16[192,1536]{1,0:T(8,128)(2,1)S(1)} %bitcast.120, bf16[96,384]{1,0:T(8,128)(2,1)S(1)} %get-tuple-element.20, bf16[96,384]{1,0:T(8,128)(2,1)S(1)} %get-tuple-element.21), kind=kOutput, calls=%fused_computation.65 | convolution fusion | flops 226787328 | bytes 3096576 | tf_op jit(solution)/shard_map/dot_general | solution.py:49
  141.5 6.1 %all-to-all-start = ((bf16[8,128,384]{2,1,0:T(8,128)(2,1)}), bf16[8,128,384]{2,1,0:T(8,128)(2,1)}, u32[]{:S(2)}, u32[]{:S(2)}) async-start(bf16[8,128,384]{2,1,0:T(8,128)(2,1)} %bitcast.117), calls=%async_computation | async-start | bytes 1572864 | tf_op jit(solution)/shard_map/all_to_all | solution.py:129
  147.6 3.1 %fusion.17 = f32[1536,384]{1,0:T(8,128)S(1)} fusion(bf16[640,1536]{1,0:T(8,128)(2,1)} %bitcast.147, bf16[320,384]{1,0:T(8,128)(2,1)} %get-tuple-element.9, bf16[320,384]{1,0:T(8,128)(2,1)} %get-tuple-element.10), kind=kOutput, calls=%fused_computation.39 | convolution fusion | flops 755957760 | bytes 4816896 | tf_op jit(solution)/shard_map/dot_general | solution.py:49
  155.1 16.2 %all-to-all-done = bf16[8,128,384]{2,1,0:T(8,128)(2,1)} async-done(((bf16[8,128,384]{2,1,0:T(8,128)(2,1)}), bf16[8,128,384]{2,1,0:T(8,128)(2,1)}, u32[]{:S(2)}, u32[]{:S(2)}) %all-to-all-start) | async-done | bytes 786464 | tf_op jit(solution)/shard_map/all_to_all | solution.py:129
  (125 shorter events, 30.1 us)
Async XLA Ops:
  0.6 65.6 %copy-start = (bf16[1536,384]{1,0:T(8,128)(2,1)S(1)}, bf16[1536,384]{1,0:T(8,128)(2,1)}, u32[]{:S(2)}) copy-start(bf16[1536,384]{1,0:T(8,128)(2,1)} %param.7) | copy-start | bytes 3538948
  0.6 23.4 %copy-start.10 = (bf16[128,384]{1,0:T(8,128)(2,1)S(1)}, bf16[128,384]{1,0:T(8,128)(2,1)}, u32[]{:S(2)}) copy-start(bf16[128,384]{1,0:T(8,128)(2,1)} %param.4) | copy-start | bytes 294916
  0.7 23.5 %collective-permute-start.15 = (bf16[128,384]{1,0:T(8,128)(2,1)}, bf16[128,384]{1,0:T(8,128)(2,1)S(1)}, u32[]{:S(2)}, u32[]{:S(2)}) collective-permute-start(bf16[128,384]{1,0:T(8,128)(2,1)} %param.4), channel_id=1, source_target_pairs={{0,64},{64,0},{128,192},{192,128},{256,320},{320,256},{384,448},{4... | collective-permute-start | bytes 294920 | tf_op jit(solution)/shard_map/ppermute | solution.py:45
  12.8 13.4 %collective-permute-start = (bf16[64,768]{1,0:T(8,128)(2,1)S(1)}, bf16[64,768]{1,0:T(8,128)(2,1)S(1)}, u32[]{:S(2)}, u32[]{:S(2)}) collective-permute-start(bf16[64,768]{1,0:T(8,128)(2,1)S(1)} %get-tuple-element.34), channel_id=1, source_target_pairs={{0,0},{1,16},{2,32},{3,48},{4,64},{5,80},{6,96},{7,112},{8,128},{9... | collective-permute-start | bytes 294920 | tf_op jit(solution)/shard_map/ppermute | solution.py:96
  21.9 9.9 %collective-permute-start.1 = (bf16[64,768]{1,0:T(8,128)(2,1)S(1)}, bf16[64,768]{1,0:T(8,128)(2,1)S(1)}, u32[]{:S(2)}, u32[]{:S(2)}) collective-permute-start(bf16[64,768]{1,0:T(8,128)(2,1)S(1)} %get-tuple-element.35), channel_id=1, source_target_pairs={{0,16},{1,0},{2,48},{3,32},{4,80},{5,64},{6,112},{7,96},{8,144},{9... | collective-permute-start | bytes 294920 | tf_op jit(solution)/shard_map/ppermute | solution.py:97
  24.2 28.1 %collective-permute-start.16 = (bf16[2,128,384]{2,1,0:T(8,128)(2,1)S(1)}, bf16[2,128,384]{2,1,0:T(8,128)(2,1)S(1)}, u32[]{:S(2)}, u32[]{:S(2)}) collective-permute-start(bf16[2,128,384]{2,1,0:T(8,128)(2,1)S(1)} %pad_maximum_fusion.4), channel_id=1, source_target_pairs={{0,448},{64,128},{128,64},{192,256},{256,192},{320,384},{384,320},... | collective-permute-start | bytes 589832 | tf_op jit(solution)/shard_map/ppermute | solution.py:45
  32.0 15.1 %collective-permute-start.2 = (bf16[40,1536]{1,0:T(8,128)(2,1)S(1)}, bf16[40,1536]{1,0:T(8,128)(2,1)S(1)}, u32[]{:S(2)}, u32[]{:S(2)}) collective-permute-start(bf16[40,1536]{1,0:T(8,128)(2,1)S(1)} %get-tuple-element.3), channel_id=1, source_target_pairs={{0,1},{1,0},{2,3},{3,2},{4,5},{5,4},{6,7},{7,6},{32,39},{33,34},{3... | collective-permute-start | bytes 368648 | tf_op jit(solution)/shard_map/ppermute | solution.py:45
  38.4 5.1 %collective-permute-start.8 = (bf16[24,1536]{1,0:T(8,128)(2,1)S(1)}, bf16[24,1536]{1,0:T(8,128)(2,1)S(1)}, u32[]{:S(2)}, u32[]{:S(2)}) collective-permute-start(bf16[24,1536]{1,0:T(8,128)(2,1)S(1)} %get-tuple-element.5), channel_id=1, source_target_pairs={{0,8},{8,0},{16,24},{24,16},{32,56},{40,48},{48,40},{56,32},{1,9},... | collective-permute-start | bytes 221192 | tf_op jit(solution)/shard_map/ppermute | solution.py:45
  43.5 10.9 %collective-permute-start.9 = (bf16[2,24,1536]{2,1,0:T(8,128)(2,1)S(1)}, bf16[2,24,1536]{2,1,0:T(8,128)(2,1)S(1)}, u32[]{:S(2)}, u32[]{:S(2)}) collective-permute-start(bf16[2,24,1536]{2,1,0:T(8,128)(2,1)S(1)} %pad_maximum_fusion.5), channel_id=1, source_target_pairs={{0,24},{8,16},{16,8},{24,0},{32,40},{40,32},{48,56},{56,48},{1,25}... | collective-permute-start | bytes 442376 | tf_op jit(solution)/shard_map/ppermute | solution.py:45
  47.2 10.0 %collective-permute-start.3 = (bf16[2,40,1536]{2,1,0:T(8,128)(2,1)S(1)}, bf16[2,40,1536]{2,1,0:T(8,128)(2,1)S(1)}, u32[]{:S(2)}, u32[]{:S(2)}) collective-permute-start(bf16[2,40,1536]{2,1,0:T(8,128)(2,1)S(1)} %pad_maximum_fusion.3), channel_id=1, source_target_pairs={{0,7},{1,2},{2,1},{3,4},{4,3},{5,6},{6,5},{7,0},{32,33},{33,32},{3... | collective-permute-start | bytes 737288 | tf_op jit(solution)/shard_map/ppermute | solution.py:45
  52.4 8.6 %collective-permute-start.17 = (bf16[2,128,384]{2,1,0:T(8,128)(2,1)S(1)}, bf16[2,128,384]{2,1,0:T(8,128)(2,1)S(1)}, u32[]{:S(2)}, u32[]{:S(2)}) collective-permute-start(bf16[2,128,384]{2,1,0:T(8,128)(2,1)S(1)} %collective-permute-done.16), channel_id=1, source_target_pairs={{0,64},{64,0},{128,192},{192,128},{256,320},{320,256},{384,448},{4... | collective-permute-start | bytes 589832 | tf_op jit(solution)/shard_map/ppermute | solution.py:45
  54.4 9.2 %collective-permute-start.10 = (bf16[4,24,1536]{2,1,0:T(8,128)(2,1)S(1)}, bf16[4,24,1536]{2,1,0:T(8,128)(2,1)S(1)}, u32[]{:S(2)}, u32[]{:S(2)}) collective-permute-start(bf16[4,24,1536]{2,1,0:T(8,128)(2,1)S(1)} %slice_dynamic-update-slice_fusion.12), channel_id=1, source_target_pairs={{0,1},{1,0},{2,3},{3,2},{4,5},{5,4},{6,7},{7,6},{32,39},{33,34},{3... | collective-permute-start | bytes 884744 | tf_op jit(solution)/shard_map/ppermute | solution.py:45
  57.2 18.1 %collective-permute-start.4 = (bf16[2,40,1536]{2,1,0:T(8,128)(2,1)S(1)}, bf16[2,40,1536]{2,1,0:T(8,128)(2,1)S(1)}, u32[]{:S(2)}, u32[]{:S(2)}) collective-permute-start(bf16[2,40,1536]{2,1,0:T(8,128)(2,1)S(1)} %collective-permute-done.3), channel_id=1, source_target_pairs={{0,1},{1,0},{2,3},{3,2},{4,5},{5,4},{6,7},{7,6},{32,39},{33,34},{3... | collective-permute-start | bytes 737288 | tf_op jit(solution)/shard_map/ppermute | solution.py:45
  61.0 6.4 %collective-permute-start.18 = (bf16[2,128,384]{2,1,0:T(8,128)(2,1)S(1)}, bf16[2,128,384]{2,1,0:T(8,128)(2,1)S(1)}, u32[]{:S(2)}, u32[]{:S(2)}) collective-permute-start(bf16[2,128,384]{2,1,0:T(8,128)(2,1)S(1)} %collective-permute-done.17), channel_id=1, source_target_pairs={{0,448},{64,128},{128,64},{192,256},{256,192},{320,384},{384,320},... | collective-permute-start | bytes 589832 | tf_op jit(solution)/shard_map/ppermute | solution.py:45
  63.7 20.8 %collective-permute-start.11 = (bf16[2,4,24,1536]{3,2,1,0:T(8,128)(2,1)S(1)}, bf16[2,4,24,1536]{3,2,1,0:T(8,128)(2,1)S(1)}, u32[]{:S(2)}, u32[]{:S(2)}) collective-permute-start(bf16[2,4,24,1536]{3,2,1,0:T(8,128)(2,1)S(1)} %pad_maximum_fusion.2), channel_id=1, source_target_pairs={{0,7},{1,2},{2,1},{3,4},{4,3},{5,6},{6,5},{7,0},{32,33},{33,32},{3... | collective-permute-start | bytes 1769480 | tf_op jit(solution)/shard_map/ppermute | solution.py:45
  67.5 20.9 %collective-permute-start.19 = (bf16[8,128,384]{2,1,0:T(8,128)(2,1)S(1)}, bf16[8,128,384]{2,1,0:T(8,128)(2,1)S(1)}, u32[]{:S(2)}, u32[]{:S(2)}) collective-permute-start(bf16[8,128,384]{2,1,0:T(8,128)(2,1)S(1)} %slice_dynamic-update-slice_fusion.6), channel_id=1, source_target_pairs={{0,32},{32,0},{1,33},{33,1},{2,34},{34,2},{3,35},{35,3},{4,36},{36... | collective-permute-start | bytes 2359304 | tf_op jit(solution)/shard_map/ppermute | solution.py:104
  75.3 7.2 %collective-permute-start.5 = (bf16[2,40,1536]{2,1,0:T(8,128)(2,1)S(1)}, bf16[2,40,1536]{2,1,0:T(8,128)(2,1)S(1)}, u32[]{:S(2)}, u32[]{:S(2)}) collective-permute-start(bf16[2,40,1536]{2,1,0:T(8,128)(2,1)S(1)} %collective-permute-done.4), channel_id=1, source_target_pairs={{0,7},{1,2},{2,1},{3,4},{4,3},{5,6},{6,5},{7,0},{32,33},{33,32},{3... | collective-permute-start | bytes 737288 | tf_op jit(solution)/shard_map/ppermute | solution.py:45
  82.6 16.7 %collective-permute-start.6 = (bf16[8,40,1536]{2,1,0:T(8,128)(2,1)S(1)}, bf16[8,40,1536]{2,1,0:T(8,128)(2,1)S(1)}, u32[]{:S(2)}, u32[]{:S(2)}) collective-permute-start(bf16[8,40,1536]{2,1,0:T(8,128)(2,1)S(1)} %slice_dynamic-update-slice_fusion), channel_id=1, source_target_pairs={{0,8},{8,0},{16,24},{24,16},{32,56},{40,48},{48,40},{56,32},{1,9},... | collective-permute-start | bytes 2949128 | tf_op jit(solution)/shard_map/ppermute | solution.py:45
  85.0 11.8 %collective-permute-start.12 = (bf16[2,4,24,1536]{3,2,1,0:T(8,128)(2,1)S(1)}, bf16[2,4,24,1536]{3,2,1,0:T(8,128)(2,1)S(1)}, u32[]{:S(2)}, u32[]{:S(2)}) collective-permute-start(bf16[2,4,24,1536]{3,2,1,0:T(8,128)(2,1)S(1)} %collective-permute-done.11), channel_id=1, source_target_pairs={{0,1},{1,0},{2,3},{3,2},{4,5},{5,4},{6,7},{7,6},{32,39},{33,34},{3... | collective-permute-start | bytes 1769480 | tf_op jit(solution)/shard_map/ppermute | solution.py:45
  96.9 10.9 %collective-permute-start.13 = (bf16[2,4,24,1536]{3,2,1,0:T(8,128)(2,1)S(1)}, bf16[2,4,24,1536]{3,2,1,0:T(8,128)(2,1)S(1)}, u32[]{:S(2)}, u32[]{:S(2)}) collective-permute-start(bf16[2,4,24,1536]{3,2,1,0:T(8,128)(2,1)S(1)} %collective-permute-done.12), channel_id=1, source_target_pairs={{0,7},{1,2},{2,1},{3,4},{4,3},{5,6},{6,5},{7,0},{32,33},{33,32},{3... | collective-permute-start | bytes 1769480 | tf_op jit(solution)/shard_map/ppermute | solution.py:45
  99.5 5.5 %copy-start.2 = (bf16[2,8,40,1536]{3,2,1,0:T(8,128)(2,1)}, bf16[2,8,40,1536]{3,2,1,0:T(8,128)(2,1)S(1)}, u32[]{:S(2)}) copy-start(bf16[2,8,40,1536]{3,2,1,0:T(8,128)(2,1)S(1)} %pad_maximum_fusion) | copy-start | bytes 5898244
  99.5 26.6 %collective-permute-start.7 = (bf16[2,8,40,1536]{3,2,1,0:T(8,128)(2,1)S(1)}, bf16[2,8,40,1536]{3,2,1,0:T(8,128)(2,1)S(1)}, u32[]{:S(2)}, u32[]{:S(2)}) collective-permute-start(bf16[2,8,40,1536]{3,2,1,0:T(8,128)(2,1)S(1)} %pad_maximum_fusion), channel_id=1, source_target_pairs={{0,24},{8,16},{16,8},{24,0},{32,40},{40,32},{48,56},{56,48},{1,25}... | collective-permute-start | bytes 5898248 | tf_op jit(solution)/shard_map/ppermute | solution.py:45
  127.5 12.8 %collective-permute-start.14 = (bf16[2,2,4,64,384]{4,3,2,1,0:T(8,128)(2,1)S(1)}, bf16[2,2,4,64,384]{4,3,2,1,0:T(8,128)(2,1)S(1)}, u32[]{:S(2)}, u32[]{:S(2)}) collective-permute-start(bf16[2,2,4,64,384]{4,3,2,1,0:T(8,128)(2,1)S(1)} %fusion.12), channel_id=1, source_target_pairs={{0,32},{32,0},{1,33},{33,1},{2,34},{34,2},{3,35},{35,3},{4,36},{36... | collective-permute-start | bytes 2359304 | tf_op jit(solution)/shard_map/ppermute | solution.py:127
  141.5 29.8 %all-to-all-start = ((bf16[8,128,384]{2,1,0:T(8,128)(2,1)}), bf16[8,128,384]{2,1,0:T(8,128)(2,1)}, u32[]{:S(2)}, u32[]{:S(2)}) async-start(bf16[8,128,384]{2,1,0:T(8,128)(2,1)} %bitcast.117), calls=%async_computation | async-start | bytes 1572864 | tf_op jit(solution)/shard_map/all_to_all | solution.py:129
  (13 other events, 25.4 us)

commit v6 on v5

--- a/solution.py
+++ b/solution.py
@@ -100,7 +100,28 @@
     slot = jnp.concatenate([low, high], axis=1)
     part_a, part_b = slot[:A], slot[A:]
 
-    own_z = place(line_of_8(inputs, "z"), z, 8, 1 - 2 * ((z + core) & 1))
+    in_1 = jnp.stack([inputs, exchange(inputs, "z", 8, 0)])
+    in_2 = exchange(in_1, "z", 8, 1)
+
+    sign_x = 1 - 2 * ((x + core) & 1)
+    sign_y = 1 - 2 * ((y + core) & 1)
+    lines_b = place(line_of_4(part_b, "x"), x, 4, sign_x)
+    lines_a = place(line_of_8(part_a, "y"), y, 8, sign_y)
+    near = exchange(lines_a, "x", 4, 0)
+    back = exchange(lines_a, "x", 4, 1)
+    far = exchange(near, "x", 4, 1)
+    pairs_a = [((0,), lines_a[None]), ((1,), near[None]), ((-1,), back[None]), ((-2,), far[None])]
+    pairs_b = line_of_8(lines_b, "y")
+    in_2, held = lax.optimization_barrier((in_2, pairs_b[2][1]))
+    pairs_b[2] = (pairs_b[2][0], held)
+    in_3 = exchange(in_2, "z", 8, 0)
+    in_4 = exchange(in_3, "z", 8, 1)
+    own_z = place(
+        [((0, 1), in_1), ((-1, -2), in_2), ((2, 3), in_3), ((-3, -4), in_4)],
+        z,
+        8,
+        1 - 2 * ((z + core) & 1),
+    )
     mate_z = lax.ppermute(own_z, "core", [(0, 1), (1, 0)])
     all_inputs = jnp.stack(
         [jnp.where(core == 0, own_z, mate_z), jnp.where(core == 0, mate_z, own_z)], axis=1
@@ -109,12 +130,6 @@
     in_a = seen[:, :, :, :, :A].transpose(3, 0, 2, 1, 4, 5).reshape(4, 8 * A, 384)
     in_b = seen[:, :, :, :, A:].transpose(2, 1, 3, 0, 4, 5).reshape(8, 4 * B, 384)
 
-    sign_x = 1 - 2 * ((x + core) & 1)
-    sign_y = 1 - 2 * ((y + core) & 1)
-    lines_b = place(line_of_4(part_b, "x"), x, 4, sign_x)
-    lines_a = place(line_of_8(part_a, "y"), y, 8, sign_y)
-    pairs_a = line_of_4(lines_a, "x")
-    pairs_b = line_of_8(lines_b, "y")
     shares_a, total = products(pairs_a, weight_t, in_a, x, 4, sign_x, 0.0)
     shares_b, total = products(pairs_b, weight_t, in_b, y, 8, sign_y, total)
     grad_weight = total.astype(BF)

time: 174 us -> 168 us (0.966)
  the two profiles are of different devices: /device:TPU:5 before, /device:TPU:1 now
where the time goes in v6:
time: 168 us; the launch traced here: 167 us
  starting transfers between devices  98.6 us (59%)
  waiting for transfers between devices  38.4 us (23%)
  matrix products  21 us (12%)
  other arithmetic  4.14 us (2%)
  local copies, waits for them, and re-layouts  3.7 us (2%)
    ppermute x17, starting transfers between devices, exchange(): return lax.ppermute(block, ROW if axis == 'z' else ('core', axis), pairs)  56.7 us
    ppermute x17, waiting for transfers between devices, exchange(): return lax.ppermute(block, ROW if axis == 'z' else ('core', axis), pairs)  26 us
    dot_general x16, matrix products, dot(): return lax.dot_general(a, b, (dims, ((), ())), preferred_element_type=F32)  21 us
    ppermute x1, starting transfers between devices, on_device(): mate_z = lax.ppermute(own_z, 'core', [(0, 1), (1, 0)])  13.9 us
    ppermute x1, starting transfers between devices, on_device(): other = lax.ppermute(other, ALL, to_slots(1))  12.9 us
    all_to_all x1, waiting for transfers between devices, on_device(): parts = lax.all_to_all(sent, 'z', 0, 0)  12.4 us
    ppermute x1, starting transfers between devices, on_device(): same = lax.ppermute(same, ALL, to_slots(0))  8.84 us
    all_to_all x1, starting transfers between devices, on_device(): parts = lax.all_to_all(sent, 'z', 0, 0)  4.39 us
  transfers between devices with their start and end apart: 22, of which 8 were waited for; matrix products, arithmetic and copies ran while one was open for 14% of the time, Pallas kernels for 0%

profile of v6, /device:TPU:1, one launch (start us, length us, event | category | flops | bytes accessed | tf_op | source)
XLA Modules:
  0.0 167.4 jit_solution(17300318290698875184)
XLA Ops:
  2.1 8.8 %collective-permute-start = (bf16[64,768]{1,0:T(8,128)(2,1)S(1)}, bf16[64,768]{1,0:T(8,128)(2,1)S(1)}, u32[]{:S(2)}, u32[]{:S(2)}) collective-permute-start(bf16[64,768]{1,0:T(8,128)(2,1)S(1)} %get-tuple-element.30), channel_id=1, source_target_pairs={{0,0},{1,16},{2,32},{3,48},{4,64},{5,80},{6,96},{7,112},{8,128},{9... | collective-permute-start | bytes 294920 | tf_op jit(solution)/shard_map/ppermute | solution.py:96
  11.0 12.9 %collective-permute-start.1 = (bf16[64,768]{1,0:T(8,128)(2,1)S(1)}, bf16[64,768]{1,0:T(8,128)(2,1)S(1)}, u32[]{:S(2)}, u32[]{:S(2)}) collective-permute-start(bf16[64,768]{1,0:T(8,128)(2,1)S(1)} %get-tuple-element.31), channel_id=1, source_target_pairs={{0,16},{1,0},{2,48},{3,32},{4,80},{5,64},{6,112},{7,96},{8,144},{9... | collective-permute-start | bytes 294920 | tf_op jit(solution)/shard_map/ppermute | solution.py:97
  26.1 11.5 %collective-permute-start.9 = (bf16[24,1536]{1,0:T(8,128)(2,1)S(1)}, bf16[24,1536]{1,0:T(8,128)(2,1)S(1)}, u32[]{:S(2)}, u32[]{:S(2)}) collective-permute-start(bf16[24,1536]{1,0:T(8,128)(2,1)S(1)} %get-tuple-element.9), channel_id=1, source_target_pairs={{0,8},{8,0},{16,24},{24,16},{32,56},{40,48},{48,40},{56,32},{1,9},... | collective-permute-start | bytes 221192 | tf_op jit(solution)/shard_map/ppermute | solution.py:45
  37.6 2.7 %collective-permute-start.14 = (bf16[2,128,384]{2,1,0:T(8,128)(2,1)S(1)}, bf16[2,128,384]{2,1,0:T(8,128)(2,1)S(1)}, u32[]{:S(2)}, u32[]{:S(2)}) collective-permute-start(bf16[2,128,384]{2,1,0:T(8,128)(2,1)S(1)} %pad_maximum_fusion.3), channel_id=1, source_target_pairs={{0,448},{64,128},{128,64},{192,256},{256,192},{320,384},{384,320},... | collective-permute-start | bytes 589832 | tf_op jit(solution)/shard_map/ppermute | solution.py:45
  44.4 2.9 %collective-permute-done.2 = bf16[40,1536]{1,0:T(8,128)(2,1)S(1)} collective-permute-done((bf16[40,1536]{1,0:T(8,128)(2,1)S(1)}, bf16[40,1536]{1,0:T(8,128)(2,1)S(1)}, u32[]{:S(2)}, u32[]{:S(2)}) %collective-permute-start.2) | collective-permute-done | bytes 122912 | tf_op jit(solution)/shard_map/ppermute | solution.py:45
  47.3 4.2 %collective-permute-start.3 = (bf16[2,40,1536]{2,1,0:T(8,128)(2,1)S(1)}, bf16[2,40,1536]{2,1,0:T(8,128)(2,1)S(1)}, u32[]{:S(2)}, u32[]{:S(2)}) collective-permute-start(bf16[2,40,1536]{2,1,0:T(8,128)(2,1)S(1)} %pad_maximum_fusion.2), channel_id=1, source_target_pairs={{0,7},{1,2},{2,1},{3,4},{4,3},{5,6},{6,5},{7,0},{32,33},{33,32},{3... | collective-permute-start | bytes 737288 | tf_op jit(solution)/shard_map/ppermute | solution.py:45
  51.6 2.7 %collective-permute-start.11 = (bf16[4,24,1536]{2,1,0:T(8,128)(2,1)S(1)}, bf16[4,24,1536]{2,1,0:T(8,128)(2,1)S(1)}, u32[]{:S(2)}, u32[]{:S(2)}) collective-permute-start(bf16[4,24,1536]{2,1,0:T(8,128)(2,1)S(1)} %slice_dynamic-update-slice_fusion.12), channel_id=1, source_target_pairs={{0,1},{1,0},{2,3},{3,2},{4,5},{5,4},{6,7},{7,6},{32,39},{33,34},{3... | collective-permute-start | bytes 884744 | tf_op jit(solution)/shard_map/ppermute | solution.py:45
  55.4 2.7 %collective-permute-start.4 = (bf16[2,40,1536]{2,1,0:T(8,128)(2,1)S(1)}, bf16[2,40,1536]{2,1,0:T(8,128)(2,1)S(1)}, u32[]{:S(2)}, u32[]{:S(2)}) collective-permute-start(bf16[2,40,1536]{2,1,0:T(8,128)(2,1)S(1)} %collective-permute-done.3), channel_id=1, source_target_pairs={{0,1},{1,0},{2,3},{3,2},{4,5},{5,4},{6,7},{7,6},{32,39},{33,34},{3... | collective-permute-start | bytes 737288 | tf_op jit(solution)/shard_map/ppermute | solution.py:45
  63.5 2.8 %collective-permute-start.5 = (bf16[2,40,1536]{2,1,0:T(8,128)(2,1)S(1)}, bf16[2,40,1536]{2,1,0:T(8,128)(2,1)S(1)}, u32[]{:S(2)}, u32[]{:S(2)}) collective-permute-start(bf16[2,40,1536]{2,1,0:T(8,128)(2,1)S(1)} %collective-permute-done.4), channel_id=1, source_target_pairs={{0,7},{1,2},{2,1},{3,4},{4,3},{5,6},{6,5},{7,0},{32,33},{33,32},{3... | collective-permute-start | bytes 737288 | tf_op jit(solution)/shard_map/ppermute | solution.py:45
  66.4 7.5 %collective-permute-done.5 = bf16[2,40,1536]{2,1,0:T(8,128)(2,1)S(1)} collective-permute-done((bf16[2,40,1536]{2,1,0:T(8,128)(2,1)S(1)}, bf16[2,40,1536]{2,1,0:T(8,128)(2,1)S(1)}, u32[]{:S(2)}, u32[]{:S(2)}) %collective-permute-start.5) | collective-permute-done | bytes 245792 | tf_op jit(solution)/shard_map/ppermute | solution.py:45
  74.0 2.4 %collective-permute-start.6 = (bf16[8,40,1536]{2,1,0:T(8,128)(2,1)S(1)}, bf16[8,40,1536]{2,1,0:T(8,128)(2,1)S(1)}, u32[]{:S(2)}, u32[]{:S(2)}) collective-permute-start(bf16[8,40,1536]{2,1,0:T(8,128)(2,1)S(1)} %slice_dynamic-update-slice_fusion), channel_id=1, source_target_pairs={{0,8},{8,0},{16,24},{24,16},{32,56},{40,48},{48,40},{56,32},{1,9},... | collective-permute-start | bytes 2949128 | tf_op jit(solution)/shard_map/ppermute | solution.py:45
  76.3 2.9 %collective-permute-start.7 = (bf16[8,40,1536]{2,1,0:T(8,128)(2,1)S(1)}, bf16[8,40,1536]{2,1,0:T(8,128)(2,1)S(1)}, u32[]{:S(2)}, u32[]{:S(2)}) collective-permute-start(bf16[8,40,1536]{2,1,0:T(8,128)(2,1)S(1)} %slice_dynamic-update-slice_fusion), channel_id=1, source_target_pairs={{0,24},{8,16},{16,8},{24,0},{32,40},{40,32},{48,56},{56,48},{1,25}... | collective-permute-start | bytes 2949128 | tf_op jit(solution)/shard_map/ppermute | solution.py:45
  80.1 6.2 %collective-permute-start.15 = (bf16[2,4,24,1536]{3,2,1,0:T(8,128)(2,1)S(1)}, bf16[2,4,24,1536]{3,2,1,0:T(8,128)(2,1)S(1)}, u32[]{:S(2)}, u32[]{:S(2)}) collective-permute-start(bf16[2,4,24,1536]{3,2,1,0:T(8,128)(2,1)S(1)} %collective-permute-done.12), channel_id=1, source_target_pairs={{0,1},{1,0},{2,3},{3,2},{4,5},{5,4},{6,7},{7,6},{32,39},{33,34},{3... | collective-permute-start | bytes 1769480 | tf_op jit(solution)/shard_map/ppermute | solution.py:45
  86.9 7.0 %collective-permute-done.15 = bf16[2,4,24,1536]{3,2,1,0:T(8,128)(2,1)S(1)} collective-permute-done((bf16[2,4,24,1536]{3,2,1,0:T(8,128)(2,1)S(1)}, bf16[2,4,24,1536]{3,2,1,0:T(8,128)(2,1)S(1)}, u32[]{:S(2)}, u32[]{:S(2)}) %collective-permute-start.15) | collective-permute-done | bytes 589856 | tf_op jit(solution)/shard_map/ppermute | solution.py:45
  93.9 3.6 %collective-permute-start.18 = (bf16[2,128,384]{2,1,0:T(8,128)(2,1)S(1)}, bf16[2,128,384]{2,1,0:T(8,128)(2,1)S(1)}, u32[]{:S(2)}, u32[]{:S(2)}) collective-permute-start(bf16[2,128,384]{2,1,0:T(8,128)(2,1)S(1)} %collective-permute-done.14), channel_id=1, source_target_pairs={{0,64},{64,0},{128,192},{192,128},{256,320},{320,256},{384,448},{4... | collective-permute-start | bytes 589832 | tf_op jit(solution)/shard_map/ppermute | solution.py:45
  98.0 2.6 %collective-permute-start.16 = (bf16[2,4,24,1536]{3,2,1,0:T(8,128)(2,1)S(1)}, bf16[2,4,24,1536]{3,2,1,0:T(8,128)(2,1)S(1)}, u32[]{:S(2)}, u32[]{:S(2)}) collective-permute-start(bf16[2,4,24,1536]{3,2,1,0:T(8,128)(2,1)S(1)} %collective-permute-done.15), channel_id=1, source_target_pairs={{0,7},{1,2},{2,1},{3,4},{4,3},{5,6},{6,5},{7,0},{32,33},{33,32},{3... | collective-permute-start | bytes 1769480 | tf_op jit(solution)/shard_map/ppermute | solution.py:45
  100.8 2.7 %collective-permute-start.8 = (bf16[8,40,1536]{2,1,0:T(8,128)(2,1)S(1)}, bf16[8,40,1536]{2,1,0:T(8,128)(2,1)S(1)}, u32[]{:S(2)}, u32[]{:S(2)}) collective-permute-start(bf16[8,40,1536]{2,1,0:T(8,128)(2,1)S(1)} %collective-permute-done.6), channel_id=1, source_target_pairs={{0,24},{8,16},{16,8},{24,0},{32,40},{40,32},{48,56},{56,48},{1,25}... | collective-permute-start | bytes 2949128 | tf_op jit(solution)/shard_map/ppermute | solution.py:45
  106.9 4.7 %collective-permute-done.19 = bf16[2,128,384]{2,1,0:T(8,128)(2,1)S(1)} collective-permute-done((bf16[2,128,384]{2,1,0:T(8,128)(2,1)S(1)}, bf16[2,128,384]{2,1,0:T(8,128)(2,1)S(1)}, u32[]{:S(2)}, u32[]{:S(2)}) %collective-permute-start.19) | collective-permute-done | bytes 196640 | tf_op jit(solution)/shard_map/ppermute | solution.py:45
  111.7 13.9 %collective-permute-start.20 = (bf16[8,128,384]{2,1,0:T(8,128)(2,1)S(1)}, bf16[8,128,384]{2,1,0:T(8,128)(2,1)S(1)}, u32[]{:S(2)}, u32[]{:S(2)}) collective-permute-start(bf16[8,128,384]{2,1,0:T(8,128)(2,1)S(1)} %slice_dynamic-update-slice_fusion.6), channel_id=1, source_target_pairs={{0,32},{32,0},{1,33},{33,1},{2,34},{34,2},{3,35},{35,3},{4,36},{36... | collective-permute-start | bytes 2359304 | tf_op jit(solution)/shard_map/ppermute | solution.py:125
  133.7 2.4 %fusion.36 = f32[1536,384]{1,0:T(8,128)} fusion(bf16[320,1536]{1,0:T(8,128)(2,1)S(1)} %bitcast.142, bf16[4,320,384]{2,1,0:T(8,128)(2,1)S(1)} %bitcast.144, s32[]{:T(128)S(6)} %select_n.150), kind=kOutput, calls=%fused_computation.62 | convolution fusion | flops 377487360 | bytes 3588100 | tf_op jit(solution)/shard_map/dot_general | solution.py:49
  136.1 2.4 %fusion.34 = f32[1536,384]{1,0:T(8,128)} fusion(bf16[320,1536]{1,0:T(8,128)(2,1)S(1)} %bitcast.143, bf16[4,320,384]{2,1,0:T(8,128)(2,1)S(1)} %bitcast.145, s32[]{:T(128)S(6)} %select_n.151), kind=kOutput, calls=%fused_computation.60 | convolution fusion | flops 377487360 | bytes 3588100 | tf_op jit(solution)/shard_map/dot_general | solution.py:49
  139.6 4.4 %all-to-all-start = ((bf16[8,128,384]{2,1,0:T(8,128)(2,1)}), bf16[8,128,384]{2,1,0:T(8,128)(2,1)}, u32[]{:S(2)}, u32[]{:S(2)}) async-start(bf16[8,128,384]{2,1,0:T(8,128)(2,1)} %bitcast.148), calls=%async_computation | async-start | bytes 1572864 | tf_op jit(solution)/shard_map/all_to_all | solution.py:144
  145.9 3.3 %fusion.2 = f32[1536,384]{1,0:T(8,128)S(1)} fusion(f32[1536,384]{1,0:T(8,128)} %fusion.34, f32[1536,384]{1,0:T(8,128)S(1)} %copy-done.2, bf16[320,1536]{1,0:T(8,128)(2,1)} %bitcast.133, bf16[4,320,384]{2,1,0:T(8,128)(2,1)} %bitcast.146, s32[]{:T(128)S(6)} %select_n.149), kind=kOutput, calls=%fused_computation.8 | convolution fusion | flops 378667008 | bytes 8306692 | tf_op jit(solution)/shard_map/dot_general | solution.py:49
  153.1 12.4 %all-to-all-done = bf16[8,128,384]{2,1,0:T(8,128)(2,1)} async-done(((bf16[8,128,384]{2,1,0:T(8,128)(2,1)}), bf16[8,128,384]{2,1,0:T(8,128)(2,1)}, u32[]{:S(2)}, u32[]{:S(2)}) %all-to-all-start) | async-done | bytes 786464 | tf_op jit(solution)/shard_map/all_to_all | solution.py:144
  (117 shorter events, 36.2 us)
Async XLA Ops:
  0.6 61.7 %copy-start = (bf16[1536,384]{1,0:T(8,128)(2,1)S(1)}, bf16[1536,384]{1,0:T(8,128)(2,1)}, u32[]{:S(2)}) copy-start(bf16[1536,384]{1,0:T(8,128)(2,1)} %param.7) | copy-start | bytes 3538948
  0.6 25.2 %copy-start.10 = (bf16[128,384]{1,0:T(8,128)(2,1)S(1)}, bf16[128,384]{1,0:T(8,128)(2,1)}, u32[]{:S(2)}) copy-start(bf16[128,384]{1,0:T(8,128)(2,1)} %param.4) | copy-start | bytes 294916
  2.1 23.9 %collective-permute-start = (bf16[64,768]{1,0:T(8,128)(2,1)S(1)}, bf16[64,768]{1,0:T(8,128)(2,1)S(1)}, u32[]{:S(2)}, u32[]{:S(2)}) collective-permute-start(bf16[64,768]{1,0:T(8,128)(2,1)S(1)} %get-tuple-element.30), channel_id=1, source_target_pairs={{0,0},{1,16},{2,32},{3,48},{4,64},{5,80},{6,96},{7,112},{8,128},{9... | collective-permute-start | bytes 294920 | tf_op jit(solution)/shard_map/ppermute | solution.py:96
  11.0 15.0 %collective-permute-start.1 = (bf16[64,768]{1,0:T(8,128)(2,1)S(1)}, bf16[64,768]{1,0:T(8,128)(2,1)S(1)}, u32[]{:S(2)}, u32[]{:S(2)}) collective-permute-start(bf16[64,768]{1,0:T(8,128)(2,1)S(1)} %get-tuple-element.31), channel_id=1, source_target_pairs={{0,16},{1,0},{2,48},{3,32},{4,80},{5,64},{6,112},{7,96},{8,144},{9... | collective-permute-start | bytes 294920 | tf_op jit(solution)/shard_map/ppermute | solution.py:97
  23.9 13.7 %collective-permute-start.13 = (bf16[128,384]{1,0:T(8,128)(2,1)}, bf16[128,384]{1,0:T(8,128)(2,1)S(1)}, u32[]{:S(2)}, u32[]{:S(2)}) collective-permute-start(bf16[128,384]{1,0:T(8,128)(2,1)} %param.4), channel_id=1, source_target_pairs={{0,64},{64,0},{128,192},{192,128},{256,320},{320,256},{384,448},{4... | collective-permute-start | bytes 294920 | tf_op jit(solution)/shard_map/ppermute | solution.py:45
  26.1 16.3 %collective-permute-start.9 = (bf16[24,1536]{1,0:T(8,128)(2,1)S(1)}, bf16[24,1536]{1,0:T(8,128)(2,1)S(1)}, u32[]{:S(2)}, u32[]{:S(2)}) collective-permute-start(bf16[24,1536]{1,0:T(8,128)(2,1)S(1)} %get-tuple-element.9), channel_id=1, source_target_pairs={{0,8},{8,0},{16,24},{24,16},{32,56},{40,48},{48,40},{56,32},{1,9},... | collective-permute-start | bytes 221192 | tf_op jit(solution)/shard_map/ppermute | solution.py:45
  37.6 49.3 %collective-permute-start.14 = (bf16[2,128,384]{2,1,0:T(8,128)(2,1)S(1)}, bf16[2,128,384]{2,1,0:T(8,128)(2,1)S(1)}, u32[]{:S(2)}, u32[]{:S(2)}) collective-permute-start(bf16[2,128,384]{2,1,0:T(8,128)(2,1)S(1)} %pad_maximum_fusion.3), channel_id=1, source_target_pairs={{0,448},{64,128},{128,64},{192,256},{256,192},{320,384},{384,320},... | collective-permute-start | bytes 589832 | tf_op jit(solution)/shard_map/ppermute | solution.py:45
  40.4 6.8 %collective-permute-start.2 = (bf16[40,1536]{1,0:T(8,128)(2,1)S(1)}, bf16[40,1536]{1,0:T(8,128)(2,1)S(1)}, u32[]{:S(2)}, u32[]{:S(2)}) collective-permute-start(bf16[40,1536]{1,0:T(8,128)(2,1)S(1)} %get-tuple-element.7), channel_id=1, source_target_pairs={{0,1},{1,0},{2,3},{3,2},{4,5},{5,4},{6,7},{7,6},{32,39},{33,34},{3... | collective-permute-start | bytes 368648 | tf_op jit(solution)/shard_map/ppermute | solution.py:45
  42.4 9.1 %collective-permute-start.10 = (bf16[2,24,1536]{2,1,0:T(8,128)(2,1)S(1)}, bf16[2,24,1536]{2,1,0:T(8,128)(2,1)S(1)}, u32[]{:S(2)}, u32[]{:S(2)}) collective-permute-start(bf16[2,24,1536]{2,1,0:T(8,128)(2,1)S(1)} %pad_maximum_fusion.4), channel_id=1, source_target_pairs={{0,24},{8,16},{16,8},{24,0},{32,40},{40,32},{48,56},{56,48},{1,25}... | collective-permute-start | bytes 442376 | tf_op jit(solution)/shard_map/ppermute | solution.py:45
  47.3 8.1 %collective-permute-start.3 = (bf16[2,40,1536]{2,1,0:T(8,128)(2,1)S(1)}, bf16[2,40,1536]{2,1,0:T(8,128)(2,1)S(1)}, u32[]{:S(2)}, u32[]{:S(2)}) collective-permute-start(bf16[2,40,1536]{2,1,0:T(8,128)(2,1)S(1)} %pad_maximum_fusion.2), channel_id=1, source_target_pairs={{0,7},{1,2},{2,1},{3,4},{4,3},{5,6},{6,5},{7,0},{32,33},{33,32},{3... | collective-permute-start | bytes 737288 | tf_op jit(solution)/shard_map/ppermute | solution.py:45
  51.6 8.7 %collective-permute-start.11 = (bf16[4,24,1536]{2,1,0:T(8,128)(2,1)S(1)}, bf16[4,24,1536]{2,1,0:T(8,128)(2,1)S(1)}, u32[]{:S(2)}, u32[]{:S(2)}) collective-permute-start(bf16[4,24,1536]{2,1,0:T(8,128)(2,1)S(1)} %slice_dynamic-update-slice_fusion.12), channel_id=1, source_target_pairs={{0,1},{1,0},{2,3},{3,2},{4,5},{5,4},{6,7},{7,6},{32,39},{33,34},{3... | collective-permute-start | bytes 884744 | tf_op jit(solution)/shard_map/ppermute | solution.py:45
  55.4 8.1 %collective-permute-start.4 = (bf16[2,40,1536]{2,1,0:T(8,128)(2,1)S(1)}, bf16[2,40,1536]{2,1,0:T(8,128)(2,1)S(1)}, u32[]{:S(2)}, u32[]{:S(2)}) collective-permute-start(bf16[2,40,1536]{2,1,0:T(8,128)(2,1)S(1)} %collective-permute-done.3), channel_id=1, source_target_pairs={{0,1},{1,0},{2,3},{3,2},{4,5},{5,4},{6,7},{7,6},{32,39},{33,34},{3... | collective-permute-start | bytes 737288 | tf_op jit(solution)/shard_map/ppermute | solution.py:45
  60.4 19.7 %collective-permute-start.12 = (bf16[2,4,24,1536]{3,2,1,0:T(8,128)(2,1)S(1)}, bf16[2,4,24,1536]{3,2,1,0:T(8,128)(2,1)S(1)}, u32[]{:S(2)}, u32[]{:S(2)}) collective-permute-start(bf16[2,4,24,1536]{3,2,1,0:T(8,128)(2,1)S(1)} %pad_maximum_fusion.1), channel_id=1, source_target_pairs={{0,7},{1,2},{2,1},{3,4},{4,3},{5,6},{6,5},{7,0},{32,33},{33,32},{3... | collective-permute-start | bytes 1769480 | tf_op jit(solution)/shard_map/ppermute | solution.py:45
  63.5 10.4 %collective-permute-start.5 = (bf16[2,40,1536]{2,1,0:T(8,128)(2,1)S(1)}, bf16[2,40,1536]{2,1,0:T(8,128)(2,1)S(1)}, u32[]{:S(2)}, u32[]{:S(2)}) collective-permute-start(bf16[2,40,1536]{2,1,0:T(8,128)(2,1)S(1)} %collective-permute-done.4), channel_id=1, source_target_pairs={{0,7},{1,2},{2,1},{3,4},{4,3},{5,6},{6,5},{7,0},{32,33},{33,32},{3... | collective-permute-start | bytes 737288 | tf_op jit(solution)/shard_map/ppermute | solution.py:45
  74.0 26.8 %collective-permute-start.6 = (bf16[8,40,1536]{2,1,0:T(8,128)(2,1)S(1)}, bf16[8,40,1536]{2,1,0:T(8,128)(2,1)S(1)}, u32[]{:S(2)}, u32[]{:S(2)}) collective-permute-start(bf16[8,40,1536]{2,1,0:T(8,128)(2,1)S(1)} %slice_dynamic-update-slice_fusion), channel_id=1, source_target_pairs={{0,8},{8,0},{16,24},{24,16},{32,56},{40,48},{48,40},{56,32},{1,9},... | collective-permute-start | bytes 2949128 | tf_op jit(solution)/shard_map/ppermute | solution.py:45
  76.3 27.9 %collective-permute-start.7 = (bf16[8,40,1536]{2,1,0:T(8,128)(2,1)S(1)}, bf16[8,40,1536]{2,1,0:T(8,128)(2,1)S(1)}, u32[]{:S(2)}, u32[]{:S(2)}) collective-permute-start(bf16[8,40,1536]{2,1,0:T(8,128)(2,1)S(1)} %slice_dynamic-update-slice_fusion), channel_id=1, source_target_pairs={{0,24},{8,16},{16,8},{24,0},{32,40},{40,32},{48,56},{56,48},{1,25}... | collective-permute-start | bytes 2949128 | tf_op jit(solution)/shard_map/ppermute | solution.py:45
  80.1 13.8 %collective-permute-start.15 = (bf16[2,4,24,1536]{3,2,1,0:T(8,128)(2,1)S(1)}, bf16[2,4,24,1536]{3,2,1,0:T(8,128)(2,1)S(1)}, u32[]{:S(2)}, u32[]{:S(2)}) collective-permute-start(bf16[2,4,24,1536]{3,2,1,0:T(8,128)(2,1)S(1)} %collective-permute-done.12), channel_id=1, source_target_pairs={{0,1},{1,0},{2,3},{3,2},{4,5},{5,4},{6,7},{7,6},{32,39},{33,34},{3... | collective-permute-start | bytes 1769480 | tf_op jit(solution)/shard_map/ppermute | solution.py:45
  93.9 11.1 %collective-permute-start.18 = (bf16[2,128,384]{2,1,0:T(8,128)(2,1)S(1)}, bf16[2,128,384]{2,1,0:T(8,128)(2,1)S(1)}, u32[]{:S(2)}, u32[]{:S(2)}) collective-permute-start(bf16[2,128,384]{2,1,0:T(8,128)(2,1)S(1)} %collective-permute-done.14), channel_id=1, source_target_pairs={{0,64},{64,0},{128,192},{192,128},{256,320},{320,256},{384,448},{4... | collective-permute-start | bytes 589832 | tf_op jit(solution)/shard_map/ppermute | solution.py:45
  98.0 27.6 %collective-permute-start.16 = (bf16[2,4,24,1536]{3,2,1,0:T(8,128)(2,1)S(1)}, bf16[2,4,24,1536]{3,2,1,0:T(8,128)(2,1)S(1)}, u32[]{:S(2)}, u32[]{:S(2)}) collective-permute-start(bf16[2,4,24,1536]{3,2,1,0:T(8,128)(2,1)S(1)} %collective-permute-done.15), channel_id=1, source_target_pairs={{0,7},{1,2},{2,1},{3,4},{4,3},{5,6},{6,5},{7,0},{32,33},{33,32},{3... | collective-permute-start | bytes 1769480 | tf_op jit(solution)/shard_map/ppermute | solution.py:45
  100.8 25.8 %collective-permute-start.8 = (bf16[8,40,1536]{2,1,0:T(8,128)(2,1)S(1)}, bf16[8,40,1536]{2,1,0:T(8,128)(2,1)S(1)}, u32[]{:S(2)}, u32[]{:S(2)}) collective-permute-start(bf16[8,40,1536]{2,1,0:T(8,128)(2,1)S(1)} %collective-permute-done.6), channel_id=1, source_target_pairs={{0,24},{8,16},{16,8},{24,0},{32,40},{40,32},{48,56},{56,48},{1,25}... | collective-permute-start | bytes 2949128 | tf_op jit(solution)/shard_map/ppermute | solution.py:45
  104.9 6.7 %collective-permute-start.19 = (bf16[2,128,384]{2,1,0:T(8,128)(2,1)S(1)}, bf16[2,128,384]{2,1,0:T(8,128)(2,1)S(1)}, u32[]{:S(2)}, u32[]{:S(2)}) collective-permute-start(bf16[2,128,384]{2,1,0:T(8,128)(2,1)S(1)} %collective-permute-done.18), channel_id=1, source_target_pairs={{0,448},{64,128},{128,64},{192,256},{256,192},{320,384},{384,320},... | collective-permute-start | bytes 589832 | tf_op jit(solution)/shard_map/ppermute | solution.py:45
  111.7 17.8 %collective-permute-start.20 = (bf16[8,128,384]{2,1,0:T(8,128)(2,1)S(1)}, bf16[8,128,384]{2,1,0:T(8,128)(2,1)S(1)}, u32[]{:S(2)}, u32[]{:S(2)}) collective-permute-start(bf16[8,128,384]{2,1,0:T(8,128)(2,1)S(1)} %slice_dynamic-update-slice_fusion.6), channel_id=1, source_target_pairs={{0,32},{32,0},{1,33},{33,1},{2,34},{34,2},{3,35},{35,3},{4,36},{36... | collective-permute-start | bytes 2359304 | tf_op jit(solution)/shard_map/ppermute | solution.py:125
  127.6 10.8 %collective-permute-start.17 = (bf16[2,2,4,64,384]{4,3,2,1,0:T(8,128)(2,1)S(1)}, bf16[2,2,4,64,384]{4,3,2,1,0:T(8,128)(2,1)S(1)}, u32[]{:S(2)}, u32[]{:S(2)}) collective-permute-start(bf16[2,2,4,64,384]{4,3,2,1,0:T(8,128)(2,1)S(1)} %fusion.22), channel_id=1, source_target_pairs={{0,32},{32,0},{1,33},{33,1},{2,34},{34,2},{3,35},{35,3},{4,36},{36... | collective-permute-start | bytes 2359304 | tf_op jit(solution)/shard_map/ppermute | solution.py:142
  139.6 25.9 %all-to-all-start = ((bf16[8,128,384]{2,1,0:T(8,128)(2,1)}), bf16[8,128,384]{2,1,0:T(8,128)(2,1)}, u32[]{:S(2)}, u32[]{:S(2)}) async-start(bf16[8,128,384]{2,1,0:T(8,128)(2,1)} %bitcast.148), calls=%async_computation | async-start | bytes 1572864 | tf_op jit(solution)/shard_map/all_to_all | solution.py:144
  (11 other events, 36.2 us)

commit v7 on v6

--- a/solution.py
+++ b/solution.py
@@ -72,18 +72,23 @@
     return whole
 
 
-def products(pairs, weight_t, tokens_of, at, size, sign, total):
+def shares_of(pairs, weight_t):
     shares = []
     for steps, pair in pairs:
-        flat = pair.reshape(-1, 1536)
-        share = dot(flat, weight_t, ((1,), (0,)))
+        share = dot(pair.reshape(-1, 1536), weight_t, ((1,), (0,)))
         shares.append((steps, share.reshape(*pair.shape[:-1], 384)))
+    return shares
+
+
+def weight_sums(pairs, tokens_of, at, size, sign, total):
+    for steps, pair in pairs:
         tokens = [
             lax.dynamic_index_in_dim(tokens_of, (at + k * sign) & (size - 1), 0, False)
             for k in steps
         ]
+        flat = pair.reshape(-1, 1536)
         total = total + dot(flat, jnp.concatenate(tokens, axis=0), ((0,), (0,)))
-    return shares, total
+    return total
 
 
 def on_device(inputs, pre_act, grad_act, weight_t):
@@ -130,16 +135,20 @@
     in_a = seen[:, :, :, :, :A].transpose(3, 0, 2, 1, 4, 5).reshape(4, 8 * A, 384)
     in_b = seen[:, :, :, :, A:].transpose(2, 1, 3, 0, 4, 5).reshape(8, 4 * B, 384)
 
-    shares_a, total = products(pairs_a, weight_t, in_a, x, 4, sign_x, 0.0)
-    shares_b, total = products(pairs_b, weight_t, in_b, y, 8, sign_y, total)
-    grad_weight = total.astype(BF)
+    shares_a = shares_of(pairs_a, weight_t)
+    shares_b = shares_of(pairs_b, weight_t)
 
     share_a = place(shares_a, x, 4, sign_x).reshape(2, 2, 2, 4, A, 384)
     share_b = place(shares_b, y, 8, sign_y).reshape(2, 4, 2, 2, B, 384).transpose(2, 3, 0, 1, 4, 5)
     share = jnp.concatenate([share_a, share_b], axis=4)
     keep = lax.dynamic_index_in_dim(share, core, 2, False)
     give = lax.dynamic_index_in_dim(share, 1 - core, 2, False).astype(BF)
-    both = keep + lax.ppermute(give, "core", [(0, 1), (1, 0)]).astype(F32)
+    mate = lax.ppermute(give, "core", [(0, 1), (1, 0)])
+    in_a, in_b, mate = lax.optimization_barrier((in_a, in_b, mate))
+    total = weight_sums(pairs_a, in_a, x, 4, sign_x, 0.0)
+    total = weight_sums(pairs_b, in_b, y, 8, sign_y, total)
+    grad_weight = total.astype(BF)
+    both = keep + mate.astype(F32)
     sent = both.astype(BF).transpose(1, 2, 0, 3, 4).reshape(8, 128, 384)
     parts = lax.all_to_all(sent, "z", 0, 0)
     grad_inputs = parts.astype(F32).sum(axis=0).astype(BF)

time: 168 us -> 168 us (level)
  local copies, waits for them, and re-layouts: 3.7 us -> 13.8 us
  matrix products: 21 us -> 12 us
  starting transfers between devices: 98.6 us -> 94.5 us
  other arithmetic: 4.14 us -> 7.42 us
    dot_general x16, matrix products: 21 us -> 12 us  [dot(): return lax.dot_general(a, b, (dims, ((), ())), preferred_element_type=F32)]
    ppermute x1, starting transfers between devices: 8.84 us -> 1.92 us  [on_device(): same = lax.ppermute(same, ALL, to_slots(0))]
    ppermute x17, starting transfers between devices: 56.7 us -> 63 us  [exchange(): return lax.ppermute(block, ROW if axis == 'z' else ('core', axis), pairs)]
    dynamic_update_slice x26, local copies, waits for them, and re-layouts: 0.48 us -> 5.43 us  [place(): whole = lax.dynamic_update_slice(whole, pair[i:i + 1], start)]
    unnamed x26 -> x42, local copies, waits for them, and re-layouts: 0.53 us -> 2.71 us
    ppermute x1, starting transfers between devices: 12.9 us -> 10.8 us  [on_device(): other = lax.ppermute(other, ALL, to_slots(1))]
  transfers between devices with their start and end apart: 22 -> 22, of which waited for: 8 -> 9; matrix products, arithmetic and copies ran while one was open for 14% -> 16% of each run, Pallas kernels for 0% -> 0%
where the time goes in v7:
time: 168 us; the launch traced here: 166 us
  starting transfers between devices  94.5 us (56%)
  waiting for transfers between devices  37 us (22%)
  local copies, waits for them, and re-layouts  13.8 us (8%)
  matrix products  12 us (7%)
  other arithmetic  7.42 us (4%)
    ppermute x17, starting transfers between devices, exchange(): return lax.ppermute(block, ROW if axis == 'z' else ('core', axis), pairs)  63 us
    ppermute x17, waiting for transfers between devices, exchange(): return lax.ppermute(block, ROW if axis == 'z' else ('core', axis), pairs)  25.6 us
    ppermute x1, starting transfers between devices, on_device(): mate_z = lax.ppermute(own_z, 'core', [(0, 1), (1, 0)])  12.4 us
    dot_general x16, matrix products, dot(): return lax.dot_general(a, b, (dims, ((), ())), preferred_element_type=F32)  12 us
    all_to_all x1, waiting for transfers between devices, on_device(): parts = lax.all_to_all(sent, 'z', 0, 0)  11.5 us
    ppermute x1, starting transfers between devices, on_device(): other = lax.ppermute(other, ALL, to_slots(1))  10.8 us
    dynamic_update_slice x26, local copies, waits for them, and re-layouts, place(): whole = lax.dynamic_update_slice(whole, pair[i:i + 1], start)  5.43 us
    all_to_all x1, starting transfers between devices, on_device(): parts = lax.all_to_all(sent, 'z', 0, 0)  4.52 us
  transfers between devices with their start and end apart: 22, of which 9 were waited for; matrix products, arithmetic and copies ran while one was open for 16% of the time, Pallas kernels for 0%

profile of v7, /device:TPU:1, one launch (start us, length us, event | category | flops | bytes accessed | tf_op | source)
XLA Modules:
  0.0 166.3 jit_solution(3603772452024024890)
XLA Ops:
  0.7 11.6 %collective-permute-start.13 = (bf16[128,384]{1,0:T(8,128)(2,1)}, bf16[128,384]{1,0:T(8,128)(2,1)S(1)}, u32[]{:S(2)}, u32[]{:S(2)}) collective-permute-start(bf16[128,384]{1,0:T(8,128)(2,1)} %param.4), channel_id=1, source_target_pairs={{0,64},{64,0},{128,192},{192,128},{256,320},{320,256},{384,448},{4... | collective-permute-start | bytes 294920 | tf_op jit(solution)/shard_map/ppermute | solution.py:45
  13.6 1.9 %collective-permute-start = (bf16[64,768]{1,0:T(8,128)(2,1)S(1)}, bf16[64,768]{1,0:T(8,128)(2,1)S(1)}, u32[]{:S(2)}, u32[]{:S(2)}) collective-permute-start(bf16[64,768]{1,0:T(8,128)(2,1)S(1)} %get-tuple-element.36), channel_id=1, source_target_pairs={{0,0},{1,16},{2,32},{3,48},{4,64},{5,80},{6,96},{7,112},{8,128},{9... | collective-permute-start | bytes 294920 | tf_op jit(solution)/shard_map/ppermute | solution.py:101
  15.6 10.8 %collective-permute-start.1 = (bf16[64,768]{1,0:T(8,128)(2,1)S(1)}, bf16[64,768]{1,0:T(8,128)(2,1)S(1)}, u32[]{:S(2)}, u32[]{:S(2)}) collective-permute-start(bf16[64,768]{1,0:T(8,128)(2,1)S(1)} %get-tuple-element.37), channel_id=1, source_target_pairs={{0,16},{1,0},{2,48},{3,32},{4,80},{5,64},{6,112},{7,96},{8,144},{9... | collective-permute-start | bytes 294920 | tf_op jit(solution)/shard_map/ppermute | solution.py:102
  28.0 2.2 %collective-permute-start.14 = (bf16[2,128,384]{2,1,0:T(8,128)(2,1)S(1)}, bf16[2,128,384]{2,1,0:T(8,128)(2,1)S(1)}, u32[]{:S(2)}, u32[]{:S(2)}) collective-permute-start(bf16[2,128,384]{2,1,0:T(8,128)(2,1)S(1)} %pad_maximum_fusion.3), channel_id=1, source_target_pairs={{0,448},{64,128},{128,64},{192,256},{256,192},{320,384},{384,320},... | collective-permute-start | bytes 589832 | tf_op jit(solution)/shard_map/ppermute | solution.py:45
  30.3 10.7 %collective-permute-start.9 = (bf16[24,1536]{1,0:T(8,128)(2,1)S(1)}, bf16[24,1536]{1,0:T(8,128)(2,1)S(1)}, u32[]{:S(2)}, u32[]{:S(2)}) collective-permute-start(bf16[24,1536]{1,0:T(8,128)(2,1)S(1)} %get-tuple-element.15), channel_id=1, source_target_pairs={{0,8},{8,0},{16,24},{24,16},{32,56},{40,48},{48,40},{56,32},{1,9},... | collective-permute-start | bytes 221192 | tf_op jit(solution)/shard_map/ppermute | solution.py:45
  41.2 2.0 %collective-permute-start.2 = (bf16[40,1536]{1,0:T(8,128)(2,1)S(1)}, bf16[40,1536]{1,0:T(8,128)(2,1)S(1)}, u32[]{:S(2)}, u32[]{:S(2)}) collective-permute-start(bf16[40,1536]{1,0:T(8,128)(2,1)S(1)} %get-tuple-element.13), channel_id=1, source_target_pairs={{0,1},{1,0},{2,3},{3,2},{4,5},{5,4},{6,7},{7,6},{32,39},{33,34},{3... | collective-permute-start | bytes 368648 | tf_op jit(solution)/shard_map/ppermute | solution.py:45
  43.8 2.3 %collective-permute-start.10 = (bf16[2,24,1536]{2,1,0:T(8,128)(2,1)S(1)}, bf16[2,24,1536]{2,1,0:T(8,128)(2,1)S(1)}, u32[]{:S(2)}, u32[]{:S(2)}) collective-permute-start(bf16[2,24,1536]{2,1,0:T(8,128)(2,1)S(1)} %pad_maximum_fusion.4), channel_id=1, source_target_pairs={{0,24},{8,16},{16,8},{24,0},{32,40},{40,32},{48,56},{56,48},{1,25}... | collective-permute-start | bytes 442376 | tf_op jit(solution)/shard_map/ppermute | solution.py:45
  46.2 2.2 %collective-permute-done.2 = bf16[40,1536]{1,0:T(8,128)(2,1)S(1)} collective-permute-done((bf16[40,1536]{1,0:T(8,128)(2,1)S(1)}, bf16[40,1536]{1,0:T(8,128)(2,1)S(1)}, u32[]{:S(2)}, u32[]{:S(2)}) %collective-permute-start.2) | collective-permute-done | bytes 122912 | tf_op jit(solution)/shard_map/ppermute | solution.py:45
  48.3 1.9 %collective-permute-start.3 = (bf16[2,40,1536]{2,1,0:T(8,128)(2,1)S(1)}, bf16[2,40,1536]{2,1,0:T(8,128)(2,1)S(1)}, u32[]{:S(2)}, u32[]{:S(2)}) collective-permute-start(bf16[2,40,1536]{2,1,0:T(8,128)(2,1)S(1)} %pad_maximum_fusion.2), channel_id=1, source_target_pairs={{0,7},{1,2},{2,1},{3,4},{4,3},{5,6},{6,5},{7,0},{32,33},{33,32},{3... | collective-permute-start | bytes 737288 | tf_op jit(solution)/shard_map/ppermute | solution.py:45
  50.4 3.9 %collective-permute-start.11 = (bf16[4,24,1536]{2,1,0:T(8,128)(2,1)S(1)}, bf16[4,24,1536]{2,1,0:T(8,128)(2,1)S(1)}, u32[]{:S(2)}, u32[]{:S(2)}) collective-permute-start(bf16[4,24,1536]{2,1,0:T(8,128)(2,1)S(1)} %slice_dynamic-update-slice_fusion.12), channel_id=1, source_target_pairs={{0,1},{1,0},{2,3},{3,2},{4,5},{5,4},{6,7},{7,6},{32,39},{33,34},{3... | collective-permute-start | bytes 884744 | tf_op jit(solution)/shard_map/ppermute | solution.py:45
  59.1 2.7 %collective-permute-start.12 = (bf16[2,4,24,1536]{3,2,1,0:T(8,128)(2,1)S(1)}, bf16[2,4,24,1536]{3,2,1,0:T(8,128)(2,1)S(1)}, u32[]{:S(2)}, u32[]{:S(2)}) collective-permute-start(bf16[2,4,24,1536]{3,2,1,0:T(8,128)(2,1)S(1)} %pad_maximum_fusion.1), channel_id=1, source_target_pairs={{0,7},{1,2},{2,1},{3,4},{4,3},{5,6},{6,5},{7,0},{32,33},{33,32},{3... | collective-permute-start | bytes 1769480 | tf_op jit(solution)/shard_map/ppermute | solution.py:45
  66.2 6.7 %collective-permute-done.5 = bf16[2,40,1536]{2,1,0:T(8,128)(2,1)S(1)} collective-permute-done((bf16[2,40,1536]{2,1,0:T(8,128)(2,1)S(1)}, bf16[2,40,1536]{2,1,0:T(8,128)(2,1)S(1)}, u32[]{:S(2)}, u32[]{:S(2)}) %collective-permute-start.5) | collective-permute-done | bytes 245792 | tf_op jit(solution)/shard_map/ppermute | solution.py:45
  72.9 2.9 %collective-permute-start.7 = (bf16[8,40,1536]{2,1,0:T(8,128)(2,1)S(1)}, bf16[8,40,1536]{2,1,0:T(8,128)(2,1)S(1)}, u32[]{:S(2)}, u32[]{:S(2)}) collective-permute-start(bf16[8,40,1536]{2,1,0:T(8,128)(2,1)S(1)} %slice_dynamic-update-slice_fusion), channel_id=1, source_target_pairs={{0,24},{8,16},{16,8},{24,0},{32,40},{40,32},{48,56},{56,48},{1,25}... | collective-permute-start | bytes 2949128 | tf_op jit(solution)/shard_map/ppermute | solution.py:45
  75.8 3.3 %collective-permute-start.6 = (bf16[8,40,1536]{2,1,0:T(8,128)(2,1)S(1)}, bf16[8,40,1536]{2,1,0:T(8,128)(2,1)S(1)}, u32[]{:S(2)}, u32[]{:S(2)}) collective-permute-start(bf16[8,40,1536]{2,1,0:T(8,128)(2,1)S(1)} %slice_dynamic-update-slice_fusion), channel_id=1, source_target_pairs={{0,8},{8,0},{16,24},{24,16},{32,56},{40,48},{48,40},{56,32},{1,9},... | collective-permute-start | bytes 2949128 | tf_op jit(solution)/shard_map/ppermute | solution.py:45
  80.0 1.9 %collective-permute-start.15 = (bf16[2,4,24,1536]{3,2,1,0:T(8,128)(2,1)S(1)}, bf16[2,4,24,1536]{3,2,1,0:T(8,128)(2,1)S(1)}, u32[]{:S(2)}, u32[]{:S(2)}) collective-permute-start(bf16[2,4,24,1536]{3,2,1,0:T(8,128)(2,1)S(1)} %collective-permute-done.12), channel_id=1, source_target_pairs={{0,1},{1,0},{2,3},{3,2},{4,5},{5,4},{6,7},{7,6},{32,39},{33,34},{3... | collective-permute-start | bytes 1769480 | tf_op jit(solution)/shard_map/ppermute | solution.py:45
  82.5 9.6 %collective-permute-done.15 = bf16[2,4,24,1536]{3,2,1,0:T(8,128)(2,1)S(1)} collective-permute-done((bf16[2,4,24,1536]{3,2,1,0:T(8,128)(2,1)S(1)}, bf16[2,4,24,1536]{3,2,1,0:T(8,128)(2,1)S(1)}, u32[]{:S(2)}, u32[]{:S(2)}) %collective-permute-start.15) | collective-permute-done | bytes 589856 | tf_op jit(solution)/shard_map/ppermute | solution.py:45
  92.1 5.5 %collective-permute-start.17 = (bf16[2,128,384]{2,1,0:T(8,128)(2,1)S(1)}, bf16[2,128,384]{2,1,0:T(8,128)(2,1)S(1)}, u32[]{:S(2)}, u32[]{:S(2)}) collective-permute-start(bf16[2,128,384]{2,1,0:T(8,128)(2,1)S(1)} %collective-permute-done.14), channel_id=1, source_target_pairs={{0,64},{64,0},{128,192},{192,128},{256,320},{320,256},{384,448},{4... | collective-permute-start | bytes 589832 | tf_op jit(solution)/shard_map/ppermute | solution.py:45
  98.1 1.9 %collective-permute-start.16 = (bf16[2,4,24,1536]{3,2,1,0:T(8,128)(2,1)S(1)}, bf16[2,4,24,1536]{3,2,1,0:T(8,128)(2,1)S(1)}, u32[]{:S(2)}, u32[]{:S(2)}) collective-permute-start(bf16[2,4,24,1536]{3,2,1,0:T(8,128)(2,1)S(1)} %collective-permute-done.15), channel_id=1, source_target_pairs={{0,7},{1,2},{2,1},{3,4},{4,3},{5,6},{6,5},{7,0},{32,33},{33,32},{3... | collective-permute-start | bytes 1769480 | tf_op jit(solution)/shard_map/ppermute | solution.py:45
  101.9 2.0 %collective-permute-start.8 = (bf16[8,40,1536]{2,1,0:T(8,128)(2,1)S(1)}, bf16[8,40,1536]{2,1,0:T(8,128)(2,1)S(1)}, u32[]{:S(2)}, u32[]{:S(2)}) collective-permute-start(bf16[8,40,1536]{2,1,0:T(8,128)(2,1)S(1)} %collective-permute-done.6), channel_id=1, source_target_pairs={{0,24},{8,16},{16,8},{24,0},{32,40},{40,32},{48,56},{56,48},{1,25}... | collective-permute-start | bytes 2949128 | tf_op jit(solution)/shard_map/ppermute | solution.py:45
  105.4 4.2 %collective-permute-start.18 = (bf16[2,128,384]{2,1,0:T(8,128)(2,1)S(1)}, bf16[2,128,384]{2,1,0:T(8,128)(2,1)S(1)}, u32[]{:S(2)}, u32[]{:S(2)}) collective-permute-start(bf16[2,128,384]{2,1,0:T(8,128)(2,1)S(1)} %collective-permute-done.17), channel_id=1, source_target_pairs={{0,448},{64,128},{128,64},{192,256},{256,192},{320,384},{384,320},... | collective-permute-start | bytes 589832 | tf_op jit(solution)/shard_map/ppermute | solution.py:45
  110.9 2.0 %collective-permute-done.18 = bf16[2,128,384]{2,1,0:T(8,128)(2,1)S(1)} collective-permute-done((bf16[2,128,384]{2,1,0:T(8,128)(2,1)S(1)}, bf16[2,128,384]{2,1,0:T(8,128)(2,1)S(1)}, u32[]{:S(2)}, u32[]{:S(2)}) %collective-permute-start.18) | collective-permute-done | bytes 196640 | tf_op jit(solution)/shard_map/ppermute | solution.py:45
  114.2 12.4 %collective-permute-start.19 = (bf16[8,128,384]{2,1,0:T(8,128)(2,1)}, bf16[8,128,384]{2,1,0:T(8,128)(2,1)}, u32[]{:S(2)}, u32[]{:S(2)}) collective-permute-start(bf16[8,128,384]{2,1,0:T(8,128)(2,1)} %slice_dynamic-update-slice_fusion.6), channel_id=1, source_target_pairs={{0,32},{32,0},{1,33},{33,1},{2,34},{34,2},{3,35},{35,3},{4,36},{36... | collective-permute-start | bytes 2359304 | tf_op jit(solution)/shard_map/ppermute | solution.py:130
  138.1 4.5 %all-to-all-start = ((bf16[8,128,384]{2,1,0:T(8,128)(2,1)}), bf16[8,128,384]{2,1,0:T(8,128)(2,1)}, u32[]{:S(2)}, u32[]{:S(2)}) async-start(bf16[8,128,384]{2,1,0:T(8,128)(2,1)} %bitcast.148), calls=%async_computation | async-start | bytes 1572864 | tf_op jit(solution)/shard_map/all_to_all | solution.py:153
  152.9 11.5 %all-to-all-done = bf16[8,128,384]{2,1,0:T(8,128)(2,1)} async-done(((bf16[8,128,384]{2,1,0:T(8,128)(2,1)}), bf16[8,128,384]{2,1,0:T(8,128)(2,1)}, u32[]{:S(2)}, u32[]{:S(2)}) %all-to-all-start) | async-done | bytes 786464 | tf_op jit(solution)/shard_map/all_to_all | solution.py:153
  (133 shorter events, 44.0 us)
Async XLA Ops:
  0.6 61.2 %copy-start = (bf16[1536,384]{1,0:T(8,128)(2,1)S(1)}, bf16[1536,384]{1,0:T(8,128)(2,1)}, u32[]{:S(2)}) copy-start(bf16[1536,384]{1,0:T(8,128)(2,1)} %param.7) | copy-start | bytes 3538948
  0.6 26.7 %copy-start.20 = (bf16[128,384]{1,0:T(8,128)(2,1)S(1)}, bf16[128,384]{1,0:T(8,128)(2,1)}, u32[]{:S(2)}) copy-start(bf16[128,384]{1,0:T(8,128)(2,1)} %param.4) | copy-start | bytes 294916
  0.7 27.3 %collective-permute-start.13 = (bf16[128,384]{1,0:T(8,128)(2,1)}, bf16[128,384]{1,0:T(8,128)(2,1)S(1)}, u32[]{:S(2)}, u32[]{:S(2)}) collective-permute-start(bf16[128,384]{1,0:T(8,128)(2,1)} %param.4), channel_id=1, source_target_pairs={{0,64},{64,0},{128,192},{192,128},{256,320},{320,256},{384,448},{4... | collective-permute-start | bytes 294920 | tf_op jit(solution)/shard_map/ppermute | solution.py:45
  13.6 16.6 %collective-permute-start = (bf16[64,768]{1,0:T(8,128)(2,1)S(1)}, bf16[64,768]{1,0:T(8,128)(2,1)S(1)}, u32[]{:S(2)}, u32[]{:S(2)}) collective-permute-start(bf16[64,768]{1,0:T(8,128)(2,1)S(1)} %get-tuple-element.36), channel_id=1, source_target_pairs={{0,0},{1,16},{2,32},{3,48},{4,64},{5,80},{6,96},{7,112},{8,128},{9... | collective-permute-start | bytes 294920 | tf_op jit(solution)/shard_map/ppermute | solution.py:101
  15.6 14.7 %collective-permute-start.1 = (bf16[64,768]{1,0:T(8,128)(2,1)S(1)}, bf16[64,768]{1,0:T(8,128)(2,1)S(1)}, u32[]{:S(2)}, u32[]{:S(2)}) collective-permute-start(bf16[64,768]{1,0:T(8,128)(2,1)S(1)} %get-tuple-element.37), channel_id=1, source_target_pairs={{0,16},{1,0},{2,48},{3,32},{4,80},{5,64},{6,112},{7,96},{8,144},{9... | collective-permute-start | bytes 294920 | tf_op jit(solution)/shard_map/ppermute | solution.py:102
  28.0 54.5 %collective-permute-start.14 = (bf16[2,128,384]{2,1,0:T(8,128)(2,1)S(1)}, bf16[2,128,384]{2,1,0:T(8,128)(2,1)S(1)}, u32[]{:S(2)}, u32[]{:S(2)}) collective-permute-start(bf16[2,128,384]{2,1,0:T(8,128)(2,1)S(1)} %pad_maximum_fusion.3), channel_id=1, source_target_pairs={{0,448},{64,128},{128,64},{192,256},{256,192},{320,384},{384,320},... | collective-permute-start | bytes 589832 | tf_op jit(solution)/shard_map/ppermute | solution.py:45
  30.3 13.5 %collective-permute-start.9 = (bf16[24,1536]{1,0:T(8,128)(2,1)S(1)}, bf16[24,1536]{1,0:T(8,128)(2,1)S(1)}, u32[]{:S(2)}, u32[]{:S(2)}) collective-permute-start(bf16[24,1536]{1,0:T(8,128)(2,1)S(1)} %get-tuple-element.15), channel_id=1, source_target_pairs={{0,8},{8,0},{16,24},{24,16},{32,56},{40,48},{48,40},{56,32},{1,9},... | collective-permute-start | bytes 221192 | tf_op jit(solution)/shard_map/ppermute | solution.py:45
  41.2 7.1 %collective-permute-start.2 = (bf16[40,1536]{1,0:T(8,128)(2,1)S(1)}, bf16[40,1536]{1,0:T(8,128)(2,1)S(1)}, u32[]{:S(2)}, u32[]{:S(2)}) collective-permute-start(bf16[40,1536]{1,0:T(8,128)(2,1)S(1)} %get-tuple-element.13), channel_id=1, source_target_pairs={{0,1},{1,0},{2,3},{3,2},{4,5},{5,4},{6,7},{7,6},{32,39},{33,34},{3... | collective-permute-start | bytes 368648 | tf_op jit(solution)/shard_map/ppermute | solution.py:45
  43.8 6.5 %collective-permute-start.10 = (bf16[2,24,1536]{2,1,0:T(8,128)(2,1)S(1)}, bf16[2,24,1536]{2,1,0:T(8,128)(2,1)S(1)}, u32[]{:S(2)}, u32[]{:S(2)}) collective-permute-start(bf16[2,24,1536]{2,1,0:T(8,128)(2,1)S(1)} %pad_maximum_fusion.4), channel_id=1, source_target_pairs={{0,24},{8,16},{16,8},{24,0},{32,40},{40,32},{48,56},{56,48},{1,25}... | collective-permute-start | bytes 442376 | tf_op jit(solution)/shard_map/ppermute | solution.py:45
  48.3 7.7 %collective-permute-start.3 = (bf16[2,40,1536]{2,1,0:T(8,128)(2,1)S(1)}, bf16[2,40,1536]{2,1,0:T(8,128)(2,1)S(1)}, u32[]{:S(2)}, u32[]{:S(2)}) collective-permute-start(bf16[2,40,1536]{2,1,0:T(8,128)(2,1)S(1)} %pad_maximum_fusion.2), channel_id=1, source_target_pairs={{0,7},{1,2},{2,1},{3,4},{4,3},{5,6},{6,5},{7,0},{32,33},{33,32},{3... | collective-permute-start | bytes 737288 | tf_op jit(solution)/shard_map/ppermute | solution.py:45
  50.4 8.7 %collective-permute-start.11 = (bf16[4,24,1536]{2,1,0:T(8,128)(2,1)S(1)}, bf16[4,24,1536]{2,1,0:T(8,128)(2,1)S(1)}, u32[]{:S(2)}, u32[]{:S(2)}) collective-permute-start(bf16[4,24,1536]{2,1,0:T(8,128)(2,1)S(1)} %slice_dynamic-update-slice_fusion.12), channel_id=1, source_target_pairs={{0,1},{1,0},{2,3},{3,2},{4,5},{5,4},{6,7},{7,6},{32,39},{33,34},{3... | collective-permute-start | bytes 884744 | tf_op jit(solution)/shard_map/ppermute | solution.py:45
  56.1 8.1 %collective-permute-start.4 = (bf16[2,40,1536]{2,1,0:T(8,128)(2,1)S(1)}, bf16[2,40,1536]{2,1,0:T(8,128)(2,1)S(1)}, u32[]{:S(2)}, u32[]{:S(2)}) collective-permute-start(bf16[2,40,1536]{2,1,0:T(8,128)(2,1)S(1)} %collective-permute-done.3), channel_id=1, source_target_pairs={{0,1},{1,0},{2,3},{3,2},{4,5},{5,4},{6,7},{7,6},{32,39},{33,34},{3... | collective-permute-start | bytes 737288 | tf_op jit(solution)/shard_map/ppermute | solution.py:45
  59.1 20.9 %collective-permute-start.12 = (bf16[2,4,24,1536]{3,2,1,0:T(8,128)(2,1)S(1)}, bf16[2,4,24,1536]{3,2,1,0:T(8,128)(2,1)S(1)}, u32[]{:S(2)}, u32[]{:S(2)}) collective-permute-start(bf16[2,4,24,1536]{3,2,1,0:T(8,128)(2,1)S(1)} %pad_maximum_fusion.1), channel_id=1, source_target_pairs={{0,7},{1,2},{2,1},{3,4},{4,3},{5,6},{6,5},{7,0},{32,33},{33,32},{3... | collective-permute-start | bytes 1769480 | tf_op jit(solution)/shard_map/ppermute | solution.py:45
  64.2 8.6 %collective-permute-start.5 = (bf16[2,40,1536]{2,1,0:T(8,128)(2,1)S(1)}, bf16[2,40,1536]{2,1,0:T(8,128)(2,1)S(1)}, u32[]{:S(2)}, u32[]{:S(2)}) collective-permute-start(bf16[2,40,1536]{2,1,0:T(8,128)(2,1)S(1)} %collective-permute-done.4), channel_id=1, source_target_pairs={{0,7},{1,2},{2,1},{3,4},{4,3},{5,6},{6,5},{7,0},{32,33},{33,32},{3... | collective-permute-start | bytes 737288 | tf_op jit(solution)/shard_map/ppermute | solution.py:45
  72.9 31.8 %collective-permute-start.7 = (bf16[8,40,1536]{2,1,0:T(8,128)(2,1)S(1)}, bf16[8,40,1536]{2,1,0:T(8,128)(2,1)S(1)}, u32[]{:S(2)}, u32[]{:S(2)}) collective-permute-start(bf16[8,40,1536]{2,1,0:T(8,128)(2,1)S(1)} %slice_dynamic-update-slice_fusion), channel_id=1, source_target_pairs={{0,24},{8,16},{16,8},{24,0},{32,40},{40,32},{48,56},{56,48},{1,25}... | collective-permute-start | bytes 2949128 | tf_op jit(solution)/shard_map/ppermute | solution.py:45
  75.8 26.1 %collective-permute-start.6 = (bf16[8,40,1536]{2,1,0:T(8,128)(2,1)S(1)}, bf16[8,40,1536]{2,1,0:T(8,128)(2,1)S(1)}, u32[]{:S(2)}, u32[]{:S(2)}) collective-permute-start(bf16[8,40,1536]{2,1,0:T(8,128)(2,1)S(1)} %slice_dynamic-update-slice_fusion), channel_id=1, source_target_pairs={{0,8},{8,0},{16,24},{24,16},{32,56},{40,48},{48,40},{56,32},{1,9},... | collective-permute-start | bytes 2949128 | tf_op jit(solution)/shard_map/ppermute | solution.py:45
  80.0 12.1 %collective-permute-start.15 = (bf16[2,4,24,1536]{3,2,1,0:T(8,128)(2,1)S(1)}, bf16[2,4,24,1536]{3,2,1,0:T(8,128)(2,1)S(1)}, u32[]{:S(2)}, u32[]{:S(2)}) collective-permute-start(bf16[2,4,24,1536]{3,2,1,0:T(8,128)(2,1)S(1)} %collective-permute-done.12), channel_id=1, source_target_pairs={{0,1},{1,0},{2,3},{3,2},{4,5},{5,4},{6,7},{7,6},{32,39},{33,34},{3... | collective-permute-start | bytes 1769480 | tf_op jit(solution)/shard_map/ppermute | solution.py:45
  92.1 13.3 %collective-permute-start.17 = (bf16[2,128,384]{2,1,0:T(8,128)(2,1)S(1)}, bf16[2,128,384]{2,1,0:T(8,128)(2,1)S(1)}, u32[]{:S(2)}, u32[]{:S(2)}) collective-permute-start(bf16[2,128,384]{2,1,0:T(8,128)(2,1)S(1)} %collective-permute-done.14), channel_id=1, source_target_pairs={{0,64},{64,0},{128,192},{192,128},{256,320},{320,256},{384,448},{4... | collective-permute-start | bytes 589832 | tf_op jit(solution)/shard_map/ppermute | solution.py:45
  98.1 28.5 %collective-permute-start.16 = (bf16[2,4,24,1536]{3,2,1,0:T(8,128)(2,1)S(1)}, bf16[2,4,24,1536]{3,2,1,0:T(8,128)(2,1)S(1)}, u32[]{:S(2)}, u32[]{:S(2)}) collective-permute-start(bf16[2,4,24,1536]{3,2,1,0:T(8,128)(2,1)S(1)} %collective-permute-done.15), channel_id=1, source_target_pairs={{0,7},{1,2},{2,1},{3,4},{4,3},{5,6},{6,5},{7,0},{32,33},{33,32},{3... | collective-permute-start | bytes 1769480 | tf_op jit(solution)/shard_map/ppermute | solution.py:45
  101.9 25.6 %collective-permute-start.8 = (bf16[8,40,1536]{2,1,0:T(8,128)(2,1)S(1)}, bf16[8,40,1536]{2,1,0:T(8,128)(2,1)S(1)}, u32[]{:S(2)}, u32[]{:S(2)}) collective-permute-start(bf16[8,40,1536]{2,1,0:T(8,128)(2,1)S(1)} %collective-permute-done.6), channel_id=1, source_target_pairs={{0,24},{8,16},{16,8},{24,0},{32,40},{40,32},{48,56},{56,48},{1,25}... | collective-permute-start | bytes 2949128 | tf_op jit(solution)/shard_map/ppermute | solution.py:45
  105.4 7.5 %collective-permute-start.18 = (bf16[2,128,384]{2,1,0:T(8,128)(2,1)S(1)}, bf16[2,128,384]{2,1,0:T(8,128)(2,1)S(1)}, u32[]{:S(2)}, u32[]{:S(2)}) collective-permute-start(bf16[2,128,384]{2,1,0:T(8,128)(2,1)S(1)} %collective-permute-done.17), channel_id=1, source_target_pairs={{0,448},{64,128},{128,64},{192,256},{256,192},{320,384},{384,320},... | collective-permute-start | bytes 589832 | tf_op jit(solution)/shard_map/ppermute | solution.py:45
  114.2 17.3 %collective-permute-start.19 = (bf16[8,128,384]{2,1,0:T(8,128)(2,1)}, bf16[8,128,384]{2,1,0:T(8,128)(2,1)}, u32[]{:S(2)}, u32[]{:S(2)}) collective-permute-start(bf16[8,128,384]{2,1,0:T(8,128)(2,1)} %slice_dynamic-update-slice_fusion.6), channel_id=1, source_target_pairs={{0,32},{32,0},{1,33},{33,1},{2,34},{34,2},{3,35},{35,3},{4,36},{36... | collective-permute-start | bytes 2359304 | tf_op jit(solution)/shard_map/ppermute | solution.py:130
  129.6 5.6 %collective-permute-start.20 = (bf16[2,2,4,64,384]{4,3,2,1,0:T(8,128)(2,1)}, bf16[2,2,4,64,384]{4,3,2,1,0:T(8,128)(2,1)}, u32[]{:S(2)}, u32[]{:S(2)}) collective-permute-start(bf16[2,2,4,64,384]{4,3,2,1,0:T(8,128)(2,1)} %fusion.22), channel_id=1, source_target_pairs={{0,32},{32,0},{1,33},{33,1},{2,34},{34,2},{3,35},{35,3},{4,36},{36... | collective-permute-start | bytes 2359304 | tf_op jit(solution)/shard_map/ppermute | solution.py:146
  138.1 26.3 %all-to-all-start = ((bf16[8,128,384]{2,1,0:T(8,128)(2,1)}), bf16[8,128,384]{2,1,0:T(8,128)(2,1)}, u32[]{:S(2)}, u32[]{:S(2)}) async-start(bf16[8,128,384]{2,1,0:T(8,128)(2,1)} %bitcast.148), calls=%async_computation | async-start | bytes 1572864 | tf_op jit(solution)/shard_map/all_to_all | solution.py:153
  (19 other events, 58.1 us)

commit v8 on v7

--- a/solution.py
+++ b/solution.py
@@ -19,7 +19,7 @@
 
 def slot_of(row, q):
     z, core = row // 2, row % 2
-    x, y = q * 2 + z // 4, core * 4 + z % 4
+    x, y = z // 2, core * 4 + z % 2 * 2 + q
     return x * 8 + y
 
 
@@ -95,7 +95,7 @@
     z, core, x, y = (lax.axis_index(a) for a in ALL)
     hidden = (grad_act.astype(F32) * gelu_prime(pre_act.astype(F32))).astype(BF)
     h = y % 2
-    q = x // 2
+    q = y & 1
     same = lax.dynamic_slice_in_dim(hidden, h * 64, 64, 0)
     other = lax.dynamic_slice_in_dim(hidden, (1 - h) * 64, 64, 0)
     same = lax.ppermute(same, ALL, to_slots(0))
@@ -131,25 +131,25 @@
     all_inputs = jnp.stack(
         [jnp.where(core == 0, own_z, mate_z), jnp.where(core == 0, mate_z, own_z)], axis=1
     )
-    seen = all_inputs.reshape(2, 4, 2, 2, 64, 384)
-    in_a = seen[:, :, :, :, :A].transpose(3, 0, 2, 1, 4, 5).reshape(4, 8 * A, 384)
+    seen = all_inputs.reshape(4, 2, 2, 2, 64, 384)
+    in_a = seen[:, :, :, :, :A].transpose(0, 2, 1, 3, 4, 5).reshape(4, 8 * A, 384)
     in_b = seen[:, :, :, :, A:].transpose(2, 1, 3, 0, 4, 5).reshape(8, 4 * B, 384)
 
     shares_a = shares_of(pairs_a, weight_t)
     shares_b = shares_of(pairs_b, weight_t)
 
-    share_a = place(shares_a, x, 4, sign_x).reshape(2, 2, 2, 4, A, 384)
-    share_b = place(shares_b, y, 8, sign_y).reshape(2, 4, 2, 2, B, 384).transpose(2, 3, 0, 1, 4, 5)
-    share = jnp.concatenate([share_a, share_b], axis=4)
-    keep = lax.dynamic_index_in_dim(share, core, 2, False)
-    give = lax.dynamic_index_in_dim(share, 1 - core, 2, False).astype(BF)
+    share_a = place(shares_a, x, 4, sign_x).reshape(4, 2, 4, A, 384)
+    share_b = place(shares_b, y, 8, sign_y).reshape(2, 4, 4, B, 384).transpose(2, 0, 1, 3, 4)
+    share = jnp.concatenate([share_a, share_b], axis=3)
+    keep = lax.dynamic_index_in_dim(share, core, 1, False)
+    give = lax.dynamic_index_in_dim(share, 1 - core, 1, False).astype(BF)
     mate = lax.ppermute(give, "core", [(0, 1), (1, 0)])
     in_a, in_b, mate = lax.optimization_barrier((in_a, in_b, mate))
     total = weight_sums(pairs_a, in_a, x, 4, sign_x, 0.0)
     total = weight_sums(pairs_b, in_b, y, 8, sign_y, total)
     grad_weight = total.astype(BF)
     both = keep + mate.astype(F32)
-    sent = both.astype(BF).transpose(1, 2, 0, 3, 4).reshape(8, 128, 384)
+    sent = both.astype(BF).reshape(8, 128, 384)
     parts = lax.all_to_all(sent, "z", 0, 0)
     grad_inputs = parts.astype(F32).sum(axis=0).astype(BF)
     return (grad_inputs, grad_weight)

time: 168 us -> 165 us (0.982)
  starting transfers between devices: 94.5 us -> 89.4 us
  waiting for transfers between devices: 37 us -> 40.3 us
  local copies, waits for them, and re-layouts: 13.8 us -> 11.6 us
  other arithmetic: 7.42 us -> 9.31 us
    ppermute x1, starting transfers between devices: 10.8 us -> 1.92 us  [on_device(): other = lax.ppermute(other, ALL, to_slots(1))]
    ppermute x17, starting transfers between devices: 63 us -> 70.3 us  [exchange(): return lax.ppermute(block, ROW if axis == 'z' else ('core', axis), pairs)]
    ppermute x1, starting transfers between devices: 12.4 us -> 8.37 us  [on_device(): mate_z = lax.ppermute(own_z, 'core', [(0, 1), (1, 0)])]
    ppermute x1, waiting for transfers between devices: 0.01 us -> 3.29 us  [on_device(): other = lax.ppermute(other, ALL, to_slots(1))]
    convert_element_type x1 -> x2, other arithmetic: 1.01 us -> 3.23 us  [the longest x1 2.22 us: on_device(): sent = both.astype(BF).reshape(8, 128, 384)]
    transpose x2 -> x0, local copies, waits for them, and re-layouts: 2.1 us -> none  [the longest x1 1.11 us: on_device(): seen[:, :, :, :, :A].transpose(3, 0, 2, 1, 4, 5).reshape(4, 8 * A, 384)]
    ppermute x17, waiting for transfers between devices: 25.6 us -> 23.5 us  [exchange(): return lax.ppermute(block, ROW if axis == 'z' else ('core', axis), pairs)]
    all_to_all x1, waiting for transfers between devices: 11.5 us -> 13.5 us  [on_device(): parts = lax.all_to_all(sent, 'z', 0, 0)]
  transfers between devices with their start and end apart: 22 -> 22, of which waited for: 9 -> 10; matrix products, arithmetic and copies ran while one was open for 16% -> 16% of each run, Pallas kernels for 0% -> 0%
where the time goes in v8:
time: 165 us; the launch traced here: 164 us
  starting transfers between devices  89.4 us (54%)
  waiting for transfers between devices  40.3 us (24%)
  matrix products  12 us (7%)
  local copies, waits for them, and re-layouts  11.6 us (7%)
  other arithmetic  9.31 us (6%)
    ppermute x17, starting transfers between devices, exchange(): return lax.ppermute(block, ROW if axis == 'z' else ('core', axis), pairs)  70.3 us
    ppermute x17, waiting for transfers between devices, exchange(): return lax.ppermute(block, ROW if axis == 'z' else ('core', axis), pairs)  23.5 us
    all_to_all x1, waiting for transfers between devices, on_device(): parts = lax.all_to_all(sent, 'z', 0, 0)  13.5 us
    dot_general x16, matrix products, dot(): return lax.dot_general(a, b, (dims, ((), ())), preferred_element_type=F32)  12 us
    ppermute x1, starting transfers between devices, on_device(): mate_z = lax.ppermute(own_z, 'core', [(0, 1), (1, 0)])  8.37 us
    dynamic_update_slice x27, local copies, waits for them, and re-layouts, place(): whole = lax.dynamic_update_slice(whole, pair[i:i + 1], start)  5.51 us
    all_to_all x1, starting transfers between devices, on_device(): parts = lax.all_to_all(sent, 'z', 0, 0)  4.95 us
  transfers between devices with their start and end apart: 22, of which 10 were waited for; matrix products, arithmetic and copies ran while one was open for 16% of the time, Pallas kernels for 0%

profile of v8, /device:TPU:1, one launch (start us, length us, event | category | flops | bytes accessed | tf_op | source)
XLA Modules:
  0.0 164.0 jit_solution(18033717377233123545)
XLA Ops:
  0.7 11.6 %collective-permute-start.13 = (bf16[128,384]{1,0:T(8,128)(2,1)}, bf16[128,384]{1,0:T(8,128)(2,1)S(1)}, u32[]{:S(2)}, u32[]{:S(2)}) collective-permute-start(bf16[128,384]{1,0:T(8,128)(2,1)} %param.4), channel_id=1, source_target_pairs={{0,64},{64,0},{128,192},{192,128},{256,320},{320,256},{384,448},{4... | collective-permute-start | bytes 294920 | tf_op jit(solution)/shard_map/ppermute | solution.py:45
  13.6 1.9 %collective-permute-start = (bf16[64,768]{1,0:T(8,128)(2,1)S(1)}, bf16[64,768]{1,0:T(8,128)(2,1)S(1)}, u32[]{:S(2)}, u32[]{:S(2)}) collective-permute-start(bf16[64,768]{1,0:T(8,128)(2,1)S(1)} %get-tuple-element.36), channel_id=1, source_target_pairs={{0,0},{1,1},{2,32},{3,33},{4,64},{5,65},{6,96},{7,97},{8,128},{9,1... | collective-permute-start | bytes 294920 | tf_op jit(solution)/shard_map/ppermute | solution.py:101
  19.1 2.2 %collective-permute-start.14 = (bf16[2,128,384]{2,1,0:T(8,128)(2,1)S(1)}, bf16[2,128,384]{2,1,0:T(8,128)(2,1)S(1)}, u32[]{:S(2)}, u32[]{:S(2)}) collective-permute-start(bf16[2,128,384]{2,1,0:T(8,128)(2,1)S(1)} %pad_maximum_fusion.3), channel_id=1, source_target_pairs={{0,448},{64,128},{128,64},{192,256},{256,192},{320,384},{384,320},... | collective-permute-start | bytes 589832 | tf_op jit(solution)/shard_map/ppermute | solution.py:45
  21.3 3.3 %collective-permute-done.1 = bf16[64,768]{1,0:T(8,128)(2,1)S(1)} collective-permute-done((bf16[64,768]{1,0:T(8,128)(2,1)S(1)}, bf16[64,768]{1,0:T(8,128)(2,1)S(1)}, u32[]{:S(2)}, u32[]{:S(2)}) %collective-permute-start.1) | collective-permute-done | bytes 98336 | tf_op jit(solution)/shard_map/ppermute | solution.py:102
  24.7 17.1 %collective-permute-start.9 = (bf16[24,1536]{1,0:T(8,128)(2,1)S(1)}, bf16[24,1536]{1,0:T(8,128)(2,1)S(1)}, u32[]{:S(2)}, u32[]{:S(2)}) collective-permute-start(bf16[24,1536]{1,0:T(8,128)(2,1)S(1)} %get-tuple-element.13), channel_id=1, source_target_pairs={{0,8},{8,0},{16,24},{24,16},{32,56},{40,48},{48,40},{56,32},{1,9},... | collective-permute-start | bytes 221192 | tf_op jit(solution)/shard_map/ppermute | solution.py:45
  44.5 3.0 %collective-permute-start.10 = (bf16[2,24,1536]{2,1,0:T(8,128)(2,1)S(1)}, bf16[2,24,1536]{2,1,0:T(8,128)(2,1)S(1)}, u32[]{:S(2)}, u32[]{:S(2)}) collective-permute-start(bf16[2,24,1536]{2,1,0:T(8,128)(2,1)S(1)} %pad_maximum_fusion.4), channel_id=1, source_target_pairs={{0,24},{8,16},{16,8},{24,0},{32,40},{40,32},{48,56},{56,48},{1,25}... | collective-permute-start | bytes 442376 | tf_op jit(solution)/shard_map/ppermute | solution.py:45
  50.8 4.2 %collective-permute-start.11 = (bf16[4,24,1536]{2,1,0:T(8,128)(2,1)S(1)}, bf16[4,24,1536]{2,1,0:T(8,128)(2,1)S(1)}, u32[]{:S(2)}, u32[]{:S(2)}) collective-permute-start(bf16[4,24,1536]{2,1,0:T(8,128)(2,1)S(1)} %slice_dynamic-update-slice_fusion.12), channel_id=1, source_target_pairs={{0,1},{1,0},{2,3},{3,2},{4,5},{5,4},{6,7},{7,6},{32,39},{33,34},{3... | collective-permute-start | bytes 884744 | tf_op jit(solution)/shard_map/ppermute | solution.py:45
  56.7 2.4 %collective-permute-start.4 = (bf16[2,40,1536]{2,1,0:T(8,128)(2,1)S(1)}, bf16[2,40,1536]{2,1,0:T(8,128)(2,1)S(1)}, u32[]{:S(2)}, u32[]{:S(2)}) collective-permute-start(bf16[2,40,1536]{2,1,0:T(8,128)(2,1)S(1)} %collective-permute-done.3), channel_id=1, source_target_pairs={{0,1},{1,0},{2,3},{3,2},{4,5},{5,4},{6,7},{7,6},{32,39},{33,34},{3... | collective-permute-start | bytes 737288 | tf_op jit(solution)/shard_map/ppermute | solution.py:45
  59.5 2.4 %collective-permute-start.12 = (bf16[2,4,24,1536]{3,2,1,0:T(8,128)(2,1)S(1)}, bf16[2,4,24,1536]{3,2,1,0:T(8,128)(2,1)S(1)}, u32[]{:S(2)}, u32[]{:S(2)}) collective-permute-start(bf16[2,4,24,1536]{3,2,1,0:T(8,128)(2,1)S(1)} %pad_maximum_fusion.1), channel_id=1, source_target_pairs={{0,7},{1,2},{2,1},{3,4},{4,3},{5,6},{6,5},{7,0},{32,33},{33,32},{3... | collective-permute-start | bytes 1769480 | tf_op jit(solution)/shard_map/ppermute | solution.py:45
  62.7 2.1 %collective-permute-done.4 = bf16[2,40,1536]{2,1,0:T(8,128)(2,1)S(1)} collective-permute-done((bf16[2,40,1536]{2,1,0:T(8,128)(2,1)S(1)}, bf16[2,40,1536]{2,1,0:T(8,128)(2,1)S(1)}, u32[]{:S(2)}, u32[]{:S(2)}) %collective-permute-start.4) | collective-permute-done | bytes 245792 | tf_op jit(solution)/shard_map/ppermute | solution.py:45
  66.8 6.3 %collective-permute-done.5 = bf16[2,40,1536]{2,1,0:T(8,128)(2,1)S(1)} collective-permute-done((bf16[2,40,1536]{2,1,0:T(8,128)(2,1)S(1)}, bf16[2,40,1536]{2,1,0:T(8,128)(2,1)S(1)}, u32[]{:S(2)}, u32[]{:S(2)}) %collective-permute-start.5) | collective-permute-done | bytes 245792 | tf_op jit(solution)/shard_map/ppermute | solution.py:45
  73.1 4.0 %collective-permute-start.7 = (bf16[8,40,1536]{2,1,0:T(8,128)(2,1)S(1)}, bf16[8,40,1536]{2,1,0:T(8,128)(2,1)S(1)}, u32[]{:S(2)}, u32[]{:S(2)}) collective-permute-start(bf16[8,40,1536]{2,1,0:T(8,128)(2,1)S(1)} %slice_dynamic-update-slice_fusion), channel_id=1, source_target_pairs={{0,24},{8,16},{16,8},{24,0},{32,40},{40,32},{48,56},{56,48},{1,25}... | collective-permute-start | bytes 2949128 | tf_op jit(solution)/shard_map/ppermute | solution.py:45
  77.2 3.0 %collective-permute-start.6 = (bf16[8,40,1536]{2,1,0:T(8,128)(2,1)S(1)}, bf16[8,40,1536]{2,1,0:T(8,128)(2,1)S(1)}, u32[]{:S(2)}, u32[]{:S(2)}) collective-permute-start(bf16[8,40,1536]{2,1,0:T(8,128)(2,1)S(1)} %slice_dynamic-update-slice_fusion), channel_id=1, source_target_pairs={{0,8},{8,0},{16,24},{24,16},{32,56},{40,48},{48,40},{56,32},{1,9},... | collective-permute-start | bytes 2949128 | tf_op jit(solution)/shard_map/ppermute | solution.py:45
  81.1 2.9 %collective-permute-start.15 = (bf16[2,4,24,1536]{3,2,1,0:T(8,128)(2,1)S(1)}, bf16[2,4,24,1536]{3,2,1,0:T(8,128)(2,1)S(1)}, u32[]{:S(2)}, u32[]{:S(2)}) collective-permute-start(bf16[2,4,24,1536]{3,2,1,0:T(8,128)(2,1)S(1)} %collective-permute-done.12), channel_id=1, source_target_pairs={{0,1},{1,0},{2,3},{3,2},{4,5},{5,4},{6,7},{7,6},{32,39},{33,34},{3... | collective-permute-start | bytes 1769480 | tf_op jit(solution)/shard_map/ppermute | solution.py:45
  84.6 8.6 %collective-permute-done.15 = bf16[2,4,24,1536]{3,2,1,0:T(8,128)(2,1)S(1)} collective-permute-done((bf16[2,4,24,1536]{3,2,1,0:T(8,128)(2,1)S(1)}, bf16[2,4,24,1536]{3,2,1,0:T(8,128)(2,1)S(1)}, u32[]{:S(2)}, u32[]{:S(2)}) %collective-permute-start.15) | collective-permute-done | bytes 589856 | tf_op jit(solution)/shard_map/ppermute | solution.py:45
  93.2 4.2 %collective-permute-start.17 = (bf16[2,128,384]{2,1,0:T(8,128)(2,1)S(1)}, bf16[2,128,384]{2,1,0:T(8,128)(2,1)S(1)}, u32[]{:S(2)}, u32[]{:S(2)}) collective-permute-start(bf16[2,128,384]{2,1,0:T(8,128)(2,1)S(1)} %collective-permute-done.14), channel_id=1, source_target_pairs={{0,64},{64,0},{128,192},{192,128},{256,320},{320,256},{384,448},{4... | collective-permute-start | bytes 589832 | tf_op jit(solution)/shard_map/ppermute | solution.py:45
  97.9 1.9 %collective-permute-start.16 = (bf16[2,4,24,1536]{3,2,1,0:T(8,128)(2,1)S(1)}, bf16[2,4,24,1536]{3,2,1,0:T(8,128)(2,1)S(1)}, u32[]{:S(2)}, u32[]{:S(2)}) collective-permute-start(bf16[2,4,24,1536]{3,2,1,0:T(8,128)(2,1)S(1)} %collective-permute-done.15), channel_id=1, source_target_pairs={{0,7},{1,2},{2,1},{3,4},{4,3},{5,6},{6,5},{7,0},{32,33},{33,32},{3... | collective-permute-start | bytes 1769480 | tf_op jit(solution)/shard_map/ppermute | solution.py:45
  102.3 2.2 %collective-permute-start.8 = (bf16[8,40,1536]{2,1,0:T(8,128)(2,1)S(1)}, bf16[8,40,1536]{2,1,0:T(8,128)(2,1)S(1)}, u32[]{:S(2)}, u32[]{:S(2)}) collective-permute-start(bf16[8,40,1536]{2,1,0:T(8,128)(2,1)S(1)} %collective-permute-done.6), channel_id=1, source_target_pairs={{0,24},{8,16},{16,8},{24,0},{32,40},{40,32},{48,56},{56,48},{1,25}... | collective-permute-start | bytes 2949128 | tf_op jit(solution)/shard_map/ppermute | solution.py:45
  106.0 3.2 %collective-permute-start.18 = (bf16[2,128,384]{2,1,0:T(8,128)(2,1)S(1)}, bf16[2,128,384]{2,1,0:T(8,128)(2,1)S(1)}, u32[]{:S(2)}, u32[]{:S(2)}) collective-permute-start(bf16[2,128,384]{2,1,0:T(8,128)(2,1)S(1)} %collective-permute-done.17), channel_id=1, source_target_pairs={{0,448},{64,128},{128,64},{192,256},{256,192},{320,384},{384,320},... | collective-permute-start | bytes 589832 | tf_op jit(solution)/shard_map/ppermute | solution.py:45
  110.5 2.2 %collective-permute-done.18 = bf16[2,128,384]{2,1,0:T(8,128)(2,1)S(1)} collective-permute-done((bf16[2,128,384]{2,1,0:T(8,128)(2,1)S(1)}, bf16[2,128,384]{2,1,0:T(8,128)(2,1)S(1)}, u32[]{:S(2)}, u32[]{:S(2)}) %collective-permute-start.18) | collective-permute-done | bytes 196640 | tf_op jit(solution)/shard_map/ppermute | solution.py:45
  114.0 8.4 %collective-permute-start.19 = (bf16[8,128,384]{2,1,0:T(8,128)(2,1)}, bf16[8,128,384]{2,1,0:T(8,128)(2,1)}, u32[]{:S(2)}, u32[]{:S(2)}) collective-permute-start(bf16[8,128,384]{2,1,0:T(8,128)(2,1)} %slice_dynamic-update-slice_fusion.6), channel_id=1, source_target_pairs={{0,32},{32,0},{1,33},{33,1},{2,34},{34,2},{3,35},{35,3},{4,36},{36... | collective-permute-start | bytes 2359304 | tf_op jit(solution)/shard_map/ppermute | solution.py:130
  131.2 2.2 %fusion.10 = bf16[4,4,64,384]{3,2,1,0:T(8,128)(2,1)} fusion(s32[]{:T(128)S(6)} %select_n.148, f32[4,2,4,40,384]{4,3,2,1,0:T(8,128)S(1)} %bitcast.139, f32[4,2,4,24,384]{4,3,2,1,0:T(8,128)S(1)} %bitcast.141, bf16[4,4,64,384]{3,2,1,0:T(8,128)(2,1)} %collective-permute-done.20), kind=kLoop, calls=%fused_computation.17 | loop fusion | flops 1572864 | bytes 4718596 | tf_op jit(solution)/shard_map/convert_element_type | solution.py:152
  133.4 5.0 %all-to-all-start = ((bf16[8,128,384]{2,1,0:T(8,128)(2,1)}), bf16[8,128,384]{2,1,0:T(8,128)(2,1)}, u32[]{:S(2)}, u32[]{:S(2)}) async-start(bf16[8,128,384]{2,1,0:T(8,128)(2,1)} %bitcast.156), calls=%async_computation | async-start | bytes 1572864 | tf_op jit(solution)/shard_map/all_to_all | solution.py:153
  148.6 13.5 %all-to-all-done = bf16[8,128,384]{2,1,0:T(8,128)(2,1)} async-done(((bf16[8,128,384]{2,1,0:T(8,128)(2,1)}), bf16[8,128,384]{2,1,0:T(8,128)(2,1)}, u32[]{:S(2)}, u32[]{:S(2)}) %all-to-all-start) | async-done | bytes 786464 | tf_op jit(solution)/shard_map/all_to_all | solution.py:153
  (131 shorter events, 44.6 us)
Async XLA Ops:
  0.6 61.3 %copy-start = (bf16[1536,384]{1,0:T(8,128)(2,1)S(1)}, bf16[1536,384]{1,0:T(8,128)(2,1)}, u32[]{:S(2)}) copy-start(bf16[1536,384]{1,0:T(8,128)(2,1)} %param.7) | copy-start | bytes 3538948
  0.6 17.8 %copy-start.20 = (bf16[128,384]{1,0:T(8,128)(2,1)S(1)}, bf16[128,384]{1,0:T(8,128)(2,1)}, u32[]{:S(2)}) copy-start(bf16[128,384]{1,0:T(8,128)(2,1)} %param.4) | copy-start | bytes 294916
  0.7 18.4 %collective-permute-start.13 = (bf16[128,384]{1,0:T(8,128)(2,1)}, bf16[128,384]{1,0:T(8,128)(2,1)S(1)}, u32[]{:S(2)}, u32[]{:S(2)}) collective-permute-start(bf16[128,384]{1,0:T(8,128)(2,1)} %param.4), channel_id=1, source_target_pairs={{0,64},{64,0},{128,192},{192,128},{256,320},{320,256},{384,448},{4... | collective-permute-start | bytes 294920 | tf_op jit(solution)/shard_map/ppermute | solution.py:45
  13.6 7.7 %collective-permute-start = (bf16[64,768]{1,0:T(8,128)(2,1)S(1)}, bf16[64,768]{1,0:T(8,128)(2,1)S(1)}, u32[]{:S(2)}, u32[]{:S(2)}) collective-permute-start(bf16[64,768]{1,0:T(8,128)(2,1)S(1)} %get-tuple-element.36), channel_id=1, source_target_pairs={{0,0},{1,1},{2,32},{3,33},{4,64},{5,65},{6,96},{7,97},{8,128},{9,1... | collective-permute-start | bytes 294920 | tf_op jit(solution)/shard_map/ppermute | solution.py:101
  15.6 9.0 %collective-permute-start.1 = (bf16[64,768]{1,0:T(8,128)(2,1)S(1)}, bf16[64,768]{1,0:T(8,128)(2,1)S(1)}, u32[]{:S(2)}, u32[]{:S(2)}) collective-permute-start(bf16[64,768]{1,0:T(8,128)(2,1)S(1)} %get-tuple-element.37), channel_id=1, source_target_pairs={{0,1},{1,0},{2,33},{3,32},{4,65},{5,64},{6,97},{7,96},{8,129},{9,1... | collective-permute-start | bytes 294920 | tf_op jit(solution)/shard_map/ppermute | solution.py:102
  19.1 65.4 %collective-permute-start.14 = (bf16[2,128,384]{2,1,0:T(8,128)(2,1)S(1)}, bf16[2,128,384]{2,1,0:T(8,128)(2,1)S(1)}, u32[]{:S(2)}, u32[]{:S(2)}) collective-permute-start(bf16[2,128,384]{2,1,0:T(8,128)(2,1)S(1)} %pad_maximum_fusion.3), channel_id=1, source_target_pairs={{0,448},{64,128},{128,64},{192,256},{256,192},{320,384},{384,320},... | collective-permute-start | bytes 589832 | tf_op jit(solution)/shard_map/ppermute | solution.py:45
  24.7 19.8 %collective-permute-start.9 = (bf16[24,1536]{1,0:T(8,128)(2,1)S(1)}, bf16[24,1536]{1,0:T(8,128)(2,1)S(1)}, u32[]{:S(2)}, u32[]{:S(2)}) collective-permute-start(bf16[24,1536]{1,0:T(8,128)(2,1)S(1)} %get-tuple-element.13), channel_id=1, source_target_pairs={{0,8},{8,0},{16,24},{24,16},{32,56},{40,48},{48,40},{56,32},{1,9},... | collective-permute-start | bytes 221192 | tf_op jit(solution)/shard_map/ppermute | solution.py:45
  41.9 6.8 %collective-permute-start.2 = (bf16[40,1536]{1,0:T(8,128)(2,1)S(1)}, bf16[40,1536]{1,0:T(8,128)(2,1)S(1)}, u32[]{:S(2)}, u32[]{:S(2)}) collective-permute-start(bf16[40,1536]{1,0:T(8,128)(2,1)S(1)} %get-tuple-element.15), channel_id=1, source_target_pairs={{0,1},{1,0},{2,3},{3,2},{4,5},{5,4},{6,7},{7,6},{32,39},{33,34},{3... | collective-permute-start | bytes 368648 | tf_op jit(solution)/shard_map/ppermute | solution.py:45
  44.5 6.2 %collective-permute-start.10 = (bf16[2,24,1536]{2,1,0:T(8,128)(2,1)S(1)}, bf16[2,24,1536]{2,1,0:T(8,128)(2,1)S(1)}, u32[]{:S(2)}, u32[]{:S(2)}) collective-permute-start(bf16[2,24,1536]{2,1,0:T(8,128)(2,1)S(1)} %pad_maximum_fusion.4), channel_id=1, source_target_pairs={{0,24},{8,16},{16,8},{24,0},{32,40},{40,32},{48,56},{56,48},{1,25}... | collective-permute-start | bytes 442376 | tf_op jit(solution)/shard_map/ppermute | solution.py:45
  48.8 7.9 %collective-permute-start.3 = (bf16[2,40,1536]{2,1,0:T(8,128)(2,1)S(1)}, bf16[2,40,1536]{2,1,0:T(8,128)(2,1)S(1)}, u32[]{:S(2)}, u32[]{:S(2)}) collective-permute-start(bf16[2,40,1536]{2,1,0:T(8,128)(2,1)S(1)} %pad_maximum_fusion.2), channel_id=1, source_target_pairs={{0,7},{1,2},{2,1},{3,4},{4,3},{5,6},{6,5},{7,0},{32,33},{33,32},{3... | collective-permute-start | bytes 737288 | tf_op jit(solution)/shard_map/ppermute | solution.py:45
  50.8 8.7 %collective-permute-start.11 = (bf16[4,24,1536]{2,1,0:T(8,128)(2,1)S(1)}, bf16[4,24,1536]{2,1,0:T(8,128)(2,1)S(1)}, u32[]{:S(2)}, u32[]{:S(2)}) collective-permute-start(bf16[4,24,1536]{2,1,0:T(8,128)(2,1)S(1)} %slice_dynamic-update-slice_fusion.12), channel_id=1, source_target_pairs={{0,1},{1,0},{2,3},{3,2},{4,5},{5,4},{6,7},{7,6},{32,39},{33,34},{3... | collective-permute-start | bytes 884744 | tf_op jit(solution)/shard_map/ppermute | solution.py:45
  56.7 8.1 %collective-permute-start.4 = (bf16[2,40,1536]{2,1,0:T(8,128)(2,1)S(1)}, bf16[2,40,1536]{2,1,0:T(8,128)(2,1)S(1)}, u32[]{:S(2)}, u32[]{:S(2)}) collective-permute-start(bf16[2,40,1536]{2,1,0:T(8,128)(2,1)S(1)} %collective-permute-done.3), channel_id=1, source_target_pairs={{0,1},{1,0},{2,3},{3,2},{4,5},{5,4},{6,7},{7,6},{32,39},{33,34},{3... | collective-permute-start | bytes 737288 | tf_op jit(solution)/shard_map/ppermute | solution.py:45
  59.5 21.5 %collective-permute-start.12 = (bf16[2,4,24,1536]{3,2,1,0:T(8,128)(2,1)S(1)}, bf16[2,4,24,1536]{3,2,1,0:T(8,128)(2,1)S(1)}, u32[]{:S(2)}, u32[]{:S(2)}) collective-permute-start(bf16[2,4,24,1536]{3,2,1,0:T(8,128)(2,1)S(1)} %pad_maximum_fusion.1), channel_id=1, source_target_pairs={{0,7},{1,2},{2,1},{3,4},{4,3},{5,6},{6,5},{7,0},{32,33},{33,32},{3... | collective-permute-start | bytes 1769480 | tf_op jit(solution)/shard_map/ppermute | solution.py:45
  64.8 8.3 %collective-permute-start.5 = (bf16[2,40,1536]{2,1,0:T(8,128)(2,1)S(1)}, bf16[2,40,1536]{2,1,0:T(8,128)(2,1)S(1)}, u32[]{:S(2)}, u32[]{:S(2)}) collective-permute-start(bf16[2,40,1536]{2,1,0:T(8,128)(2,1)S(1)} %collective-permute-done.4), channel_id=1, source_target_pairs={{0,7},{1,2},{2,1},{3,4},{4,3},{5,6},{6,5},{7,0},{32,33},{33,32},{3... | collective-permute-start | bytes 737288 | tf_op jit(solution)/shard_map/ppermute | solution.py:45
  73.1 32.1 %collective-permute-start.7 = (bf16[8,40,1536]{2,1,0:T(8,128)(2,1)S(1)}, bf16[8,40,1536]{2,1,0:T(8,128)(2,1)S(1)}, u32[]{:S(2)}, u32[]{:S(2)}) collective-permute-start(bf16[8,40,1536]{2,1,0:T(8,128)(2,1)S(1)} %slice_dynamic-update-slice_fusion), channel_id=1, source_target_pairs={{0,24},{8,16},{16,8},{24,0},{32,40},{40,32},{48,56},{56,48},{1,25}... | collective-permute-start | bytes 2949128 | tf_op jit(solution)/shard_map/ppermute | solution.py:45
  77.2 25.2 %collective-permute-start.6 = (bf16[8,40,1536]{2,1,0:T(8,128)(2,1)S(1)}, bf16[8,40,1536]{2,1,0:T(8,128)(2,1)S(1)}, u32[]{:S(2)}, u32[]{:S(2)}) collective-permute-start(bf16[8,40,1536]{2,1,0:T(8,128)(2,1)S(1)} %slice_dynamic-update-slice_fusion), channel_id=1, source_target_pairs={{0,8},{8,0},{16,24},{24,16},{32,56},{40,48},{48,40},{56,32},{1,9},... | collective-permute-start | bytes 2949128 | tf_op jit(solution)/shard_map/ppermute | solution.py:45
  81.1 12.1 %collective-permute-start.15 = (bf16[2,4,24,1536]{3,2,1,0:T(8,128)(2,1)S(1)}, bf16[2,4,24,1536]{3,2,1,0:T(8,128)(2,1)S(1)}, u32[]{:S(2)}, u32[]{:S(2)}) collective-permute-start(bf16[2,4,24,1536]{3,2,1,0:T(8,128)(2,1)S(1)} %collective-permute-done.12), channel_id=1, source_target_pairs={{0,1},{1,0},{2,3},{3,2},{4,5},{5,4},{6,7},{7,6},{32,39},{33,34},{3... | collective-permute-start | bytes 1769480 | tf_op jit(solution)/shard_map/ppermute | solution.py:45
  93.2 12.8 %collective-permute-start.17 = (bf16[2,128,384]{2,1,0:T(8,128)(2,1)S(1)}, bf16[2,128,384]{2,1,0:T(8,128)(2,1)S(1)}, u32[]{:S(2)}, u32[]{:S(2)}) collective-permute-start(bf16[2,128,384]{2,1,0:T(8,128)(2,1)S(1)} %collective-permute-done.14), channel_id=1, source_target_pairs={{0,64},{64,0},{128,192},{192,128},{256,320},{320,256},{384,448},{4... | collective-permute-start | bytes 589832 | tf_op jit(solution)/shard_map/ppermute | solution.py:45
  97.9 24.4 %collective-permute-start.16 = (bf16[2,4,24,1536]{3,2,1,0:T(8,128)(2,1)S(1)}, bf16[2,4,24,1536]{3,2,1,0:T(8,128)(2,1)S(1)}, u32[]{:S(2)}, u32[]{:S(2)}) collective-permute-start(bf16[2,4,24,1536]{3,2,1,0:T(8,128)(2,1)S(1)} %collective-permute-done.15), channel_id=1, source_target_pairs={{0,7},{1,2},{2,1},{3,4},{4,3},{5,6},{6,5},{7,0},{32,33},{33,32},{3... | collective-permute-start | bytes 1769480 | tf_op jit(solution)/shard_map/ppermute | solution.py:45
  102.3 20.8 %collective-permute-start.8 = (bf16[8,40,1536]{2,1,0:T(8,128)(2,1)S(1)}, bf16[8,40,1536]{2,1,0:T(8,128)(2,1)S(1)}, u32[]{:S(2)}, u32[]{:S(2)}) collective-permute-start(bf16[8,40,1536]{2,1,0:T(8,128)(2,1)S(1)} %collective-permute-done.6), channel_id=1, source_target_pairs={{0,24},{8,16},{16,8},{24,0},{32,40},{40,32},{48,56},{56,48},{1,25}... | collective-permute-start | bytes 2949128 | tf_op jit(solution)/shard_map/ppermute | solution.py:45
  106.0 6.7 %collective-permute-start.18 = (bf16[2,128,384]{2,1,0:T(8,128)(2,1)S(1)}, bf16[2,128,384]{2,1,0:T(8,128)(2,1)S(1)}, u32[]{:S(2)}, u32[]{:S(2)}) collective-permute-start(bf16[2,128,384]{2,1,0:T(8,128)(2,1)S(1)} %collective-permute-done.17), channel_id=1, source_target_pairs={{0,448},{64,128},{128,64},{192,256},{256,192},{320,384},{384,320},... | collective-permute-start | bytes 589832 | tf_op jit(solution)/shard_map/ppermute | solution.py:45
  114.0 13.1 %collective-permute-start.19 = (bf16[8,128,384]{2,1,0:T(8,128)(2,1)}, bf16[8,128,384]{2,1,0:T(8,128)(2,1)}, u32[]{:S(2)}, u32[]{:S(2)}) collective-permute-start(bf16[8,128,384]{2,1,0:T(8,128)(2,1)} %slice_dynamic-update-slice_fusion.6), channel_id=1, source_target_pairs={{0,32},{32,0},{1,33},{33,1},{2,34},{34,2},{3,35},{35,3},{4,36},{36... | collective-permute-start | bytes 2359304 | tf_op jit(solution)/shard_map/ppermute | solution.py:130
  125.2 5.5 %collective-permute-start.20 = (bf16[4,4,64,384]{3,2,1,0:T(8,128)(2,1)}, bf16[4,4,64,384]{3,2,1,0:T(8,128)(2,1)}, u32[]{:S(2)}, u32[]{:S(2)}) collective-permute-start(bf16[4,4,64,384]{3,2,1,0:T(8,128)(2,1)} %fusion.20), channel_id=1, source_target_pairs={{0,32},{32,0},{1,33},{33,1},{2,34},{34,2},{3,35},{35,3},{4,36},{36... | collective-permute-start | bytes 2359304 | tf_op jit(solution)/shard_map/ppermute | solution.py:146
  133.4 28.7 %all-to-all-start = ((bf16[8,128,384]{2,1,0:T(8,128)(2,1)}), bf16[8,128,384]{2,1,0:T(8,128)(2,1)}, u32[]{:S(2)}, u32[]{:S(2)}) async-start(bf16[8,128,384]{2,1,0:T(8,128)(2,1)} %bitcast.156), calls=%async_computation | async-start | bytes 1572864 | tf_op jit(solution)/shard_map/all_to_all | solution.py:153
  (19 other events, 58.7 us)
